TPU v7x, 32 devices: a whole 2x2x4 slice. The times are simulated.
32 devices in a mesh: ctx: 8 (over z, y), ch: 4 (over x, core).
Axes of the slice: x: 2, y: 2, z: 4, core: 2. Of those that a mesh axis runs over, the one named last changes fastest.
Arguments:
- signal: bfloat16 [256, 512, 1024], P('ctx', None, 'ch'), may hold values from -15 to 15
- factor_first: bfloat16 [4, 512, 512], P('ch'), may hold values from -0.25 to 0.25
- factor_second: bfloat16 [4, 256, 256], P('ch'), may hold values from -0.375 to 0.375
- up_weight: bfloat16 [4, 256, 1024], P('ch'), may hold values from -0.375 to 0.375
- down_weight: bfloat16 [4, 1024, 256], P('ch'), may hold values from -0.1875 to 0.1875
- norm_gain: float32 [4, 256], P('ch'), may hold values from 0.1 to 1.9
- cotangent: bfloat16 [512, 256, 1024], P('ctx', None, 'ch'), may hold values from -6 to 6
Outputs:
- layer_out: bfloat16 [512, 256, 1024], P('ctx', None, 'ch')
- grad_signal: bfloat16 [256, 512, 1024], P('ctx', None, 'ch')
- grad_first: float32 [4, 512, 512], P('ch', 'ctx')
- grad_second: float32 [4, 256, 256], P('ch', 'ctx')
- grad_up: float32 [4, 256, 1024], P('ch', 'ctx')
- grad_down: float32 [4, 1024, 256], P('ch', 'ctx')
- grad_gain: float32 [4, 256], P('ch', 'ctx')
All inputs are finite; a program needn't handle non-finite values.
Results may differ from a plain program's by a relative error of at most 0.0095.
Values may be sent and summed in bfloat16 or wider, within the bound.
No kernel may reach another device: no remote copies, remote signals or barrier semaphores. Data moves between devices by JAX's collectives and lax.ppermute only.
A program may use at most 256 MiB of HBM per device.

v0:
```python
import jax
import jax.numpy as jnp
from jax import lax
from jax.sharding import PartitionSpec as P

D = 1024
NB = 512
NA = 256


EPSILON = 1e-05


def transpose_slab(block):
    return lax.all_to_all(block, "ctx", split_axis=1, concat_axis=0, tiled=True)


def channel_total(partial_value):
    return lax.psum(partial_value, "ch")


def shards(signal, factor_first, factor_second, up_weight, down_weight, norm_gain, cotangent):
    groups = factor_first.shape[0]
    group_width = up_weight.shape[1]
    local_rows = signal.shape[0]
    row_count = signal.shape[1]
    inputs = signal.reshape(local_rows, row_count, groups, group_width)
    first_mix = jnp.einsum(
        "abgc,gbj->ajgc", inputs, factor_first, preferred_element_type=jnp.float32
    )
    gate_open = jax.nn.sigmoid(inputs.astype(jnp.float32))
    gated_rows = (first_mix * gate_open).astype(jnp.bfloat16)
    moved_rows = transpose_slab(gated_rows)
    mixed_rows = jnp.einsum(
        "ajgc,gai->jigc", moved_rows, factor_second, preferred_element_type=jnp.float32
    )
    mean_square = channel_total(jnp.sum(mixed_rows * mixed_rows, axis=(2, 3))) / D
    inverse = lax.rsqrt(mean_square + EPSILON)[:, :, None, None]
    gain_rows = norm_gain[None, None]
    normed = (mixed_rows * inverse * gain_rows).astype(jnp.bfloat16)
    preact = jnp.einsum("jigc,gch->jigh", normed, up_weight, preferred_element_type=jnp.float32)
    activation, gelu_back = jax.vjp(jax.nn.gelu, preact)
    act_rows = activation.astype(jnp.bfloat16)
    layer_out = (
        mixed_rows
        + jnp.einsum("jigh,ghc->jigc", act_rows, down_weight, preferred_element_type=jnp.float32)
    ).astype(jnp.bfloat16)
    upstream = cotangent.reshape(mixed_rows.shape)
    grad_act = jnp.einsum(
        "jigc,ghc->jigh", upstream, down_weight, preferred_element_type=jnp.float32
    )
    grad_pre = gelu_back(grad_act)[0].astype(jnp.bfloat16)
    grad_down = jnp.einsum("jigh,jigc->ghc", act_rows, upstream, preferred_element_type=jnp.float32)
    grad_up = jnp.einsum("jigc,jigh->gch", normed, grad_pre, preferred_element_type=jnp.float32)
    grad_normed = jnp.einsum(
        "jigh,gch->jigc", grad_pre, up_weight, preferred_element_type=jnp.float32
    )
    grad_gain = jnp.sum(grad_normed * mixed_rows * inverse, axis=(0, 1))
    grad_scaled = grad_normed * gain_rows
    cross = channel_total(jnp.sum(grad_scaled * mixed_rows, axis=(2, 3))) / D
    grad_mixed = (
        upstream.astype(jnp.float32)
        + inverse * grad_scaled
        - inverse**3 * mixed_rows * cross[:, :, None, None]
    ).astype(jnp.bfloat16)
    grad_second = jnp.einsum(
        "ajgc,jigc->gai", moved_rows, grad_mixed, preferred_element_type=jnp.float32
    )
    grad_moved = jnp.einsum(
        "jigc,gai->jagc", grad_mixed, factor_second, preferred_element_type=jnp.float32
    ).astype(jnp.bfloat16)
    grad_gated = jnp.swapaxes(transpose_slab(grad_moved), 0, 1)
    gated_float = grad_gated.astype(jnp.float32)
    grad_first_mix = (gated_float * gate_open).astype(jnp.bfloat16)
    grad_gate = gated_float * first_mix * gate_open * (1.0 - gate_open)
    grad_input = (
        jnp.einsum(
            "ajgc,gbj->abgc", grad_first_mix, factor_first, preferred_element_type=jnp.float32
        )
        + grad_gate
    ).astype(jnp.bfloat16)
    grad_first = jnp.einsum(
        "abgc,ajgc->gbj", inputs, grad_first_mix, preferred_element_type=jnp.float32
    )
    summed = (
        lax.psum_scatter(grad_first, "ctx", scatter_dimension=1, tiled=True),
        lax.psum_scatter(grad_second, "ctx", scatter_dimension=1, tiled=True),
        lax.psum_scatter(grad_up, "ctx", scatter_dimension=1, tiled=True),
        lax.psum_scatter(grad_down, "ctx", scatter_dimension=1, tiled=True),
        lax.psum_scatter(grad_gain, "ctx", scatter_dimension=1, tiled=True),
    )
    grad_scale = (NA * NB) ** (-0.5)
    return (
        layer_out.reshape(cotangent.shape),
        grad_input.reshape(signal.shape),
        summed[0] * grad_scale,
        summed[1] * grad_scale,
        summed[2] * grad_scale,
        summed[3] * grad_scale,
        summed[4] * grad_scale,
    )


def solution(mesh):
    placed = (
        P("ctx", None, "ch"),
        P("ch", None, None),
        P("ch", None, None),
        P("ch", None, None),
        P("ch", None, None),
        P("ch", None),
        P("ctx", None, "ch"),
    )
    return jax.shard_map(
        shards,
        mesh=mesh,
        in_specs=placed,
        out_specs=(
            P("ctx", None, "ch"),
            P("ctx", None, "ch"),
            P("ch", "ctx", None),
            P("ch", "ctx", None),
            P("ch", "ctx", None),
            P("ch", "ctx", None),
            P("ch", "ctx"),
        ),
        check_vma=False,
    )
```

profile of v0, /device:TPU:0, one launch (start us, length us, event | category | flops | bytes accessed | tf_op | source)
XLA Modules:
  0.0 978.9 jit_solution(12320619936932615688)
XLA Ops:
  7.2 17.9 %fusion.25 = (bf16[32,512,1,256]{3,1,0,2:T(8,128)(2,1)}, f32[512,32,256]{2,0,1:T(8,128)}) fusion(bf16[32,512,256]{2,1,0:T(8,128)(2,1)} %param.7, bf16[1,512,512]{2,1,0:T(8,128)(2,1)} %param.8), kind=kOutput, calls=%fused_computation.39 | convolution fusion | flops 4320133120 | bytes 34078720 | tf_op jit(solution)/shard_map/abgc,gbj->ajgc/dot_general | solution.py:28
  36.7 190.4 %all_to_all.24 = bf16[32,512,1,256]{3,0,2,1:T(8,128)(2,1)} all-to-all(bf16[32,512,1,256]{3,0,2,1:T(8,128)(2,1)} %copy.66), channel_id=1, replica_groups=mesh['ctx'=8,'ch'=4] {'ctx'}, dimensions={1} | all-to-all | bytes 16777216 | tf_op jit(solution)/shard_map/all_to_all | solution.py:15
  227.1 11.6 %copy.67 = bf16[32,512,1,256]{3,1,0,2:T(8,128)(2,1)} copy(bf16[32,512,1,256]{3,0,2,1:T(8,128)(2,1)} %all_to_all.24) | data formatting | bytes 16777216 | tf_op jit(solution)/shard_map/all_to_all | solution.py:15
  247.2 25.8 %fusion.28 = (f32[64,256]{1,0:T(8,128)}, f32[64,256,256]{2,1,0:T(8,128)}) fusion(bf16[1,256,256]{2,1,0:T(8,128)(2,1)S(1)} %copy-done.7, bf16[256,64,256]{2,1,0:T(8,128)(2,1)} %bitcast.262), kind=kOutput, calls=%fused_computation.47 | convolution fusion | flops 2155855872 | bytes 25362432 | tf_op jit(solution)/shard_map/ajgc,gai->jigc/dot_general | solution.py:34
  273.0 30.2 %all-reduce.5.cloned.1.call-done = f32[64,256]{1,0:T(8,128)} async-done(((f32[64,256]{1,0:T(8,128)}), f32[64,256]{1,0:T(8,128)}) %all-reduce.5.cloned.1.call-update) | async-done | bytes 65552 | tf_op jit(solution)/shard_map/psum | solution.py:19
  304.8 29.3 %fusion.70 = f32[64,256,1024]{2,1,0:T(8,128)} fusion(bf16[1,256,1024]{2,1,0:T(8,128)(2,1)S(1)} %copy-done, f32[64,256,256]{2,1,0:T(8,128)} %get-tuple-element.42, f32[256]{0:T(256)S(1)} %bitcast.268, f32[64,256]{1,0:T(8,128)S(1)} %get-tuple-element.38), kind=kOutput, calls=%fused_computation.75 | convolution fusion | flops 8602517504 | bytes 84476928 | tf_op jit(solution)/shard_map/jigc,gch->jigh/dot_general | solution.py:41
  334.1 54.4 %fusion.6 = bf16[64,256,1,1024]{3,1,0,2:T(8,128)(2,1)} fusion(f32[64,256,1024]{2,1,0:T(8,128)} %fusion.70, bf16[64,256,256]{2,1,0:T(8,128)(2,1)} %param.13, bf16[1,1024,256]{2,1,0:T(8,128)(2,1)S(1)} %copy-done.11), kind=kOutput, calls=%fused_computation.8 | convolution fusion | flops 8925478912 | bytes 109576192 | tf_op jit(solution)/shard_map/jigc,ghc->jigh/dot_general | solution.py:49
  388.4 26.9 %fusion.24 = (f32[256]{0:T(256)S(1)}, f32[64,256]{1,0:T(8,128)}, f32[64,256,256]{1,2,0:T(8,128)}) fusion(f32[64,256,256]{2,1,0:T(8,128)} %get-tuple-element.42, f32[64,256]{1,0:T(8,128)} %copy-done.4, f32[256]{0:T(256)S(1)} %bitcast.269, bf16[1,256,1024]{2,1,0:T(8,128)(2,1)S(1)} %copy-done, bf16[64,256,1,1024]{3,1,0,2:T(8,128)(2,1)} %fusion.6), kind=kOutput, calls=%fused_computation.35 | convolution fusion | flops 8615084032 | bytes 67766272 | tf_op jit(solution)/shard_map/jigh,gch->jigc/dot_general | solution.py:55
  415.5 11.9 %copy.72 = bf16[64,256,256]{1,2,0:T(8,128)(2,1)} copy(bf16[64,256,256]{2,1,0:T(8,128)(2,1)} %param.13) | data formatting | bytes 16777216 | tf_op args[6]
  429.5 17.2 %all-reduce.7.cloned.1.call-done = f32[64,256]{1,0:T(8,128)} async-done(((f32[64,256]{1,0:T(8,128)}), f32[64,256]{1,0:T(8,128)}) %all-reduce.7.cloned.1.call-update) | async-done | bytes 65552 | tf_op jit(solution)/shard_map/psum | solution.py:19
  447.5 15.5 %fusion.38 = bf16[64,256,256]{1,2,0:T(8,128)(2,1)S(1)} fusion(f32[64,256,256]{2,1,0:T(8,128)} %get-tuple-element.42, f32[64,256,256]{1,2,0:T(8,128)} %get-tuple-element.43, bf16[64,256,256]{1,2,0:T(8,128)(2,1)} %copy.72, f32[64,256]{1,0:T(8,128)S(1)} %broadcast_multiply_fusion.2, f32[64,256]{1,0:T(8,128)S(1)} %copy-done.6, f32[256]{0:T(256)S(1)} %bitcast.270, ...), kind=kLoop, calls=%fused_computation.54 | loop fusion | flops 33554432 | bytes 50529280 | tf_op jit(solution)/shard_map/reshape.36
  466.4 13.4 %fusion.61 = f32[1,256,256]{2,1,0:T(8,128)} fusion(bf16[64,256,256]{1,2,0:T(8,128)(2,1)S(1)} %fusion.38, bf16[256,64,256]{2,1,0:T(8,128)(2,1)} %bitcast.263), kind=kOutput, calls=%fused_computation.68 | convolution fusion | flops 2147483648 | bytes 17039360 | tf_op jit(solution)/shard_map/ajgc,jigc->gai/dot_general | solution.py:66
  488.9 12.4 %copy.75 = bf16[64,256,1,256]{3,0,2,1:T(8,128)(2,1)} copy(bf16[64,256,1,256]{1,3,0,2:T(8,128)(2,1)} %convert_bitcast_fusion.1) | data formatting | bytes 16777216 | tf_op jit(solution)/shard_map/convert_element_type | solution.py:71
  507.5 30.9 %fusion.55 = f32[1,1024,256]{2,1,0:T(8,128)} fusion(bf16[64,256,256]{2,1,0:T(8,128)(2,1)} %param.13, f32[64,256,1024]{2,1,0:T(8,128)} %fusion.70), kind=kOutput, calls=%fused_computation.66 | convolution fusion | flops 8740929536 | bytes 76546048 | tf_op jit(solution)/shard_map/jigh,jigc->ghc/dot_general | solution.py:53
  538.5 21.0 %fusion.58 = f32[1,256,1024]{2,1,0:T(8,128)} fusion(bf16[64,256,1,1024]{3,1,0,2:T(8,128)(2,1)} %fusion.6, f32[64,256,256]{2,1,0:T(8,128)} %get-tuple-element.42, f32[256]{0:T(256)S(1)} %bitcast.271, f32[64,256]{1,0:T(8,128)S(1)} %copy-done.5), kind=kOutput, calls=%fused_computation.67 | convolution fusion | flops 8602517504 | bytes 51446784 | tf_op jit(solution)/shard_map/jigc,jigh->gch/dot_general | solution.py:54
  559.6 35.9 %fusion.49 = bf16[64,256,256]{1,2,0:T(8,128)(2,1)} fusion(f32[64,256,1024]{2,1,0:T(8,128)} %fusion.70, f32[64,256,256]{2,1,0:T(8,128)} %get-tuple-element.42, bf16[1,1024,256]{2,1,0:T(8,128)(2,1)S(1)} %copy-done.11), kind=kOutput, calls=%fused_computation.64 | convolution fusion | flops 8749318144 | bytes 92798976 | tf_op jit(solution)/shard_map/jigh,ghc->jigc/dot_general | solution.py:46
  595.5 12.1 %copy.84 = bf16[64,256,256]{2,1,0:T(8,128)(2,1)} copy(bf16[64,256,256]{1,2,0:T(8,128)(2,1)} %fusion.49) | data formatting | bytes 16777216
  608.9 90.8 %reduce-scatter.7.cloned.1.call-done = f32[1,32,256]{2,1,0:T(8,128)} async-done(((f32[1,256,256]{2,1,0:T(8,128)}), f32[1,32,256]{2,1,0:T(8,128)}) %reduce-scatter.7.cloned.1.call-update) | async-done | bytes 32784 | tf_op jit(solution)/shard_map/reduce_scatter | solution.py:87
  701.1 63.4 %reduce-scatter.11.cloned.1.call-done = f32[1,128,256]{2,1,0:T(8,128)} async-done(((f32[1,1024,256]{2,1,0:T(8,128)}), f32[1,128,256]{2,1,0:T(8,128)}) %reduce-scatter.11.cloned.1.call-update) | async-done | bytes 131088 | tf_op jit(solution)/shard_map/reduce_scatter | solution.py:89
  766.1 64.6 %reduce-scatter.9.cloned.1.call-done = f32[1,32,1024]{2,1,0:T(8,128)} async-done(((f32[1,256,1024]{2,1,0:T(8,128)}), f32[1,32,1024]{2,1,0:T(8,128)}) %reduce-scatter.9.cloned.1.call-update) | async-done | bytes 131088 | tf_op jit(solution)/shard_map/reduce_scatter | solution.py:88
  832.2 11.5 %copy.76 = bf16[64,256,1,256]{3,1,0,2:T(8,128)(2,1)} copy(bf16[64,256,1,256]{3,0,2,1:T(8,128)(2,1)} %all-to-all-done.1) | data formatting | bytes 16777216 | tf_op jit(solution)/shard_map/all_to_all | solution.py:15
  855.3 15.4 %copy.77 = f32[8,64,32,1,256]{4,1,0,2,3:T(8,128)S(1)} copy(f32[8,64,32,1,256]{4,2,0,1,3:T(8,128)} %convert_bitcast_fusion) | data formatting | bytes 33554432 | tf_op jit(solution)/shard_map/convert_element_type | solution.py:73
  892.8 21.5 %fusion.46 = bf16[32,512,256]{2,1,0:T(8,128)(2,1)} fusion(f32[512,32,256]{2,0,1:T(8,128)} %get-tuple-element.40, f32[8,64,32,1,256]{4,1,0,2,3:T(8,128)} %copy-done.2, bf16[32,512,1,256]{3,1,0,2:T(8,128)(2,1)} %fusion.27, bf16[1,512,512]{2,1,0:T(8,128)(2,1)S(1)} %copy-done.12, bf16[32,512,256]{2,1,0:T(8,128)(2,1)} %param.7), kind=kOutput, calls=%fused_computation.63 | convolution fusion | flops 4336910336 | bytes 59244544 | tf_op jit(solution)/shard_map/ajgc,gbj->abgc/dot_general | solution.py:77
  914.3 55.6 %all-reduce.9.cloned.1.call-done = f32[1,512,512]{2,0,1:T(1,128)} async-done(((f32[1,512,512]{2,0,1:T(1,128)}), f32[1,512,512]{2,0,1:T(1,128)}) %all-reduce.9.cloned.1.call-update) | async-done | bytes 1048592
  (68 shorter events, 83.9 us)
Async XLA Ops:
  7.2 297.6 %copy-start = (bf16[1,256,1024]{2,1,0:T(8,128)(2,1)S(1)}, bf16[1,256,1024]{2,1,0:T(8,128)(2,1)}, u32[]{:S(2)}) copy-start(bf16[1,256,1024]{2,1,0:T(8,128)(2,1)} %param.10) | copy-start | bytes 1572868
  7.2 296.1 %all-reduce.5.cloned.1.call-start = ((), (), s32[]{:S(2)}) async-start(), calls=%async_computation.6 | async-start | bytes 131072 | tf_op jit(solution)/shard_map/psum | solution.py:19
  227.1 20.0 %copy-start.7 = (bf16[1,256,256]{2,1,0:T(8,128)(2,1)S(1)}, bf16[1,256,256]{2,1,0:T(8,128)(2,1)}, u32[]{:S(2)}) copy-start(bf16[1,256,256]{2,1,0:T(8,128)(2,1)} %param.9) | copy-start | bytes 393220
  247.1 57.6 %copy-start.9 = (f32[1,256]{1,0:T(1,128)S(1)}, f32[1,256]{1,0:T(1,128)}, u32[]{:S(2)}) copy-start(f32[1,256]{1,0:T(1,128)} %param.12) | copy-start | bytes 3076
  273.0 173.7 %all-reduce.7.cloned.1.call-start = ((), (), s32[]{:S(2)}) async-start(), calls=%async_computation.7 | async-start | bytes 131072 | tf_op jit(solution)/shard_map/psum | solution.py:19
  304.8 29.3 %copy-start.4 = (f32[64,256]{1,0:T(8,128)}, f32[64,256]{1,0:T(8,128)S(1)}, u32[]{:S(2)}) copy-start(f32[64,256]{1,0:T(8,128)S(1)} %get-tuple-element.38) | copy-start | bytes 196612
  304.8 29.3 %copy-start.11 = (bf16[1,1024,256]{2,1,0:T(8,128)(2,1)S(1)}, bf16[1,1024,256]{2,1,0:T(8,128)(2,1)}, u32[]{:S(2)}) copy-start(bf16[1,1024,256]{2,1,0:T(8,128)(2,1)} %param.11) | copy-start | bytes 1572868
  334.1 54.4 %copy-start.10 = (f32[1,256]{1,0:T(1,128)S(1)}, f32[1,256]{1,0:T(1,128)}, u32[]{:S(2)}) copy-start(f32[1,256]{1,0:T(1,128)} %param.12) | copy-start | bytes 3076
  415.4 12.0 %copy-start.13 = (u32[32]{0:T(128)S(1)}, u32[32]{0:T(128)}, u32[]{:S(2)}) copy-start(u32[32]{0:T(128)} %constant.34) | copy-start | bytes 388
  415.4 32.1 %copy-start.5 = (f32[64,256]{1,0:T(8,128)S(1)}, f32[64,256]{1,0:T(8,128)}, u32[]{:S(2)}) copy-start(f32[64,256]{1,0:T(8,128)} %copy-done.4) | copy-start | bytes 196612
  415.4 32.1 %copy-start.6 = (f32[64,256]{1,0:T(8,128)S(1)}, f32[64,256]{1,0:T(8,128)}, u32[]{:S(2)}) copy-start(f32[64,256]{1,0:T(8,128)} %get-tuple-element.37) | copy-start | bytes 196612
  415.4 192.2 %reduce-scatter.13.cloned.1.call-start = ((), (), s32[]{:S(2)}) async-start(), calls=%async_computation.11 | async-start | bytes 147456
  463.0 3.4 copy-start.3
  466.4 13.4 %copy-start.8 = (bf16[1,256,256]{2,1,0:T(8,128)(2,1)S(1)}, bf16[1,256,256]{2,1,0:T(8,128)(2,1)}, u32[]{:S(2)}) copy-start(bf16[1,256,256]{2,1,0:T(8,128)(2,1)} %param.9) | copy-start | bytes 393220
  501.4 330.9 %all-to-all-start.1 = ((bf16[64,256,1,256]{3,0,2,1:T(8,128)(2,1)}), bf16[64,256,1,256]{3,0,2,1:T(8,128)(2,1)}, u32[]{:S(2)}, u32[]{:S(2)}) async-start(bf16[64,256,1,256]{3,0,2,1:T(8,128)(2,1)} %copy.75), calls=%async_computation.1 | async-start | bytes 16777216 | tf_op jit(solution)/shard_map/all_to_all | solution.py:15
  506.9 192.8 %reduce-scatter.7.cloned.1.call-start = ((), (), s32[]{:S(2)}) async-start(), calls=%async_computation.8 | async-start | bytes 294912 | tf_op jit(solution)/shard_map/reduce_scatter | solution.py:87
  507.5 257.0 %reduce-scatter.11.cloned.1.call-start = ((), (), s32[]{:S(2)}) async-start(), calls=%async_computation.10 | async-start | bytes 1179648 | tf_op jit(solution)/shard_map/reduce_scatter | solution.py:89
  538.5 292.2 %reduce-scatter.9.cloned.1.call-start = ((), (), s32[]{:S(2)}) async-start(), calls=%async_computation.9 | async-start | bytes 1179648 | tf_op jit(solution)/shard_map/reduce_scatter | solution.py:88
  559.5 410.4 %all-reduce.9.cloned.1.call-start = ((), (), s32[]{:S(2)}) async-start(), calls=%async_computation.12 | async-start | bytes 2097152
  843.8 32.6 %slice-start = ((s8[8388608]{0:T(1024)(128)(4,1)}), s8[4194304]{0:T(1024)(128)(4,1)S(1)}, s32[]{:S(2)}) async-start(s8[8388608]{0:T(1024)(128)(4,1)} %bitcast.264), calls=%async_computation.13 | async-start | bytes 8388608
  855.3 21.1 %slice-start.1 = ((s8[8388608]{0:T(1024)(128)(4,1)}), s8[4194304]{0:T(1024)(128)(4,1)S(1)}, s32[]{:S(2)}) async-start(s8[8388608]{0:T(1024)(128)(4,1)} %bitcast.264), calls=%async_computation.14 | async-start | bytes 8388608
  870.7 5.7 copy-start.2
  883.6 9.2 copy-start.12
  892.8 78.8 %copy-start.1 = (bf16[1,256,1024]{2,1,0:T(8,128)(2,1)S(1)}, bf16[1,256,1024]{2,1,0:T(8,128)(2,1)}, u32[]{:S(2)}) copy-start(bf16[1,256,1024]{2,1,0:T(8,128)(2,1)} %param.10) | copy-start | bytes 1572868
Sparse Core Ops, SparseCore 0:
  273.1 30.1 all-reduce.4
  415.5 31.1 all-reduce.6
  450.6 60.8 reduce-scatter.12
  514.7 184.9 reduce-scatter.6
  702.9 61.5 reduce-scatter.10
  768.1 62.4 reduce-scatter.8
  892.9 76.9 all-reduce.8
where the time goes:
time: 987 us; the launch traced here: 979 us
  waiting for transfers between devices  323 us (33%)
  matrix products  293 us (30%)
  blocking collectives  190 us (19%)
  local copies, waits for them, and re-layouts  109 us (11%)
  other arithmetic  42.5 us (4%)
  between operations  15.3 us (2%)
    all_to_all x1, blocking collectives, transpose_slab(): return lax.all_to_all(block, 'ctx', split_axis=1, concat_axis=0, tiled=True)  190 us
    reduce_scatter x1, waiting for transfers between devices, shards(): lax.psum_scatter(grad_second, 'ctx', scatter_dimension=1, tiled=True)  90.8 us
    reduce_scatter x1, waiting for transfers between devices, shards(): lax.psum_scatter(grad_up, 'ctx', scatter_dimension=1, tiled=True)  64.6 us
    reduce_scatter x1, waiting for transfers between devices, shards(): lax.psum_scatter(grad_down, 'ctx', scatter_dimension=1, tiled=True)  63.4 us
    unnamed x9, waiting for transfers between devices  56.2 us
    dot_general x1, matrix products, shards(): jnp.einsum('jigc,ghc->jigh', upstream, down_weight, preferred_element_typ...  54.4 us
    psum x2, waiting for transfers between devices, channel_total(): return lax.psum(partial_value, 'ch')  47.5 us
    unnamed x38, local copies, waits for them, and re-layouts  36 us
  transfers between devices with their start and end apart: 8, of which 6 were waited for; matrix products, arithmetic and copies ran while one was open for 20% of the time, Pallas kernels for 0%

commit v1 on v0

v1 whole, which is shorter than its diff:
```python
import functools

import jax
import jax.numpy as jnp
from jax import lax
from jax.experimental import pallas as pl
from jax.experimental.pallas import tpu as pltpu
from jax.sharding import PartitionSpec as P

EPSILON = 1e-05
TANH_SCALE = 0.7978845608028654
TANH_CUBIC = 0.044715
BF16 = jnp.bfloat16
F32 = jnp.float32
VMEM_LIMIT = 56 * 1024 * 1024


def sigmoid(values):
    return 0.5 * jnp.tanh(0.5 * values) + 0.5


def dot(left, right, left_dim, right_dim):
    return lax.dot_general(
        left, right, (((left_dim,), (right_dim,)), ((), ())), preferred_element_type=F32
    )


def to_row(column):
    return jnp.broadcast_to(column, (column.shape[0], 128)).T[0:1, :]


def to_column(row, width):
    spread = jnp.broadcast_to(row, (128, row.shape[1])).T
    return jnp.concatenate([spread] * (width // 128), axis=1)


def call(body, out_shape, cost, operands, in_specs, after=(), **options):
    flops, bytes_accessed = cost
    given, waits = len(operands), len(after)

    def ordered(*refs):
        body(*refs[:given], *refs[given + waits :])

    return pl.pallas_call(
        ordered,
        out_shape=out_shape,
        in_specs=[*in_specs, *([pl.BlockSpec(memory_space=pl.ANY)] * waits)],
        compiler_params=pltpu.CompilerParams(vmem_limit_bytes=VMEM_LIMIT),
        cost_estimate=pl.CostEstimate(
            flops=int(flops), bytes_accessed=int(bytes_accessed), transcendentals=0
        ),
        **options,
    )(*operands, *after)


def whole(array):
    return pl.BlockSpec(array.shape, lambda s: (0,) * array.ndim)


def first_mix_body(slab, offset, ctx, signal_ref, factor_ref, gated_ref, slope_ref, turn):
    rows, depth, width = signal_ref.shape
    piece = gated_ref.shape[0] // ctx
    count = ctx * piece
    for a in range(rows):
        first = dot(factor_ref[...], signal_ref[a], 1, 0)
        own = jnp.concatenate(
            [signal_ref[a, d * slab + offset : d * slab + offset + piece, :] for d in range(ctx)],
            axis=0,
        )
        gate = sigmoid(own.astype(F32))
        gated = first * gate
        slope_ref[a] = (gated * (1.0 - gate)).astype(BF16)
        for lane in range(width // 128):
            turn[lane, pl.ds(a, count, stride=rows), :] = gated[:, lane * 128 : (lane + 1) * 128]
    for lane in range(width // 128):
        gated_ref[:, :, lane * 128 : (lane + 1) * 128] = (
            turn[lane].reshape(count, rows, 128).astype(BF16)
        )


def first_mix(signal, factor_turned, slab, offset, ctx, after=()):
    rows, depth, width = signal.shape
    count = factor_turned.shape[0]
    block = min(16, rows)
    return call(
        functools.partial(first_mix_body, slab, offset, ctx),
        (
            jax.ShapeDtypeStruct((count, rows, width), BF16),
            jax.ShapeDtypeStruct((rows, count, width), BF16),
        ),
        (2 * rows * depth * count * width, 2 * rows * width * (depth + 2 * count)),
        (signal, factor_turned),
        [
            pl.BlockSpec((block, depth, width), lambda s: (s, 0, 0)),
            pl.BlockSpec((count, depth), lambda s: (0, 0)),
        ],
        after,
        grid=(rows // block,),
        out_specs=(
            pl.BlockSpec((count, block, width), lambda s: (0, s, 0)),
            pl.BlockSpec((block, count, width), lambda s: (s, 0, 0)),
        ),
        scratch_shapes=[pltpu.VMEM((width // 128, count * block, 128), F32)],
        name="first_mix",
    )


def tokens_of(gated_ref, t):
    ctx, _, rows, width = gated_ref.shape
    return gated_ref[:, t].reshape(ctx * rows, width)


def square_body(gated_ref, factor_ref, square_ref):
    steps, inner, _ = square_ref.shape
    for t in range(steps * inner):
        mixed = dot(factor_ref[...], tokens_of(gated_ref, t), 1, 0)
        square_ref[t // inner, t % inner : t % inner + 1, :] = to_row(
            jnp.sum(mixed * mixed, axis=1, keepdims=True)
        )


def squares(gated, factor_turned, inner, after=()):
    ctx, piece, rows, width = gated.shape
    tall = factor_turned.shape[0]
    block = min(8, piece)
    return call(
        square_body,
        jax.ShapeDtypeStruct((piece // inner, inner, tall), F32),
        (2 * piece * tall * tall * width, 2 * gated.size),
        (gated, factor_turned),
        [
            pl.BlockSpec((ctx, block, rows, width), lambda s: (0, s, 0, 0)),
            whole(factor_turned),
        ],
        after,
        grid=(piece // block,),
        out_specs=pl.BlockSpec((block // inner, inner, tall), lambda s: (s, 0, 0)),
        name="squares",
    )


def gathered(parts_ref, step, t):
    return sum(parts_ref[g, step, t : t + 1, :] for g in range(parts_ref.shape[0]))


def inverse_of(square_ref, step, t, channels):
    return lax.rsqrt(gathered(square_ref, step, t) * (1.0 / channels) + EPSILON)


def mlp_body(
    channels, carried, gated_ref, factor_ref, square_ref, gain_ref, up_ref, up_turned_ref,
    down_ref, down_turned_ref, cotangent_ref, up_in_ref, down_in_ref, gain_in_ref, *refs,
):
    (layer_ref, pull_ref, cross_ref, up_out_ref, down_out_ref, gain_out_ref,
     mixed_all, normed_all, act_all, pre_all, spread_all) = refs[carried:]
    inner = square_ref.shape[2]
    tall = factor_ref.shape[0]
    width = gain_ref.shape[1]
    hidden = up_ref.shape[1]

    @pl.when(pl.program_id(0) == 0)
    def _():
        up_out_ref[...] = up_in_ref[...]
        down_out_ref[...] = down_in_ref[...]
        gain_out_ref[...] = gain_in_ref[...]

    for t in range(inner):
        inverse = inverse_of(square_ref, 0, t, channels)
        part = slice(t * tall, (t + 1) * tall)
        mixed = dot(factor_ref[...], tokens_of(gated_ref, t), 1, 0)
        spread = to_column(inverse, width)
        mixed_all[part, :] = mixed
        spread_all[part, :] = spread
        normed_all[part, :] = (mixed * spread * gain_ref[...]).astype(BF16)
    upstream = cotangent_ref[...].reshape(inner * tall, width)
    normed = normed_all[...]
    step = min(256, hidden)
    for h in range(0, hidden, step):
        part = slice(h, h + step)
        pre = dot(normed, up_ref[:, part], 1, 0)
        back = dot(upstream, down_turned_ref[:, part], 1, 0)
        square = pre * pre
        lean = jnp.tanh(pre * (square * (TANH_SCALE * TANH_CUBIC) + TANH_SCALE))
        half = 0.5 * lean + 0.5
        act = pre * half
        act_all[:, part] = act.astype(BF16)
        bend = square * (6.0 * TANH_SCALE * TANH_CUBIC) + 2.0 * TANH_SCALE
        pre_all[:, part] = (back * (half + act * (1.0 - half) * bend)).astype(BF16)
    mixed = mixed_all[...]
    layer = mixed + dot(act_all[...], down_ref[...], 1, 0)
    layer_ref[...] = layer.astype(BF16).reshape(layer_ref.shape)
    down_out_ref[...] += dot(upstream, act_all[...], 0, 0)
    up_out_ref[...] += dot(normed, pre_all[...], 0, 0)
    grad_normed = dot(pre_all[...], up_turned_ref[...], 1, 0)
    spread = spread_all[...]
    gain = gain_ref[...]
    weighed = grad_normed * mixed
    gain_out_ref[...] += jnp.sum(weighed * spread, axis=0, keepdims=True)
    cross = jnp.sum(weighed * gain, axis=1, keepdims=True)
    for t in range(inner):
        cross_ref[0, t : t + 1, :] = to_row(cross[t * tall : (t + 1) * tall])
    pull_ref[...] = (grad_normed * gain * spread).astype(BF16).reshape(pull_ref.shape)


def mlp(gated, part, factor_turned, square, gain, up, up_turned, down, down_turned, cotangent,
        first_piece, sums, layer_pull, channels, after=()):
    ctx, _, rows, width = gated.shape
    groups, _, inner, tall = square.shape
    hidden = up.shape[1]
    begin, piece = part
    steps, skip = piece // inner, begin // inner
    start = (first_piece + begin) // inner
    tokens = inner * tall
    by_token = pl.BlockSpec((inner, tall, width), lambda s: (s + start, 0, 0))
    stays = pl.BlockSpec(memory_space=pl.ANY)
    full = jax.ShapeDtypeStruct(cotangent.shape, BF16)
    carried = len(layer_pull)
    aliases = {9: 3, 10: 4, 11: 5}
    for i in range(carried):
        aliases[12 + i] = i
    return call(
        functools.partial(mlp_body, channels, carried),
        (
            full,
            full,
            jax.ShapeDtypeStruct((steps, inner, tall), F32),
            *(jax.ShapeDtypeStruct(array.shape, F32) for array in sums),
        ),
        (12 * piece * tall * width * hidden, 8 * piece * tall * width),
        (gated, factor_turned, square, gain, up, up_turned, down, down_turned, cotangent, *sums,
         *layer_pull),
        [
            pl.BlockSpec((ctx, inner, rows, width), lambda s: (0, s + skip, 0, 0)),
            whole(factor_turned),
            pl.BlockSpec((groups, 1, inner, tall), lambda s: (0, s + skip, 0, 0)),
            whole(gain), whole(up), whole(up_turned), whole(down), whole(down_turned),
            by_token,
            *(whole(array) for array in sums),
            *([stays] * carried),
        ],
        after,
        grid=(steps,),
        out_specs=(
            by_token, by_token,
            pl.BlockSpec((1, inner, tall), lambda s: (s, 0, 0)),
            *(whole(array) for array in sums),
        ),
        scratch_shapes=[
            pltpu.VMEM((tokens, width), F32),
            pltpu.VMEM((tokens, width), BF16),
            pltpu.VMEM((tokens, hidden), BF16),
            pltpu.VMEM((tokens, hidden), BF16),
            pltpu.VMEM((tokens, width), F32),
        ],
        input_output_aliases=aliases,
        name="mlp",
    )


def second_body(
    channels, gated_ref, factor_ref, factor_turned_ref, square_ref, cross_ref, pull_ref,
    cotangent_ref, sum_in_ref, moved_ref, sum_out_ref,
):
    _, steps, inner, tall = square_ref.shape
    ctx, _, rows, width = gated_ref.shape

    @pl.when(pl.program_id(0) == 0)
    def _():
        sum_out_ref[...] = sum_in_ref[...]

    total = sum_out_ref[...]
    for t in range(steps * inner):
        gated = tokens_of(gated_ref, t)
        mixed = dot(factor_turned_ref[...], gated, 1, 0)
        inverse = inverse_of(square_ref, t // inner, t % inner, channels)
        cross = gathered(cross_ref, t // inner, t % inner)
        weight = to_column(inverse * inverse * inverse * cross * (1.0 / channels), width)
        grad = (
            cotangent_ref[t].astype(F32) + pull_ref[t].astype(F32) - mixed * weight
        ).astype(BF16)
        total += dot(gated, grad, 1, 1)
        moved_ref[:, t] = dot(factor_ref[...], grad, 1, 0).astype(BF16).reshape(ctx, rows, width)
    sum_out_ref[...] = total


def second(gated, factor, factor_turned, square, cross, pull, cotangent, first_piece, total,
           channels, after=()):
    ctx, piece, rows, width = gated.shape
    groups, steps, inner, tall = square.shape
    block = max(size for size in (4, 2, 1) if steps % size == 0)
    count = block * inner
    start = first_piece // count
    by_piece = pl.BlockSpec((groups, block, inner, tall), lambda s: (0, s, 0, 0))
    by_token = pl.BlockSpec((count, tall, width), lambda s: (s + start, 0, 0))
    return call(
        functools.partial(second_body, channels),
        (
            jax.ShapeDtypeStruct(gated.shape, BF16),
            jax.ShapeDtypeStruct(total.shape, F32),
        ),
        (6 * piece * tall * tall * width, 8 * gated.size),
        (gated, factor, factor_turned, square, cross, pull, cotangent, total),
        [
            pl.BlockSpec((ctx, count, rows, width), lambda s: (0, s, 0, 0)),
            whole(factor), whole(factor_turned), by_piece, by_piece, by_token, by_token,
            whole(total),
        ],
        after,
        grid=(steps // block,),
        out_specs=(
            pl.BlockSpec((ctx, count, rows, width), lambda s: (0, s, 0, 0)),
            whole(total),
        ),
        input_output_aliases={7: 1},
        name="second",
    )


def gate_body(slab, offset, ctx, moved_ref, signal_ref, slope_ref, first_ref, gate_ref, sum_ref,
              turn):
    rows, depth, width = signal_ref.shape
    count = moved_ref.shape[0]
    piece = count // ctx

    @pl.when(pl.program_id(0) == 0)
    def _():
        sum_ref[...] = jnp.zeros_like(sum_ref)

    for lane in range(width // 128):
        turn[lane] = (
            moved_ref[:, :, lane * 128 : (lane + 1) * 128]
            .astype(F32)
            .reshape(count * rows, 128)
        )
    total = sum_ref[...]
    for a in range(rows):
        grad = jnp.concatenate(
            [turn[lane, pl.ds(a, count, stride=rows), :] for lane in range(width // 128)], axis=1
        )
        own = jnp.concatenate(
            [signal_ref[a, d * slab + offset : d * slab + offset + piece, :] for d in range(ctx)],
            axis=0,
        )
        first = (grad * sigmoid(own.astype(F32))).astype(BF16)
        first_ref[a] = first
        gate_ref[a] = (grad * slope_ref[a].astype(F32)).astype(BF16)
        total += dot(signal_ref[a], first, 1, 1)
    sum_ref[...] = total


def gate(moved, signal, slope, slab, offset, ctx, after=()):
    rows, depth, width = signal.shape
    count = moved.shape[0]
    block = min(16, rows)
    by_row = pl.BlockSpec((block, count, width), lambda s: (s, 0, 0))
    return call(
        functools.partial(gate_body, slab, offset, ctx),
        (
            jax.ShapeDtypeStruct((rows, count, width), BF16),
            jax.ShapeDtypeStruct((rows, count, width), BF16),
            jax.ShapeDtypeStruct((depth, count), F32),
        ),
        (2 * rows * depth * count * width, 2 * rows * width * (depth + 4 * count)),
        (moved, signal, slope),
        [
            pl.BlockSpec((count, block, width), lambda s: (0, s, 0)),
            pl.BlockSpec((block, depth, width), lambda s: (s, 0, 0)),
            by_row,
        ],
        after,
        grid=(rows // block,),
        out_specs=(by_row, by_row, pl.BlockSpec((depth, count), lambda s: (0, 0))),
        scratch_shapes=[pltpu.VMEM((width // 128, count * block, 128), F32)],
        name="gate",
    )


def signal_body(offsets, slab, ctx, factor_ref, *refs):
    pieces = len(offsets)
    firsts, gates, out_ref = refs[:pieces], refs[pieces : 2 * pieces], refs[-1]
    for a in range(out_ref.shape[0]):
        grads = jnp.concatenate([first[a] for first in firsts], axis=0)
        total = dot(factor_ref[...], grads, 1, 0)
        for gate_ref, offset in zip(gates, offsets):
            piece = gate_ref.shape[1] // ctx
            for d in range(ctx):
                place = slice(d * slab + offset, d * slab + offset + piece)
                out_ref[a, place, :] = (
                    total[place] + gate_ref[a, d * piece : (d + 1) * piece, :].astype(F32)
                ).astype(BF16)


def signal_grad(factor, firsts, gates, offsets, slab, ctx, after=()):
    rows, _, width = firsts[0].shape
    depth = factor.shape[0]
    block = min(4, rows)
    by_row = [pl.BlockSpec((block, *array.shape[1:]), lambda s: (s, 0, 0)) for array in firsts]
    return call(
        functools.partial(signal_body, offsets, slab, ctx),
        jax.ShapeDtypeStruct((rows, depth, width), BF16),
        (2 * rows * depth * depth * width, 6 * rows * depth * width),
        (factor, *firsts, *gates),
        [whole(factor), *by_row, *by_row],
        after,
        grid=(rows // block,),
        out_specs=pl.BlockSpec((block, depth, width), lambda s: (s, 0, 0)),
        name="signal_grad",
    )


def scatter_total(partial_sum, ctx):
    if ctx & (ctx - 1):
        return lax.psum_scatter(partial_sum, "ctx", scatter_dimension=0, tiled=False)
    me = lax.axis_index("ctx")
    bit = 1
    values = partial_sum
    while bit < ctx:
        halves = values.reshape((-1, 2) + values.shape[1:])
        mine = (me // bit) % 2
        keep = lax.dynamic_index_in_dim(halves, mine, 1, keepdims=False)
        give = lax.dynamic_index_in_dim(halves, 1 - mine, 1, keepdims=False)
        got = lax.ppermute(give.astype(BF16), "ctx", [(i, i ^ bit) for i in range(ctx)])
        values = keep + got.astype(F32)
        bit *= 2
    return values[0]


def block_total_body(parts_ref, total_ref):
    total_ref[...] = jnp.sum(parts_ref[...].astype(F32), axis=0)


def block_total(parts, after=()):
    return call(
        block_total_body,
        jax.ShapeDtypeStruct(parts.shape[1:], F32),
        (parts.size, 4 * parts.size),
        (parts,),
        [whole(parts)],
        after,
        grid=(1,),
        out_specs=pl.BlockSpec(parts.shape[1:], lambda s: (0, 0)),
        name="block_total",
    )


def from_groups(partial_value):
    return lax.all_gather(partial_value, "ch")


def exchange(block):
    return lax.all_to_all(block, "ctx", split_axis=0, concat_axis=0, tiled=True)


def shards(ctx, channels, token_count, signal, factor_first, factor_second, up_weight,
           down_weight, norm_gain, cotangent):
    rows, depth, width = signal.shape
    slab, tall, _ = cotangent.shape
    first, factor = factor_first[0], factor_second[0]
    up, down = up_weight[0], down_weight[0]
    hidden = up.shape[1]
    factor_turned, up_turned, down_turned = factor.T, up.T, down.T
    unit = min(16, slab)
    sizes = (unit, slab - 2 * unit, unit) if slab > 2 * unit else (slab,)
    last = len(sizes) - 1
    offsets = tuple(sum(sizes[:k]) for k in range(len(sizes)))
    inner = 2
    by_owner = first.reshape(depth, ctx, slab)
    columns = [
        by_owner[:, :, start : start + size].reshape(depth, ctx * size)
        for start, size in zip(offsets, sizes)
    ]
    mix = lambda k, after=(): first_mix(signal, columns[k].T, slab, offsets[k], ctx, after)
    sent = lambda k, gated: exchange(gated).reshape(ctx, sizes[k], rows, width)
    total = len(sizes)
    slopes, arrived, squared, crossed, moved = ([None] * total for _ in range(5))
    sums = (
        jnp.zeros((width, hidden), F32),
        jnp.zeros((width, hidden), F32),
        jnp.zeros((1, width), F32),
    )
    state = dict(sums=sums, layer_pull=(), second=jnp.zeros((tall, tall), F32))

    def square_of(k, after=()):
        squared[k] = from_groups(squares(arrived[k], factor_turned, inner, after))

    def mlp_of(k, begin, size, after=()):
        layer, pull, cross, *new_sums = mlp(
            arrived[k], (begin, size), factor_turned, squared[k], norm_gain, up, up_turned, down,
            down_turned, cotangent, offsets[k], state["sums"], state["layer_pull"], channels,
            after,
        )
        state.update(sums=new_sums, layer_pull=(layer, pull))
        return cross

    def second_of(k, after=()):
        out, state["second"] = second(
            arrived[k], factor, factor_turned, squared[k], crossed[k], state["layer_pull"][1],
            cotangent, offsets[k], state["second"], channels, after,
        )
        moved[k] = out.reshape(ctx * sizes[k], rows, width)
        return out

    def back(k):
        moved[k] = exchange(moved[k])

    def gate_of(k, after=()):
        return gate(moved[k], signal, slopes[k], slab, offsets[k], ctx, after)

    first_block = lambda sums: sums.reshape(ctx, depth // ctx, sums.shape[1])
    outs = [None] * total
    gated, slopes[0] = mix(0)
    arrived[0] = sent(0, gated)
    if last:
        gated, slopes[1] = mix(1)
        arrived[1] = sent(1, gated)
        square_of(0)
        cross_0 = mlp_of(0, 0, sizes[0])
        gated, slopes[2] = mix(2, (cross_0,))
        arrived[2] = sent(2, gated)
        crossed[0] = from_groups(cross_0)
        square_of(1, (cross_0,))
        cross_1 = mlp_of(1, 0, unit)
        done = second_of(0, (cross_1,))
        back(0)
        cross_2 = mlp_of(1, unit, sizes[1] - unit, (done,))
        crossed[1] = from_groups(jnp.concatenate([cross_1, cross_2]))
        done = second_of(1)
        back(1)
        square_of(2, (done, moved[0]))
        crossed[2] = from_groups(mlp_of(2, 0, sizes[2]))
        done = second_of(2)
        back(2)
    else:
        square_of(0)
        crossed[0] = from_groups(mlp_of(0, 0, sizes[0]))
        done = second_of(0)
        back(0)
    for k in range(total):
        outs[k] = gate_of(k)
    first_sums = [
        scatter_total(first_block(out[2]), ctx).reshape(depth // ctx, ctx, size)
        for out, size in zip(outs[:-1], sizes)
    ]
    parts = exchange(outs[-1][2].astype(BF16)).reshape(ctx, depth // ctx, ctx * sizes[-1])
    grad_signal = signal_grad(
        jnp.concatenate(columns, axis=1),
        [out[0] for out in outs], [out[1] for out in outs], offsets, slab, ctx,
    )
    first_sums.append(
        block_total(parts, (grad_signal,)).reshape(depth // ctx, ctx, sizes[-1])
    )
    scale = token_count ** (-0.5)
    grad_first = jnp.concatenate(first_sums, axis=2).reshape(1, depth // ctx, depth)
    up_sum, down_sum, gain_sum = state["sums"]
    packed = jnp.concatenate(
        [
            up_sum.reshape(ctx, width // ctx * (hidden // tall), tall),
            down_sum.T.reshape(ctx, hidden * width // (ctx * tall), tall),
            state["second"].reshape(ctx, tall // ctx, tall),
            jnp.broadcast_to(gain_sum.reshape(ctx, width // ctx, 1), (ctx, width // ctx, tall)),
        ],
        axis=1,
    )
    packed = scatter_total(packed, ctx) * scale
    ends = (width // ctx * (hidden // tall), hidden * width // (ctx * tall), tall // ctx)
    a, b, c = ends[0], ends[0] + ends[1], sum(ends)
    return (
        state["layer_pull"][0],
        grad_signal,
        grad_first * scale,
        packed[b:c][None],
        packed[:a].reshape(1, width // ctx, hidden),
        packed[a:b].reshape(1, hidden // ctx, width),
        packed[c:, 0][None],
    )


def solution(mesh):
    placed = (
        P("ctx", None, "ch"),
        P("ch", None, None),
        P("ch", None, None),
        P("ch", None, None),
        P("ch", None, None),
        P("ch", None),
        P("ctx", None, "ch"),
    )

    def layer(signal, factor_first, factor_second, up_weight, down_weight, norm_gain, cotangent):
        body = functools.partial(
            shards, mesh.shape["ctx"], signal.shape[2], signal.shape[0] * signal.shape[1]
        )
        return jax.shard_map(
            body,
            mesh=mesh,
            in_specs=placed,
            out_specs=(
                P("ctx", None, "ch"),
                P("ctx", None, "ch"),
                P("ch", "ctx", None),
                P("ch", "ctx", None),
                P("ch", "ctx", None),
                P("ch", "ctx", None),
                P("ch", "ctx"),
            ),
            check_vma=False,
        )(signal, factor_first, factor_second, up_weight, down_weight, norm_gain, cotangent)

    return layer
```

time: 987 us -> 504 us (0.51)
  matrix products: 293 us -> 0 us
  Pallas kernels: 0 us -> 205 us
  blocking collectives: 190 us -> 37.1 us
  waiting for transfers between devices: 323 us -> 176 us
  local copies, waits for them, and re-layouts: 109 us -> 25.4 us
  starting transfers between devices: 5.81 us -> 42.6 us
  other arithmetic: 42.5 us -> 7.56 us
  between operations: 15.3 us -> 1.59 us
    dot_general x12 -> x0, matrix products: 293 us -> none  [the longest x1 54.4 us: shards(): jnp.einsum('jigc,ghc->jigh', upstream, down_weight, preferred_element_typ...]
    reduce_scatter x3 -> x0, waiting for transfers between devices: 219 us -> none  [the longest x1 90.8 us: shards(): lax.psum_scatter(grad_second, 'ctx', scatter_dimension=1, tiled=True)]
    pallas_call x0 -> x18, Pallas kernels: none -> 205 us  [call(): pl.pallas_call(ordered, out_shape=out_shape, in_specs=[*in_specs, *[pl.Bl...]
    all_to_all x1 -> x0, blocking collectives: 190 us -> none  [transpose_slab(): return lax.all_to_all(block, 'ctx', split_axis=1, concat_axis=0, tiled=True)]
    all_to_all x1 -> x7, waiting for transfers between devices: 0.01 us -> 124 us  [exchange(): return lax.all_to_all(block, 'ctx', split_axis=0, concat_axis=0, tiled=True)]
    unnamed x9 -> x0, waiting for transfers between devices: 56.2 us -> none
    ppermute x0 -> x9, waiting for transfers between devices: none -> 51.6 us  [scatter_total(): lax.ppermute(give.astype(BF16), 'ctx', [(i, i ^ bit) for i in range(ctx)])]
    psum x2 -> x0, waiting for transfers between devices: 47.5 us -> none  [channel_total(): return lax.psum(partial_value, 'ch')]
  transfers between devices with their start and end apart: 8 -> 16, of which waited for: 6 -> 9; matrix products, arithmetic and copies ran while one was open for 20% -> 5% of each run, Pallas kernels for 0% -> 40%
where the time goes in v1:
time: 504 us; the launch traced here: 495 us
  Pallas kernels  205 us (41%)
  waiting for transfers between devices  176 us (35%)
  starting transfers between devices  42.6 us (8%)
  blocking collectives  37.1 us (7%)
  local copies, waits for them, and re-layouts  25.4 us (5%)
  other arithmetic  7.56 us (2%)
    pallas_call x18, Pallas kernels, call(): pl.pallas_call(ordered, out_shape=out_shape, in_specs=[*in_specs, *[pl.Bl...  205 us
    all_to_all x7, waiting for transfers between devices, exchange(): return lax.all_to_all(block, 'ctx', split_axis=0, concat_axis=0, tiled=True)  124 us
    ppermute x9, waiting for transfers between devices, scatter_total(): lax.ppermute(give.astype(BF16), 'ctx', [(i, i ^ bit) for i in range(ctx)])  51.6 us
    all_gather x6, blocking collectives, from_groups(): return lax.all_gather(partial_value, 'ch')  37.1 us
    all_to_all x7, starting transfers between devices, exchange(): return lax.all_to_all(block, 'ctx', split_axis=0, concat_axis=0, tiled=True)  33.6 us
  transfers between devices with their start and end apart: 16, of which 9 were waited for; matrix products, arithmetic and copies ran while one was open for 5% of the time, Pallas kernels for 40%

profile of v1, /device:TPU:0, one launch (start us, length us, event | category | flops | bytes accessed | tf_op | source)
XLA Modules:
  0.0 494.8 jit_solution(2813704124553833465)
XLA Ops:
  2.6 6.6 %first_mix.3 = (bf16[128,32,256]{2,1,0:T(8,128)(2,1)}, bf16[32,128,256]{2,1,0:T(8,128)(2,1)}) custom-call(bf16[32,512,256]{2,1,0:T(8,128)(2,1)} %refs_1_.5, bf16[128,512]{1,0:T(8,128)(2,1)} %bitcast.115), custom_call_target="tpu_custom_call" | custom-call | flops 1073741824 | bytes 12582912 | tf_op jit(solution)/shard_map/first_mix/pallas_call | solution.py:44
  9.2 7.3 %all-to-all-start = ((bf16[128,32,256]{2,1,0:T(8,128)(2,1)}), bf16[128,32,256]{2,1,0:T(8,128)(2,1)S(1)}, u32[]{:S(2)}, u32[]{:S(2)}) async-start(bf16[128,32,256]{2,1,0:T(8,128)(2,1)} %get-tuple-element.52), calls=%async_computation | async-start | bytes 4194304 | tf_op jit(solution)/shard_map/all_to_all | solution.py:451
  17.2 9.9 %first_mix.5 = (bf16[256,32,256]{2,1,0:T(8,128)(2,1)}, bf16[32,256,256]{2,1,0:T(8,128)(2,1)}) custom-call(bf16[32,512,256]{2,1,0:T(8,128)(2,1)} %refs_1_.5, bf16[256,512]{1,0:T(8,128)(2,1)} %bitcast.103), custom_call_target="tpu_custom_call" | custom-call | flops 2147483648 | bytes 16777216 | tf_op jit(solution)/shard_map/first_mix/pallas_call | solution.py:44
  27.1 37.6 %all-to-all-done = bf16[128,32,256]{2,1,0:T(8,128)(2,1)S(1)} async-done(((bf16[128,32,256]{2,1,0:T(8,128)(2,1)}), bf16[128,32,256]{2,1,0:T(8,128)(2,1)S(1)}, u32[]{:S(2)}, u32[]{:S(2)}) %all-to-all-start) | async-done | bytes 2097184 | tf_op jit(solution)/shard_map/all_to_all | solution.py:451
  76.8 6.6 %all-gather = f32[32,2,256]{2,1,0:T(2,128)} all-gather(f32[8,2,256]{2,1,0:T(2,128)} %squares.3), channel_id=2, replica_groups=mesh['ctx'=8,'ch'=4] {'ch'}, dimensions={0}, use_global_device_ids=true | all-gather | bytes 81920 | tf_op jit(solution)/shard_map/all_gather | solution.py:447
  86.3 25.2 %mlp.4 = (bf16[64,256,256]{2,1,0:T(8,128)(2,1)}, bf16[64,256,256]{2,1,0:T(8,128)(2,1)}, f32[8,2,256]{2,1,0:T(2,128)}, f32[256,1024]{1,0:T(8,128)}, f32[256,1024]{1,0:T(8,128)}, /*index=5*/f32[1,256]{1,0:T(1,128)}) custom-call(bf16[8,16,32,256]{3,2,1,0:T(8,128)(2,1)} %bitcast.86, ...), custom_call_target="tpu_custom_call", output_to_operand_aliasing={{3}: (9, {}), {4}: (10, {}), {5}: (11, {})} | custom-call | flops 12884901888 | bytes 8388608 | tf_op jit(solution)/shard_map/mlp/pallas_call | solution.py:44
  111.5 6.6 %first_mix.4 = (bf16[128,32,256]{2,1,0:T(8,128)(2,1)}, bf16[32,128,256]{2,1,0:T(8,128)(2,1)}) custom-call(bf16[32,512,256]{2,1,0:T(8,128)(2,1)} %refs_1_.5, bf16[128,512]{1,0:T(8,128)(2,1)} %bitcast.113, f32[8,2,256]{2,1,0:T(2,128)} %get-tuple-element.53.refs_2_), custom_call_target="tpu_custom_call" | custom-call | flops 1073741824 | bytes 12582912 | tf_op jit(solution)/shard_map/first_mix/pallas_call | solution.py:44
  118.1 45.0 %all-to-all-done.2 = bf16[256,32,256]{2,1,0:T(8,128)(2,1)} async-done(((bf16[256,32,256]{2,1,0:T(8,128)(2,1)}), bf16[256,32,256]{2,1,0:T(8,128)(2,1)}, u32[]{:S(2)}, u32[]{:S(2)}) %all-to-all-start.2) | async-done | bytes 4194336 | tf_op jit(solution)/shard_map/all_to_all | solution.py:451
  177.9 7.1 %all-gather.1 = f32[64,2,256]{2,1,0:T(2,128)} all-gather(f32[16,2,256]{2,1,0:T(2,128)} %squares.4), channel_id=3, replica_groups=mesh['ctx'=8,'ch'=4] {'ch'}, dimensions={0}, use_global_device_ids=true | all-gather | bytes 163840 | tf_op jit(solution)/shard_map/all_gather | solution.py:447
  185.0 25.4 %mlp.5 = (bf16[64,256,256]{2,1,0:T(8,128)(2,1)}, bf16[64,256,256]{2,1,0:T(8,128)(2,1)}, f32[8,2,256]{2,1,0:T(2,128)}, f32[256,1024]{1,0:T(8,128)}, f32[256,1024]{1,0:T(8,128)}, /*index=5*/f32[1,256]{1,0:T(1,128)}) custom-call(bf16[8,32,32,256]{3,2,1,0:T(8,128)(2,1)} %bitcast.19.refs_0_, ...), custom_call_target="tpu_custom_call", output_to_operand_aliasing={{3}: (9, {}), {4}: (10, {}), {5}: (11, {}), {0}: (12, {}), ... | custom-call | flops 12884901888 | bytes 8388608 | tf_op jit(solution)/shard_map/mlp/pallas_call | solution.py:44
  211.1 7.8 %second.3 = (bf16[8,16,32,256]{3,2,1,0:T(8,128)(2,1)}, f32[256,256]{1,0:T(8,128)}) custom-call(bf16[8,16,32,256]{3,2,1,0:T(8,128)(2,1)} %bitcast.87, bf16[256,256]{1,0:T(8,128)(2,1)} %bitcast.105, bf16[256,256]{1,0:T(8,128)(2,1)} %bitcast.94, f32[4,8,2,256]{3,2,1,0:T(2,128)} %bitcast.146, ...), custom_call_target="tpu_custom_call", output_to_operand_aliasing={{1}: (7, {})} | custom-call | flops 1610612736 | bytes 8388608 | tf_op jit(solution)/shard_map/second/pallas_call | solution.py:44
  224.9 25.4 %mlp.6 = (bf16[64,256,256]{2,1,0:T(8,128)(2,1)}, bf16[64,256,256]{2,1,0:T(8,128)(2,1)}, f32[8,2,256]{2,1,0:T(2,128)}, f32[256,1024]{1,0:T(8,128)}, f32[256,1024]{1,0:T(8,128)}, /*index=5*/f32[1,256]{1,0:T(1,128)}) custom-call(bf16[8,32,32,256]{3,2,1,0:T(8,128)(2,1)} %bitcast.19.refs_0_, ...), custom_call_target="tpu_custom_call", output_to_operand_aliasing={{3}: (9, {}), {4}: (10, {}), {5}: (11, {}), {0}: (12, {}), ... | custom-call | flops 12884901888 | bytes 8388608 | tf_op jit(solution)/shard_map/mlp/pallas_call | solution.py:44
  256.9 12.5 %second.4 = (bf16[8,32,32,256]{3,2,1,0:T(8,128)(2,1)}, f32[256,256]{1,0:T(8,128)}) custom-call(bf16[8,32,32,256]{3,2,1,0:T(8,128)(2,1)} %bitcast.19.refs_0_, bf16[256,256]{1,0:T(8,128)(2,1)} %bitcast.106, bf16[256,256]{1,0:T(8,128)(2,1)} %bitcast.96, f32[4,16,2,256]{3,2,1,0:T(2,128)} %bitcast.122, ...), custom_call_target="tpu_custom_call", output_to_operand_aliasing={{1}: (7, {})} | custom-call | flops 3221225472 | bytes 16777216 | tf_op jit(solution)/shard_map/second/pallas_call | solution.py:44
  283.7 6.1 %all-gather.4 = f32[32,2,256]{2,1,0:T(2,128)} all-gather(f32[8,2,256]{2,1,0:T(2,128)} %squares.5), channel_id=6, replica_groups=mesh['ctx'=8,'ch'=4] {'ch'}, dimensions={0}, use_global_device_ids=true | all-gather | bytes 81920 | tf_op jit(solution)/shard_map/all_gather | solution.py:447
  289.8 25.3 %mlp.7 = (bf16[64,256,256]{2,1,0:T(8,128)(2,1)}, bf16[64,256,256]{2,1,0:T(8,128)(2,1)}, f32[8,2,256]{2,1,0:T(2,128)}, f32[256,1024]{1,0:T(8,128)}, f32[256,1024]{1,0:T(8,128)}, /*index=5*/f32[1,256]{1,0:T(1,128)}) custom-call(bf16[8,16,32,256]{3,2,1,0:T(8,128)(2,1)} %bitcast.83, ...), custom_call_target="tpu_custom_call", output_to_operand_aliasing={{3}: (9, {}), {4}: (10, {}), {5}: (11, {}), {0}: (12, {}), ... | custom-call | flops 12884901888 | bytes 8388608 | tf_op jit(solution)/shard_map/mlp/pallas_call | solution.py:44
  326.3 7.8 %second.5 = (bf16[8,16,32,256]{3,2,1,0:T(8,128)(2,1)}, f32[256,256]{1,0:T(8,128)}) custom-call(bf16[8,16,32,256]{3,2,1,0:T(8,128)(2,1)} %bitcast.84, bf16[256,256]{1,0:T(8,128)(2,1)} %bitcast.107, bf16[256,256]{1,0:T(8,128)(2,1)} %bitcast.99, f32[4,8,2,256]{3,2,1,0:T(2,128)} %bitcast.148, ...), custom_call_target="tpu_custom_call", output_to_operand_aliasing={{1}: (7, {})} | custom-call | flops 1610612736 | bytes 8388608 | tf_op jit(solution)/shard_map/second/pallas_call | solution.py:44
  334.1 37.3 %all-to-all-done.4.refs_0_ = bf16[256,32,256]{2,1,0:T(8,128)(2,1)} async-done(((bf16[256,32,256]{2,1,0:T(8,128)(2,1)}), bf16[256,32,256]{2,1,0:T(8,128)(2,1)}, u32[]{:S(2)}, u32[]{:S(2)}) %all-to-all-start.4) | async-done | bytes 4194336 | tf_op jit(solution)/shard_map/all_to_all | solution.py:451
  379.0 7.3 %gate.3 = (bf16[32,128,256]{2,1,0:T(8,128)(2,1)}, bf16[32,128,256]{2,1,0:T(8,128)(2,1)}, f32[512,128]{1,0:T(8,128)}) custom-call(bf16[128,32,256]{2,1,0:T(8,128)(2,1)} %all-to-all-done.3.refs_3_.refs_0_, bf16[32,512,256]{2,1,0:T(8,128)(2,1)} %refs_1_.5, bf16[32,128,256]{2,1,0:T(8,128)(2,1)} %get-tuple-element.77.refs_2_), custom_call_target="tpu_custom_call" | custom-call | flops 1073741824 | bytes 16777216 | tf_op jit(solution)/shard_map/gate/pallas_call | solution.py:44
  388.2 27.4 %collective-permute-done = bf16[4,64,128]{2,1,0:T(8,128)(2,1)S(1)} collective-permute-done((bf16[4,64,128]{2,1,0:T(8,128)(2,1)S(1)}, bf16[4,64,128]{2,1,0:T(8,128)(2,1)S(1)}, u32[]{:S(2)}, u32[]{:S(2)}) %collective-permute-start) | collective-permute-done | bytes 65568 | tf_op jit(solution)/shard_map/ppermute | solution.py:422
  424.8 6.9 %collective-permute-done.7 = bf16[2,320,256]{2,1,0:T(8,128)(2,1)S(1)} collective-permute-done((bf16[2,320,256]{2,1,0:T(8,128)(2,1)S(1)}, bf16[2,320,256]{2,1,0:T(8,128)(2,1)S(1)}, u32[]{:S(2)}, u32[]{:S(2)}) %collective-permute-start.7) | collective-permute-done | bytes 327712 | tf_op jit(solution)/shard_map/ppermute | solution.py:422
  432.3 9.7 %collective-permute-done.8 = bf16[1,320,256]{2,1,0:T(8,128)(2,1)S(1)} collective-permute-done((bf16[1,320,256]{2,1,0:T(8,128)(2,1)S(1)}, bf16[1,320,256]{2,1,0:T(8,128)(2,1)S(1)}, u32[]{:S(2)}, u32[]{:S(2)}) %collective-permute-start.8) | collective-permute-done | bytes 163872 | tf_op jit(solution)/shard_map/ppermute | solution.py:422
  442.1 10.6 %gate.4 = (bf16[32,256,256]{2,1,0:T(8,128)(2,1)}, bf16[32,256,256]{2,1,0:T(8,128)(2,1)}, f32[512,256]{1,0:T(8,128)}) custom-call(bf16[256,32,256]{2,1,0:T(8,128)(2,1)} %all-to-all-done.4.refs_0_, bf16[32,512,256]{2,1,0:T(8,128)(2,1)} %refs_1_.5, bf16[32,256,256]{2,1,0:T(8,128)(2,1)} %get-tuple-element.79.refs_2_), custom_call_target="tpu_custom_call" | custom-call | flops 2147483648 | bytes 25165824 | tf_op jit(solution)/shard_map/gate/pallas_call | solution.py:44
  461.6 7.2 %gate.5 = (bf16[32,128,256]{2,1,0:T(8,128)(2,1)}, bf16[32,128,256]{2,1,0:T(8,128)(2,1)}, f32[512,128]{1,0:T(8,128)}) custom-call(bf16[128,32,256]{2,1,0:T(8,128)(2,1)} %copy-done.2, bf16[32,512,256]{2,1,0:T(8,128)(2,1)} %refs_1_.5, bf16[32,128,256]{2,1,0:T(8,128)(2,1)} %get-tuple-element.85.refs_2_), custom_call_target="tpu_custom_call" | custom-call | flops 1073741824 | bytes 16777216 | tf_op jit(solution)/shard_map/gate/pallas_call | solution.py:44
  477.1 13.3 %signal_grad.1.refs_1_ = bf16[32,512,256]{2,1,0:T(8,128)(2,1)} custom-call(bf16[512,512]{1,0:T(8,128)(2,1)} %pad_maximum_fusion.1.refs_0_, bf16[32,128,256]{2,1,0:T(8,128)(2,1)} %get-tuple-element.78.refs_1_, bf16[32,256,256]{2,1,0:T(8,128)(2,1)} %get-tuple-element.80.refs_2_, bf16[32,128,256]{2,1,0:T(8,128)(2,1)} %get-tuple-element.86.refs_3_, ...), custom_call_target="tpu_custom_call" | custom-call | flops 4294967296 | bytes 25165824 | tf_op jit(solution)/shard_map/signal_grad/pallas_call | solution.py:44
  (120 shorter events, 111.3 us)
Async XLA Ops:
  9.2 55.5 %all-to-all-start = ((bf16[128,32,256]{2,1,0:T(8,128)(2,1)}), bf16[128,32,256]{2,1,0:T(8,128)(2,1)S(1)}, u32[]{:S(2)}, u32[]{:S(2)}) async-start(bf16[128,32,256]{2,1,0:T(8,128)(2,1)} %get-tuple-element.52), calls=%async_computation | async-start | bytes 4194304 | tf_op jit(solution)/shard_map/all_to_all | solution.py:451
  64.7 6.6 %copy-start.11 = (bf16[1,256,1024]{2,1,0:T(8,128)(2,1)S(1)}, bf16[1,256,1024]{2,1,0:T(8,128)(2,1)}, u32[]{:S(2)}) copy-start(bf16[1,256,1024]{2,1,0:T(8,128)(2,1)} %param.10) | copy-start | bytes 1572868
  64.7 7.6 %copy-start.12 = (bf16[1,1024,256]{2,1,0:T(8,128)(2,1)S(1)}, bf16[1,1024,256]{2,1,0:T(8,128)(2,1)}, u32[]{:S(2)}) copy-start(bf16[1,1024,256]{2,1,0:T(8,128)(2,1)} %param.11) | copy-start | bytes 1572868
  66.0 97.1 %all-to-all-start.2 = ((bf16[256,32,256]{2,1,0:T(8,128)(2,1)}), bf16[256,32,256]{2,1,0:T(8,128)(2,1)}, u32[]{:S(2)}, u32[]{:S(2)}) async-start(bf16[256,32,256]{2,1,0:T(8,128)(2,1)} %get-tuple-element.55), calls=%async_computation.2 | async-start | bytes 8388608 | tf_op jit(solution)/shard_map/all_to_all | solution.py:451
  118.1 48.7 %copy-start.14 = (f32[8,2,256]{2,1,0:T(2,128)S(1)}, f32[8,2,256]{2,1,0:T(2,128)}, u32[]{:S(2)}) copy-start(f32[8,2,256]{2,1,0:T(2,128)} %get-tuple-element.53.refs_2_) | copy-start | bytes 49156
  163.1 55.8 %all-to-all-start.1 = ((bf16[128,32,256]{2,1,0:T(8,128)(2,1)}), bf16[128,32,256]{2,1,0:T(8,128)(2,1)S(1)}, u32[]{:S(2)}, u32[]{:S(2)}) async-start(bf16[128,32,256]{2,1,0:T(8,128)(2,1)} %get-tuple-element.54), calls=%async_computation.1 | async-start | bytes 4194304 | tf_op jit(solution)/shard_map/all_to_all | solution.py:451
  218.9 31.4 %copy-start = (bf16[128,32,256]{2,1,0:T(8,128)(2,1)}, bf16[128,32,256]{2,1,0:T(8,128)(2,1)S(1)}, u32[]{:S(2)}) copy-start(bf16[128,32,256]{2,1,0:T(8,128)(2,1)S(1)} %all-to-all-done.1) | copy-start | bytes 6291460
  218.9 54.8 %all-to-all-start.3 = ((bf16[128,32,256]{2,1,0:T(8,128)(2,1)}), bf16[128,32,256]{2,1,0:T(8,128)(2,1)}, u32[]{:S(2)}, u32[]{:S(2)}) async-start(bf16[128,32,256]{2,1,0:T(8,128)(2,1)} %bitcast.109), calls=%async_computation.3 | async-start | bytes 4194304 | tf_op jit(solution)/shard_map/all_to_all | solution.py:451
  224.9 25.4 %copy-start.15 = (f32[8,2,256]{2,1,0:T(2,128)S(1)}, f32[8,2,256]{2,1,0:T(2,128)}, u32[]{:S(2)}) copy-start(f32[8,2,256]{2,1,0:T(2,128)} %get-tuple-element.61.refs_8_) | copy-start | bytes 49156
  273.8 97.6 %all-to-all-start.4 = ((bf16[256,32,256]{2,1,0:T(8,128)(2,1)}), bf16[256,32,256]{2,1,0:T(8,128)(2,1)}, u32[]{:S(2)}, u32[]{:S(2)}) async-start(bf16[256,32,256]{2,1,0:T(8,128)(2,1)} %bitcast.88), calls=%async_computation.4 | async-start | bytes 8388608 | tf_op jit(solution)/shard_map/all_to_all | solution.py:451
  334.1 41.3 %copy-start.3 = (f32[256,256]{1,0:T(8,128)S(1)}, f32[256,256]{1,0:T(8,128)}, u32[]{:S(2)}) copy-start(f32[256,256]{1,0:T(8,128)} %get-tuple-element.95) | copy-start | bytes 786436
  371.3 88.9 %all-to-all-start.5 = ((bf16[128,32,256]{2,1,0:T(8,128)(2,1)}), bf16[128,32,256]{2,1,0:T(8,128)(2,1)S(1)}, u32[]{:S(2)}, u32[]{:S(2)}) async-start(bf16[128,32,256]{2,1,0:T(8,128)(2,1)} %bitcast.108), calls=%async_computation.5 | async-start | bytes 4194304 | tf_op jit(solution)/shard_map/all_to_all | solution.py:451
  376.9 39.8 %collective-permute-start.6 = (bf16[4,320,256]{2,1,0:T(8,128)(2,1)S(1)}, bf16[4,320,256]{2,1,0:T(8,128)(2,1)S(1)}, u32[]{:S(2)}, u32[]{:S(2)}) collective-permute-start(bf16[4,320,256]{2,1,0:T(8,128)(2,1)S(1)} %fusion), channel_id=1, source_target_pairs={{0,4},{4,0},{8,12},{12,8},{16,20},{20,16},{24,28},{28,24},{1,5},{5... | collective-permute-start | bytes 1966088 | tf_op jit(solution)/shard_map/ppermute | solution.py:422
  379.0 8.4 %copy-start.9 = (bf16[512,256]{1,0:T(8,128)(2,1)S(1)}, bf16[512,256]{1,0:T(8,128)(2,1)}, u32[]{:S(2)}) copy-start(bf16[512,256]{1,0:T(8,128)(2,1)} %copy.121) | copy-start | bytes 786436
  379.0 8.4 %copy-start.13 = (bf16[512,128]{1,0:T(8,128)(2,1)S(1)}, bf16[512,128]{1,0:T(8,128)(2,1)}, u32[]{:S(2)}) copy-start(bf16[512,128]{1,0:T(8,128)(2,1)} %copy.122) | copy-start | bytes 393220
  387.2 28.4 %collective-permute-start = (bf16[4,64,128]{2,1,0:T(8,128)(2,1)S(1)}, bf16[4,64,128]{2,1,0:T(8,128)(2,1)S(1)}, u32[]{:S(2)}, u32[]{:S(2)}) collective-permute-start(bf16[4,64,128]{2,1,0:T(8,128)(2,1)S(1)} %fusion.4), channel_id=1, source_target_pairs={{0,4},{4,0},{8,12},{12,8},{16,20},{20,16},{24,28},{28,24},{1,5},{5... | collective-permute-start | bytes 196616 | tf_op jit(solution)/shard_map/ppermute | solution.py:422
  416.6 7.8 %collective-permute-start.1 = (bf16[2,64,128]{2,1,0:T(8,128)(2,1)S(1)}, bf16[2,64,128]{2,1,0:T(8,128)(2,1)S(1)}, u32[]{:S(2)}, u32[]{:S(2)}) collective-permute-start(bf16[2,64,128]{2,1,0:T(8,128)(2,1)S(1)} %fusion.5), channel_id=1, source_target_pairs={{0,8},{4,12},{8,0},{12,4},{16,24},{20,28},{24,16},{28,20},{1,9},{5... | collective-permute-start | bytes 98312 | tf_op jit(solution)/shard_map/ppermute | solution.py:422
  416.9 14.8 %collective-permute-start.7 = (bf16[2,320,256]{2,1,0:T(8,128)(2,1)S(1)}, bf16[2,320,256]{2,1,0:T(8,128)(2,1)S(1)}, u32[]{:S(2)}, u32[]{:S(2)}) collective-permute-start(bf16[2,320,256]{2,1,0:T(8,128)(2,1)S(1)} %fusion.1), channel_id=1, source_target_pairs={{0,8},{4,12},{8,0},{12,4},{16,24},{20,28},{24,16},{28,20},{1,9},{5... | collective-permute-start | bytes 983048 | tf_op jit(solution)/shard_map/ppermute | solution.py:422
  424.4 7.8 %collective-permute-start.2 = (bf16[1,64,128]{2,1,0:T(8,128)(2,1)S(1)}, bf16[1,64,128]{2,1,0:T(8,128)(2,1)S(1)}, u32[]{:S(2)}, u32[]{:S(2)}) collective-permute-start(bf16[1,64,128]{2,1,0:T(8,128)(2,1)S(1)} %dynamic-slice_convert_fusion.6), channel_id=1, source_target_pairs={{0,16},{4,20},{8,24},{12,28},{16,0},{20,4},{24,8},{28,12},{1,17},{... | collective-permute-start | bytes 49160 | tf_op jit(solution)/shard_map/ppermute | solution.py:422
  431.8 10.2 %collective-permute-start.8 = (bf16[1,320,256]{2,1,0:T(8,128)(2,1)S(1)}, bf16[1,320,256]{2,1,0:T(8,128)(2,1)S(1)}, u32[]{:S(2)}, u32[]{:S(2)}) collective-permute-start(bf16[1,320,256]{2,1,0:T(8,128)(2,1)S(1)} %dynamic-slice_convert_fusion.2), channel_id=1, source_target_pairs={{0,16},{4,20},{8,24},{12,28},{16,0},{20,4},{24,8},{28,12},{1,17},{... | collective-permute-start | bytes 491528 | tf_op jit(solution)/shard_map/ppermute | solution.py:422
  453.6 5.5 %collective-permute-start.3 = (bf16[4,64,256]{2,1,0:T(8,128)(2,1)S(1)}, bf16[4,64,256]{2,1,0:T(8,128)(2,1)S(1)}, u32[]{:S(2)}, u32[]{:S(2)}) collective-permute-start(bf16[4,64,256]{2,1,0:T(8,128)(2,1)S(1)} %fusion.2), channel_id=1, source_target_pairs={{0,4},{4,0},{8,12},{12,8},{16,20},{20,16},{24,28},{28,24},{1,5},{5... | collective-permute-start | bytes 393224 | tf_op jit(solution)/shard_map/ppermute | solution.py:422
  460.1 13.9 %collective-permute-start.4 = (bf16[2,64,256]{2,1,0:T(8,128)(2,1)S(1)}, bf16[2,64,256]{2,1,0:T(8,128)(2,1)S(1)}, u32[]{:S(2)}, u32[]{:S(2)}) collective-permute-start(bf16[2,64,256]{2,1,0:T(8,128)(2,1)S(1)} %fusion.3), channel_id=1, source_target_pairs={{0,8},{4,12},{8,0},{12,4},{16,24},{20,28},{24,16},{28,20},{1,9},{5... | collective-permute-start | bytes 196616 | tf_op jit(solution)/shard_map/ppermute | solution.py:422
  470.4 20.1 %all-to-all-start.6 = ((bf16[8,64,128]{2,1,0:T(8,128)(2,1)}), bf16[8,64,128]{2,1,0:T(8,128)(2,1)S(1)}, u32[]{:S(2)}, u32[]{:S(2)}) async-start(bf16[8,64,128]{2,1,0:T(8,128)(2,1)} %bitcast.45), calls=%async_computation.6 | async-start | bytes 262144 | tf_op jit(solution)/shard_map/all_to_all | solution.py:451
  474.1 16.3 %collective-permute-start.5 = (bf16[1,64,256]{2,1,0:T(8,128)(2,1)S(1)}, bf16[1,64,256]{2,1,0:T(8,128)(2,1)S(1)}, u32[]{:S(2)}, u32[]{:S(2)}) collective-permute-start(bf16[1,64,256]{2,1,0:T(8,128)(2,1)S(1)} %dynamic-slice_convert_fusion.4), channel_id=1, source_target_pairs={{0,16},{4,20},{8,24},{12,28},{16,0},{20,4},{24,8},{28,12},{1,17},{... | collective-permute-start | bytes 98312 | tf_op jit(solution)/shard_map/ppermute | solution.py:422
  (10 other events, 33.1 us)

commit v2 on v1

--- a/solution.py
+++ b/solution.py
@@ -316,15 +316,15 @@
     )
 
 
-def gate_body(slab, offset, ctx, moved_ref, signal_ref, slope_ref, first_ref, gate_ref, sum_ref,
-              turn):
+def gate_body(slab, offset, ctx, carried, moved_ref, signal_ref, slope_ref, *refs):
+    first_ref, gate_ref, sum_ref, turn, total_ref = refs[carried:]
     rows, depth, width = signal_ref.shape
     count = moved_ref.shape[0]
     piece = count // ctx
 
     @pl.when(pl.program_id(0) == 0)
     def _():
-        sum_ref[...] = jnp.zeros_like(sum_ref)
+        total_ref[...] = jnp.zeros_like(total_ref)
 
     for lane in range(width // 128):
         turn[lane] = (
@@ -332,7 +332,7 @@
             .astype(F32)
             .reshape(count * rows, 128)
         )
-    total = sum_ref[...]
+    total = total_ref[...]
     for a in range(rows):
         grad = jnp.concatenate(
             [turn[lane, pl.ds(a, count, stride=rows), :] for lane in range(width // 128)], axis=1
@@ -345,32 +345,45 @@
         first_ref[a] = first
         gate_ref[a] = (grad * slope_ref[a].astype(F32)).astype(BF16)
         total += dot(signal_ref[a], first, 1, 1)
-    sum_ref[...] = total
-
-
-def gate(moved, signal, slope, slab, offset, ctx, after=()):
+    total_ref[...] = total
+
+    @pl.when(pl.program_id(0) == pl.num_programs(0) - 1)
+    def _():
+        sum_ref[...] = total_ref[...].astype(BF16).reshape(sum_ref.shape)
+
+
+def gate(moved, signal, slope, slab, k, pieces, sums, ctx, after=()):
     rows, depth, width = signal.shape
     count = moved.shape[0]
     block = min(16, rows)
     by_row = pl.BlockSpec((block, count, width), lambda s: (s, 0, 0))
     return call(
-        functools.partial(gate_body, slab, offset, ctx),
+        functools.partial(gate_body, slab, k * (count // ctx), ctx, len(sums)),
         (
             jax.ShapeDtypeStruct((rows, count, width), BF16),
             jax.ShapeDtypeStruct((rows, count, width), BF16),
-            jax.ShapeDtypeStruct((depth, count), F32),
+            jax.ShapeDtypeStruct((ctx, pieces, depth // ctx, count), BF16),
         ),
         (2 * rows * depth * count * width, 2 * rows * width * (depth + 4 * count)),
-        (moved, signal, slope),
+        (moved, signal, slope, *sums),
         [
             pl.BlockSpec((count, block, width), lambda s: (0, s, 0)),
             pl.BlockSpec((block, depth, width), lambda s: (s, 0, 0)),
             by_row,
+            *([pl.BlockSpec(memory_space=pl.ANY)] * len(sums)),
         ],
         after,
         grid=(rows // block,),
-        out_specs=(by_row, by_row, pl.BlockSpec((depth, count), lambda s: (0, 0))),
-        scratch_shapes=[pltpu.VMEM((width // 128, count * block, 128), F32)],
+        out_specs=(
+            by_row,
+            by_row,
+            pl.BlockSpec((ctx, 1, depth // ctx, count), lambda s: (0, k, 0, 0)),
+        ),
+        scratch_shapes=[
+            pltpu.VMEM((width // 128, count * block, 128), F32),
+            pltpu.VMEM((depth, count), F32),
+        ],
+        input_output_aliases={3: 2} if sums else {},
         name="gate",
     )
 
@@ -408,37 +421,72 @@
     )
 
 
-def scatter_total(partial_sum, ctx):
+def fold_body(mine_ref, values_ref, got_ref, *refs):
+    del mine_ref
+    refs[-1][...] = values_ref[...].reshape(refs[-1].shape) + got_ref[...].astype(F32)
+
+
+def fold(values, got, mine, after=()):
+    blocks, _, rows, columns = values.shape
+    return pl.pallas_call(
+        fold_body,
+        out_shape=jax.ShapeDtypeStruct((blocks, rows, columns), F32),
+        grid_spec=pltpu.PrefetchScalarGridSpec(
+            num_scalar_prefetch=1,
+            grid=(blocks,),
+            in_specs=[
+                pl.BlockSpec((1, 1, rows, columns), lambda s, mine: (s, mine[0], 0, 0)),
+                pl.BlockSpec((1, rows, columns), lambda s, mine: (s, 0, 0)),
+                *([pl.BlockSpec(memory_space=pl.ANY)] * len(after)),
+            ],
+            out_specs=pl.BlockSpec((1, rows, columns), lambda s, mine: (s, 0, 0)),
+        ),
+        cost_estimate=pl.CostEstimate(
+            flops=got.size, bytes_accessed=10 * got.size, transcendentals=0
+        ),
+        name="fold",
+    )(mine.reshape(1), values, got, *after)
+
+
+def scatter_total(values, ctx, afters):
     if ctx & (ctx - 1):
-        return lax.psum_scatter(partial_sum, "ctx", scatter_dimension=0, tiled=False)
+        return lax.psum_scatter(values, "ctx", scatter_dimension=0, tiled=False)
     me = lax.axis_index("ctx")
-    bit = 1
-    values = partial_sum
+    bit, step = 1, 0
     while bit < ctx:
         halves = values.reshape((-1, 2) + values.shape[1:])
         mine = (me // bit) % 2
-        keep = lax.dynamic_index_in_dim(halves, mine, 1, keepdims=False)
         give = lax.dynamic_index_in_dim(halves, 1 - mine, 1, keepdims=False)
         got = lax.ppermute(give.astype(BF16), "ctx", [(i, i ^ bit) for i in range(ctx)])
-        values = keep + got.astype(F32)
-        bit *= 2
+        values = fold(halves, got, mine, afters[step] if step < len(afters) else ())
+        bit, step = bit * 2, step + 1
     return values[0]
 
 
-def block_total_body(parts_ref, total_ref):
-    total_ref[...] = jnp.sum(parts_ref[...].astype(F32), axis=0)
-
-
-def block_total(parts, after=()):
+def block_total_body(scale, parts_ref, total_ref):
+    ctx, pieces, _, count = parts_ref.shape
+    size = count // ctx
+    for k in range(pieces):
+        total = parts_ref[0, k].astype(F32)
+        for source in range(1, ctx):
+            total += parts_ref[source, k].astype(F32)
+        total *= scale
+        for d in range(ctx):
+            place = (d * pieces + k) * size
+            total_ref[:, place : place + size] = total[:, d * size : (d + 1) * size]
+
+
+def block_total(parts, scale, after=()):
+    _, pieces, rows, count = parts.shape
     return call(
-        block_total_body,
-        jax.ShapeDtypeStruct(parts.shape[1:], F32),
+        functools.partial(block_total_body, scale),
+        jax.ShapeDtypeStruct((rows, pieces * count), F32),
         (parts.size, 4 * parts.size),
         (parts,),
         [whole(parts)],
         after,
         grid=(1,),
-        out_specs=pl.BlockSpec(parts.shape[1:], lambda s: (0, 0)),
+        out_specs=pl.BlockSpec((rows, pieces * count), lambda s: (0, 0)),
         name="block_total",
     )
 
@@ -459,119 +507,81 @@
     up, down = up_weight[0], down_weight[0]
     hidden = up.shape[1]
     factor_turned, up_turned, down_turned = factor.T, up.T, down.T
-    unit = min(16, slab)
-    sizes = (unit, slab - 2 * unit, unit) if slab > 2 * unit else (slab,)
-    last = len(sizes) - 1
-    offsets = tuple(sum(sizes[:k]) for k in range(len(sizes)))
+    pieces = 2 if slab % 32 == 0 else 1
+    size = slab // pieces
+    unit = min(16, size)
     inner = 2
-    by_owner = first.reshape(depth, ctx, slab)
-    columns = [
-        by_owner[:, :, start : start + size].reshape(depth, ctx * size)
-        for start, size in zip(offsets, sizes)
-    ]
-    mix = lambda k, after=(): first_mix(signal, columns[k].T, slab, offsets[k], ctx, after)
-    sent = lambda k, gated: exchange(gated).reshape(ctx, sizes[k], rows, width)
-    total = len(sizes)
-    slopes, arrived, squared, crossed, moved = ([None] * total for _ in range(5))
+    by_owner = first.reshape(depth, ctx, pieces, size)
+    columns = [by_owner[:, :, k].reshape(depth, ctx * size) for k in range(pieces)]
     sums = (
         jnp.zeros((width, hidden), F32),
         jnp.zeros((width, hidden), F32),
         jnp.zeros((1, width), F32),
     )
-    state = dict(sums=sums, layer_pull=(), second=jnp.zeros((tall, tall), F32))
-
-    def square_of(k, after=()):
-        squared[k] = from_groups(squares(arrived[k], factor_turned, inner, after))
-
-    def mlp_of(k, begin, size, after=()):
-        layer, pull, cross, *new_sums = mlp(
-            arrived[k], (begin, size), factor_turned, squared[k], norm_gain, up, up_turned, down,
-            down_turned, cotangent, offsets[k], state["sums"], state["layer_pull"], channels,
-            after,
-        )
-        state.update(sums=new_sums, layer_pull=(layer, pull))
-        return cross
-
-    def second_of(k, after=()):
-        out, state["second"] = second(
-            arrived[k], factor, factor_turned, squared[k], crossed[k], state["layer_pull"][1],
-            cotangent, offsets[k], state["second"], channels, after,
-        )
-        moved[k] = out.reshape(ctx * sizes[k], rows, width)
-        return out
-
-    def back(k):
-        moved[k] = exchange(moved[k])
-
-    def gate_of(k, after=()):
-        return gate(moved[k], signal, slopes[k], slab, offsets[k], ctx, after)
-
-    first_block = lambda sums: sums.reshape(ctx, depth // ctx, sums.shape[1])
-    outs = [None] * total
-    gated, slopes[0] = mix(0)
-    arrived[0] = sent(0, gated)
-    if last:
-        gated, slopes[1] = mix(1)
-        arrived[1] = sent(1, gated)
-        square_of(0)
-        cross_0 = mlp_of(0, 0, sizes[0])
-        gated, slopes[2] = mix(2, (cross_0,))
-        arrived[2] = sent(2, gated)
-        crossed[0] = from_groups(cross_0)
-        square_of(1, (cross_0,))
-        cross_1 = mlp_of(1, 0, unit)
-        done = second_of(0, (cross_1,))
-        back(0)
-        cross_2 = mlp_of(1, unit, sizes[1] - unit, (done,))
-        crossed[1] = from_groups(jnp.concatenate([cross_1, cross_2]))
-        done = second_of(1)
-        back(1)
-        square_of(2, (done, moved[0]))
-        crossed[2] = from_groups(mlp_of(2, 0, sizes[2]))
-        done = second_of(2)
-        back(2)
-    else:
-        square_of(0)
-        crossed[0] = from_groups(mlp_of(0, 0, sizes[0]))
-        done = second_of(0)
-        back(0)
-    for k in range(total):
-        outs[k] = gate_of(k)
-    first_sums = [
-        scatter_total(first_block(out[2]), ctx).reshape(depth // ctx, ctx, size)
-        for out, size in zip(outs[:-1], sizes)
-    ]
-    parts = exchange(outs[-1][2].astype(BF16)).reshape(ctx, depth // ctx, ctx * sizes[-1])
-    grad_signal = signal_grad(
-        jnp.concatenate(columns, axis=1),
-        [out[0] for out in outs], [out[1] for out in outs], offsets, slab, ctx,
-    )
-    first_sums.append(
-        block_total(parts, (grad_signal,)).reshape(depth // ctx, ctx, sizes[-1])
-    )
-    scale = token_count ** (-0.5)
-    grad_first = jnp.concatenate(first_sums, axis=2).reshape(1, depth // ctx, depth)
-    up_sum, down_sum, gain_sum = state["sums"]
+    layer_pull = ()
+    second_sum = jnp.zeros((tall, tall), F32)
+    slopes, arrived, moved = [], [], []
+    for k in range(pieces):
+        gated, slope = first_mix(signal, columns[k].T, slab, k * size, ctx)
+        slopes.append(slope)
+        arrived.append(exchange(gated).reshape(ctx, size, rows, width))
+    waits = ()
+    for k in range(pieces):
+        square = from_groups(squares(arrived[k], factor_turned, inner, waits))
+        crosses = []
+        for begin in range(0, size, unit):
+            layer, pull, cross, *sums = mlp(
+                arrived[k], (begin, unit), factor_turned, square, norm_gain, up, up_turned, down,
+                down_turned, cotangent, k * size, sums, layer_pull, channels,
+            )
+            layer_pull = (layer, pull)
+            crosses.append(cross)
+        cross = from_groups(jnp.concatenate(crosses))
+        back, second_sum = second(
+            arrived[k], factor, factor_turned, square, cross, pull, cotangent, k * size,
+            second_sum, channels,
+        )
+        waits = (back,)
+        moved.append(exchange(back.reshape(ctx * size, rows, width)))
+    up_sum, down_sum, gain_sum = sums
+    gain_width = width // ctx
     packed = jnp.concatenate(
         [
-            up_sum.reshape(ctx, width // ctx * (hidden // tall), tall),
+            up_sum.reshape(ctx, gain_width * (hidden // tall), tall),
             down_sum.T.reshape(ctx, hidden * width // (ctx * tall), tall),
-            state["second"].reshape(ctx, tall // ctx, tall),
-            jnp.broadcast_to(gain_sum.reshape(ctx, width // ctx, 1), (ctx, width // ctx, tall)),
+            second_sum.reshape(ctx, tall // ctx, tall),
+            jnp.pad(gain_sum.reshape(ctx, 1, gain_width), ((0, 0), (0, 15), (0, tall - gain_width))),
         ],
         axis=1,
     )
-    packed = scatter_total(packed, ctx) * scale
-    ends = (width // ctx * (hidden // tall), hidden * width // (ctx * tall), tall // ctx)
-    a, b, c = ends[0], ends[0] + ends[1], sum(ends)
+    sums, firsts, gates = (), [], []
+    for k in range(pieces):
+        first_grad, gate_grad, first_sum = gate(
+            moved[k], signal, slopes[k], slab, k, pieces, sums, ctx
+        )
+        sums = (first_sum,)
+        firsts.append(first_grad)
+        gates.append(gate_grad)
+    packed = scatter_total(packed, ctx, ((firsts[0],), (firsts[-1],)))
+    parts = exchange(first_sum)
+    grad_signal = signal_grad(
+        jnp.concatenate(columns, axis=1), firsts, gates, tuple(k * size for k in range(pieces)),
+        slab, ctx,
+    )
+    scale = token_count ** (-0.5)
+    grad_first = block_total(parts, scale, (grad_signal,))
+    packed = packed * scale
+    a = gain_width * (hidden // tall)
+    b = a + hidden * width // (ctx * tall)
+    c = b + tall // ctx
     return (
-        state["layer_pull"][0],
+        layer,
         grad_signal,
-        grad_first * scale,
+        grad_first[None],
         packed[b:c][None],
-        packed[:a].reshape(1, width // ctx, hidden),
+        packed[:a].reshape(1, gain_width, hidden),
         packed[a:b].reshape(1, hidden // ctx, width),
-        packed[c:, 0][None],
+        packed[c, :gain_width][None],
     )
 
 

time: 504 us -> 451 us (0.89); the launches traced: 495 us -> 449 us
  starting transfers between devices: 42.6 us -> 29.8 us
  blocking collectives: 37.1 us -> 26 us
  waiting for transfers between devices: 176 us -> 166 us
  local copies, waits for them, and re-layouts: 25.4 us -> 19.6 us
    ppermute x9 -> x3, waiting for transfers between devices: 51.6 us -> 31.9 us  [scatter_total(): lax.ppermute(give.astype(BF16), 'ctx', [(i, i ^ bit) for i in range(ctx)])]
    all_gather x6 -> x4, blocking collectives: 37.1 us -> 26 us  [from_groups(): return lax.all_gather(partial_value, 'ch')]
    pallas_call x18 -> x14, Pallas kernels: 205 us -> 194 us  [call(): pl.pallas_call(ordered, out_shape=out_shape, in_specs=[*in_specs, *[pl.Bl...]
    all_to_all x7 -> x5, waiting for transfers between devices: 124 us -> 134 us  [exchange(): return lax.all_to_all(block, 'ctx', split_axis=0, concat_axis=0, tiled=True)]
    all_to_all x7 -> x5, starting transfers between devices: 33.6 us -> 25.2 us  [exchange(): return lax.all_to_all(block, 'ctx', split_axis=0, concat_axis=0, tiled=True)]
    pallas_call x0 -> x3, Pallas kernels: none -> 7.27 us  [fold(): pl.pallas_call(fold_body, out_shape=jax.ShapeDtypeStruct((blocks, rows, c...]
  transfers between devices with their start and end apart: 16 -> 8, of which waited for: 9 -> 6; matrix products, arithmetic and copies ran while one was open for 5% -> 5% of each run, Pallas kernels for 40% -> 42%
where the time goes in v2:
time: 451 us; the launch traced here: 449 us
  Pallas kernels  201 us (45%)
  waiting for transfers between devices  166 us (37%)
  starting transfers between devices  29.8 us (7%)
  blocking collectives  26 us (6%)
  local copies, waits for them, and re-layouts  19.6 us (4%)
  other arithmetic  5.76 us (1%)
    pallas_call x14, Pallas kernels, call(): pl.pallas_call(ordered, out_shape=out_shape, in_specs=[*in_specs, *[pl.Bl...  194 us
    all_to_all x5, waiting for transfers between devices, exchange(): return lax.all_to_all(block, 'ctx', split_axis=0, concat_axis=0, tiled=True)  134 us
    ppermute x3, waiting for transfers between devices, scatter_total(): lax.ppermute(give.astype(BF16), 'ctx', [(i, i ^ bit) for i in range(ctx)])  31.9 us
    all_gather x4, blocking collectives, from_groups(): return lax.all_gather(partial_value, 'ch')  26 us
    all_to_all x5, starting transfers between devices, exchange(): return lax.all_to_all(block, 'ctx', split_axis=0, concat_axis=0, tiled=True)  25.2 us
  transfers between devices with their start and end apart: 8, of which 6 were waited for; matrix products, arithmetic and copies ran while one was open for 5% of the time, Pallas kernels for 42%

profile of v2, /device:TPU:0, one launch (start us, length us, event | category | flops | bytes accessed | tf_op | source)
XLA Modules:
  0.0 449.4 jit_solution(15658196181021407289)
XLA Ops:
  2.7 10.1 %first_mix.3 = (bf16[256,32,256]{2,1,0:T(8,128)(2,1)}, bf16[32,256,256]{2,1,0:T(8,128)(2,1)}) custom-call(bf16[32,512,256]{2,1,0:T(8,128)(2,1)} %refs_1_.3, bf16[256,512]{1,0:T(8,128)(2,1)} %bitcast.70), custom_call_target="tpu_custom_call" | custom-call | flops 2147483648 | bytes 16777216 | tf_op jit(solution)/shard_map/first_mix/pallas_call | solution.py:44
  12.8 7.3 %all-to-all-start.1 = ((bf16[256,32,256]{2,1,0:T(8,128)(2,1)}), bf16[256,32,256]{2,1,0:T(8,128)(2,1)}, u32[]{:S(2)}, u32[]{:S(2)}) async-start(bf16[256,32,256]{2,1,0:T(8,128)(2,1)} %get-tuple-element.46), calls=%async_computation.1 | async-start | bytes 8388608 | tf_op jit(solution)/shard_map/all_to_all | solution.py:499
  20.1 9.9 %first_mix.2 = (bf16[256,32,256]{2,1,0:T(8,128)(2,1)}, bf16[32,256,256]{2,1,0:T(8,128)(2,1)}) custom-call(bf16[32,512,256]{2,1,0:T(8,128)(2,1)} %refs_1_.3, bf16[256,512]{1,0:T(8,128)(2,1)} %bitcast.68), custom_call_target="tpu_custom_call" | custom-call | flops 2147483648 | bytes 16777216 | tf_op jit(solution)/shard_map/first_mix/pallas_call | solution.py:44
  30.0 83.4 %all-to-all-done.1 = bf16[256,32,256]{2,1,0:T(8,128)(2,1)} async-done(((bf16[256,32,256]{2,1,0:T(8,128)(2,1)}), bf16[256,32,256]{2,1,0:T(8,128)(2,1)}, u32[]{:S(2)}, u32[]{:S(2)}) %all-to-all-start.1) | async-done | bytes 4194336 | tf_op jit(solution)/shard_map/all_to_all | solution.py:499
  113.4 4.7 %all-to-all-start = ((bf16[256,32,256]{2,1,0:T(8,128)(2,1)}), bf16[256,32,256]{2,1,0:T(8,128)(2,1)}, u32[]{:S(2)}, u32[]{:S(2)}) async-start(bf16[256,32,256]{2,1,0:T(8,128)(2,1)} %get-tuple-element.45), calls=%async_computation | async-start | bytes 8388608 | tf_op jit(solution)/shard_map/all_to_all | solution.py:499
  120.9 5.5 %squares.2 = f32[16,2,256]{2,1,0:T(2,128)} custom-call(bf16[8,32,32,256]{3,2,1,0:T(8,128)(2,1)} %bitcast.9.refs_0_, bf16[256,256]{1,0:T(8,128)(2,1)} %bitcast.59), custom_call_target="tpu_custom_call" | custom-call | flops 1073741824 | bytes 4194304 | tf_op jit(solution)/shard_map/squares/pallas_call | solution.py:44
  126.4 7.1 %all-gather = f32[64,2,256]{2,1,0:T(2,128)} all-gather(f32[16,2,256]{2,1,0:T(2,128)} %squares.2), channel_id=2, replica_groups=mesh['ctx'=8,'ch'=4] {'ch'}, dimensions={0}, use_global_device_ids=true | all-gather | bytes 163840 | tf_op jit(solution)/shard_map/all_gather | solution.py:495
  136.3 25.2 %mlp.4 = (bf16[64,256,256]{2,1,0:T(8,128)(2,1)}, bf16[64,256,256]{2,1,0:T(8,128)(2,1)}, f32[8,2,256]{2,1,0:T(2,128)}, f32[256,1024]{1,0:T(8,128)}, f32[256,1024]{1,0:T(8,128)}, /*index=5*/f32[1,256]{1,0:T(1,128)}) custom-call(bf16[8,32,32,256]{3,2,1,0:T(8,128)(2,1)} %bitcast.9.refs_0_, ...), custom_call_target="tpu_custom_call", output_to_operand_aliasing={{3}: (9, {}), {4}: (10, {}), {5}: (11, {})} | custom-call | flops 12884901888 | bytes 8388608 | tf_op jit(solution)/shard_map/mlp/pallas_call | solution.py:44
  161.5 25.3 %mlp.5 = (bf16[64,256,256]{2,1,0:T(8,128)(2,1)}, bf16[64,256,256]{2,1,0:T(8,128)(2,1)}, f32[8,2,256]{2,1,0:T(2,128)}, f32[256,1024]{1,0:T(8,128)}, f32[256,1024]{1,0:T(8,128)}, /*index=5*/f32[1,256]{1,0:T(1,128)}) custom-call(bf16[8,32,32,256]{3,2,1,0:T(8,128)(2,1)} %bitcast.9.refs_0_,, ...), custom_call_target="tpu_custom_call", output_to_operand_aliasing={{3}: (9, {}), {4}: (10, {}), {5}: (11, {}), {0}: (12, {}), ... | custom-call | flops 12884901888 | bytes 8388608 | tf_op jit(solution)/shard_map/mlp/pallas_call | solution.py:44
  187.6 5.9 %all-gather.1 = f32[64,2,256]{2,1,0:T(2,128)} all-gather(f32[16,2,256]{2,1,0:T(2,128)S(1)} %pad_maximum_fusion.2), channel_id=3, replica_groups=mesh['ctx'=8,'ch'=4] {'ch'}, dimensions={0}, use_global_device_ids=true | all-gather | bytes 163840 | tf_op jit(solution)/shard_map/all_gather | solution.py:495
  194.2 12.4 %second.2 = (bf16[8,32,32,256]{3,2,1,0:T(8,128)(2,1)}, f32[256,256]{1,0:T(8,128)}) custom-call(bf16[8,32,32,256]{3,2,1,0:T(8,128)(2,1)} %bitcast.9.refs_0_, bf16[256,256]{1,0:T(8,128)(2,1)} %bitcast.73, bf16[256,256]{1,0:T(8,128)(2,1)} %bitcast.62, f32[4,16,2,256]{3,2,1,0:T(2,128)} %bitcast.80, ...), custom_call_target="tpu_custom_call", output_to_operand_aliasing={{1}: (7, {})} | custom-call | flops 3221225472 | bytes 16777216 | tf_op jit(solution)/shard_map/second/pallas_call | solution.py:44
  215.2 5.5 %squares.3 = f32[16,2,256]{2,1,0:T(2,128)} custom-call(bf16[8,32,32,256]{3,2,1,0:T(8,128)(2,1)} %bitcast.3.refs_0_, bf16[256,256]{1,0:T(8,128)(2,1)} %bitcast.63, bf16[8,32,32,256]{3,2,1,0:T(8,128)(2,1)} %get-tuple-element.55.refs_2_), custom_call_target="tpu_custom_call" | custom-call | flops 1073741824 | bytes 4194304 | tf_op jit(solution)/shard_map/squares/pallas_call | solution.py:44
  220.7 7.1 %all-gather.2 = f32[64,2,256]{2,1,0:T(2,128)} all-gather(f32[16,2,256]{2,1,0:T(2,128)} %squares.3), channel_id=4, replica_groups=mesh['ctx'=8,'ch'=4] {'ch'}, dimensions={0}, use_global_device_ids=true | all-gather | bytes 163840 | tf_op jit(solution)/shard_map/all_gather | solution.py:495
  227.8 25.3 %mlp.6 = (bf16[64,256,256]{2,1,0:T(8,128)(2,1)}, bf16[64,256,256]{2,1,0:T(8,128)(2,1)}, f32[8,2,256]{2,1,0:T(2,128)}, f32[256,1024]{1,0:T(8,128)}, f32[256,1024]{1,0:T(8,128)}, /*index=5*/f32[1,256]{1,0:T(1,128)}) custom-call(bf16[8,32,32,256]{3,2,1,0:T(8,128)(2,1)} %bitcast.3.refs_0_,, ...), custom_call_target="tpu_custom_call", output_to_operand_aliasing={{3}: (9, {}), {4}: (10, {}), {5}: (11, {}), {0}: (12, {}), ... | custom-call | flops 12884901888 | bytes 8388608 | tf_op jit(solution)/shard_map/mlp/pallas_call | solution.py:44
  253.2 25.3 %mlp.7 = (bf16[64,256,256]{2,1,0:T(8,128)(2,1)}, bf16[64,256,256]{2,1,0:T(8,128)(2,1)}, f32[8,2,256]{2,1,0:T(2,128)}, f32[256,1024]{1,0:T(8,128)}, f32[256,1024]{1,0:T(8,128)}, /*index=5*/f32[1,256]{1,0:T(1,128)}) custom-call(bf16[8,32,32,256]{3,2,1,0:T(8,128)(2,1)} %bitcast.3.refs_0_,, ...), custom_call_target="tpu_custom_call", output_to_operand_aliasing={{3}: (9, {}), {4}: (10, {}), {5}: (11, {}), {0}: (12, {}), ... | custom-call | flops 12884901888 | bytes 8388608 | tf_op jit(solution)/shard_map/mlp/pallas_call | solution.py:44
  279.3 5.9 %all-gather.3 = f32[64,2,256]{2,1,0:T(2,128)} all-gather(f32[16,2,256]{2,1,0:T(2,128)S(1)} %pad_maximum_fusion.3), channel_id=5, replica_groups=mesh['ctx'=8,'ch'=4] {'ch'}, dimensions={0}, use_global_device_ids=true | all-gather | bytes 163840 | tf_op jit(solution)/shard_map/all_gather | solution.py:495
  285.2 12.5 %second.3 = (bf16[8,32,32,256]{3,2,1,0:T(8,128)(2,1)}, f32[256,256]{1,0:T(8,128)}) custom-call(bf16[8,32,32,256]{3,2,1,0:T(8,128)(2,1)} %bitcast.3.refs_0_, bf16[256,256]{1,0:T(8,128)(2,1)} %bitcast.74, bf16[256,256]{1,0:T(8,128)(2,1)} %bitcast.66, f32[4,16,2,256]{3,2,1,0:T(2,128)} %bitcast.77, ...), custom_call_target="tpu_custom_call", output_to_operand_aliasing={{1}: (7, {})} | custom-call | flops 3221225472 | bytes 16777216 | tf_op jit(solution)/shard_map/second/pallas_call | solution.py:44
  297.7 10.1 %all-to-all-done.2.refs_0_ = bf16[256,32,256]{2,1,0:T(8,128)(2,1)} async-done(((bf16[256,32,256]{2,1,0:T(8,128)(2,1)}), bf16[256,32,256]{2,1,0:T(8,128)(2,1)}, u32[]{:S(2)}, u32[]{:S(2)}) %all-to-all-start.2) | async-done | bytes 4194336 | tf_op jit(solution)/shard_map/all_to_all | solution.py:499
  307.7 5.0 %all-to-all-start.3 = ((bf16[256,32,256]{2,1,0:T(8,128)(2,1)}), bf16[256,32,256]{2,1,0:T(8,128)(2,1)}, u32[]{:S(2)}, u32[]{:S(2)}) async-start(bf16[256,32,256]{2,1,0:T(8,128)(2,1)} %bitcast.57), calls=%async_computation.3 | async-start | bytes 8388608 | tf_op jit(solution)/shard_map/all_to_all | solution.py:499
  321.4 10.7 %gate.2 = (bf16[32,256,256]{2,1,0:T(8,128)(2,1)}, bf16[32,256,256]{2,1,0:T(8,128)(2,1)}, bf16[8,2,64,256]{3,2,1,0:T(8,128)(2,1)}) custom-call(bf16[256,32,256]{2,1,0:T(8,128)(2,1)} %all-to-all-done.2.refs_0_, bf16[32,512,256]{2,1,0:T(8,128)(2,1)} %refs_1_.3, bf16[32,256,256]{2,1,0:T(8,128)(2,1)} %get-tuple-element.66.refs_2_), custom_call_target="tpu_custom_call" | custom-call | flops 2147483648 | bytes 25165824 | tf_op jit(solution)/shard_map/gate/pallas_call | solution.py:44
  332.1 30.6 %collective-permute-done.got_ref = bf16[4,304,256]{2,1,0:T(8,128)(2,1)} collective-permute-done((bf16[4,304,256]{2,1,0:T(8,128)(2,1)}, bf16[4,304,256]{2,1,0:T(8,128)(2,1)}, u32[]{:S(2)}, u32[]{:S(2)}) %collective-permute-start) | collective-permute-done | bytes 622624 | tf_op jit(solution)/shard_map/ppermute | solution.py:460
  368.3 36.7 %all-to-all-done.3.refs_0_ = bf16[256,32,256]{2,1,0:T(8,128)(2,1)} async-done(((bf16[256,32,256]{2,1,0:T(8,128)(2,1)}), bf16[256,32,256]{2,1,0:T(8,128)(2,1)}, u32[]{:S(2)}, u32[]{:S(2)}) %all-to-all-start.3) | async-done | bytes 4194336 | tf_op jit(solution)/shard_map/all_to_all | solution.py:499
  405.1 10.7 %gate.3 = (bf16[32,256,256]{2,1,0:T(8,128)(2,1)}, bf16[32,256,256]{2,1,0:T(8,128)(2,1)}, bf16[8,2,64,256]{3,2,1,0:T(8,128)(2,1)}) custom-call(bf16[256,32,256]{2,1,0:T(8,128)(2,1)} %all-to-all-done.3.refs_0_, bf16[32,512,256]{2,1,0:T(8,128)(2,1)} %refs_1_.3, bf16[32,256,256]{2,1,0:T(8,128)(2,1)} %get-tuple-element.73.refs_2_, ...), custom_call_target="tpu_custom_call", output_to_operand_aliasing={{2}: (3, {})} | custom-call | flops 2147483648 | bytes 25165824 | tf_op jit(solution)/shard_map/gate/pallas_call | solution.py:44
  426.1 13.4 %signal_grad.1.refs_1_ = bf16[32,512,256]{2,1,0:T(8,128)(2,1)} custom-call(bf16[512,512]{1,0:T(8,128)(2,1)} %pad_maximum_fusion.1.refs_0_, bf16[32,256,256]{2,1,0:T(8,128)(2,1)} %get-tuple-element.67.refs_1_.refs_0_, bf16[32,256,256]{2,1,0:T(8,128)(2,1)} %get-tuple-element.75.refs_2_.refs_0_, bf16[32,256,256]{2,1,0:T(8,128)(2,1)} %get-tuple-element.76.refs_3_, ...), custom_call_target="tpu_custom_call" | custom-call | flops 4294967296 | bytes 25165824 | tf_op jit(solution)/shard_map/signal_grad/pallas_call | solution.py:44
  (72 shorter events, 52.6 us)
Async XLA Ops:
  12.8 100.6 %all-to-all-start.1 = ((bf16[256,32,256]{2,1,0:T(8,128)(2,1)}), bf16[256,32,256]{2,1,0:T(8,128)(2,1)}, u32[]{:S(2)}, u32[]{:S(2)}) async-start(bf16[256,32,256]{2,1,0:T(8,128)(2,1)} %get-tuple-element.46), calls=%async_computation.1 | async-start | bytes 8388608 | tf_op jit(solution)/shard_map/all_to_all | solution.py:499
  113.4 4.7 %copy-start.7 = (bf16[1,256,256]{2,1,0:T(8,128)(2,1)S(1)}, bf16[1,256,256]{2,1,0:T(8,128)(2,1)}, u32[]{:S(2)}) copy-start(bf16[1,256,256]{2,1,0:T(8,128)(2,1)} %param.9) | copy-start | bytes 393220
  113.4 5.5 %copy-start.8 = (bf16[1,256,1024]{2,1,0:T(8,128)(2,1)S(1)}, bf16[1,256,1024]{2,1,0:T(8,128)(2,1)}, u32[]{:S(2)}) copy-start(bf16[1,256,1024]{2,1,0:T(8,128)(2,1)} %param.10) | copy-start | bytes 1572868
  113.4 6.5 %copy-start.9 = (bf16[1,1024,256]{2,1,0:T(8,128)(2,1)S(1)}, bf16[1,1024,256]{2,1,0:T(8,128)(2,1)}, u32[]{:S(2)}) copy-start(bf16[1,1024,256]{2,1,0:T(8,128)(2,1)} %param.11) | copy-start | bytes 1572868
  113.4 97.2 %all-to-all-start = ((bf16[256,32,256]{2,1,0:T(8,128)(2,1)}), bf16[256,32,256]{2,1,0:T(8,128)(2,1)}, u32[]{:S(2)}, u32[]{:S(2)}) async-start(bf16[256,32,256]{2,1,0:T(8,128)(2,1)} %get-tuple-element.45), calls=%async_computation | async-start | bytes 8388608 | tf_op jit(solution)/shard_map/all_to_all | solution.py:499
  161.5 25.3 %copy-start.13 = (f32[8,2,256]{2,1,0:T(2,128)S(1)}, f32[8,2,256]{2,1,0:T(2,128)}, u32[]{:S(2)}) copy-start(f32[8,2,256]{2,1,0:T(2,128)} %get-tuple-element.47) | copy-start | bytes 49156
  210.6 97.1 %all-to-all-start.2 = ((bf16[256,32,256]{2,1,0:T(8,128)(2,1)}), bf16[256,32,256]{2,1,0:T(8,128)(2,1)}, u32[]{:S(2)}, u32[]{:S(2)}) async-start(bf16[256,32,256]{2,1,0:T(8,128)(2,1)} %bitcast.52), calls=%async_computation.2 | async-start | bytes 8388608 | tf_op jit(solution)/shard_map/all_to_all | solution.py:499
  253.2 25.4 %copy-start.12 = (f32[8,2,256]{2,1,0:T(2,128)S(1)}, f32[8,2,256]{2,1,0:T(2,128)}, u32[]{:S(2)}) copy-start(f32[8,2,256]{2,1,0:T(2,128)} %get-tuple-element.68) | copy-start | bytes 49156
  307.7 5.0 %copy-start.3 = (f32[256,1024]{1,0:T(8,128)S(1)}, f32[256,1024]{1,0:T(8,128)}, u32[]{:S(2)}) copy-start(f32[256,1024]{1,0:T(8,128)} %get-tuple-element.80) | copy-start | bytes 3145732
  307.7 6.4 %copy-start.2 = (f32[256,1024]{1,0:T(8,128)S(1)}, f32[256,1024]{1,0:T(8,128)}, u32[]{:S(2)}) copy-start(f32[256,1024]{1,0:T(8,128)} %get-tuple-element.79) | copy-start | bytes 3145732
  307.7 97.4 %all-to-all-start.3 = ((bf16[256,32,256]{2,1,0:T(8,128)(2,1)}), bf16[256,32,256]{2,1,0:T(8,128)(2,1)}, u32[]{:S(2)}, u32[]{:S(2)}) async-start(bf16[256,32,256]{2,1,0:T(8,128)(2,1)} %bitcast.57), calls=%async_computation.3 | async-start | bytes 8388608 | tf_op jit(solution)/shard_map/all_to_all | solution.py:499
  312.7 3.1 copy-start.14
  312.7 3.9 copy-start.1
  314.1 7.0 %copy-start.5 = (bf16[512,8,1,32]{0,3,2,1:T(8,128)(2,1)S(1)}, bf16[512,8,1,32]{0,3,2,1:T(8,128)(2,1)}, u32[]{:S(2)}) copy-start(bf16[512,8,1,32]{0,3,2,1:T(8,128)(2,1)} %get-tuple-element.83) | copy-start | bytes 786436
  314.1 7.1 %copy-start.4 = (bf16[512,8,1,32]{0,3,2,1:T(8,128)(2,1)S(1)}, bf16[512,8,1,32]{0,3,2,1:T(8,128)(2,1)}, u32[]{:S(2)}) copy-start(bf16[512,8,1,32]{0,3,2,1:T(8,128)(2,1)} %get-tuple-element.84) | copy-start | bytes 786436
  318.4 13.7 %copy-start = (f32[4,2,304,256]{3,2,1,0:T(8,128)}, f32[4,2,304,256]{3,2,1,0:T(8,128)S(1)}, u32[]{:S(2)}) copy-start(f32[4,2,304,256]{3,2,1,0:T(8,128)S(1)} %pad_maximum_fusion.values_ref) | copy-start | bytes 7471108
  319.5 43.3 %collective-permute-start = (bf16[4,304,256]{2,1,0:T(8,128)(2,1)}, bf16[4,304,256]{2,1,0:T(8,128)(2,1)}, u32[]{:S(2)}, u32[]{:S(2)}) collective-permute-start(bf16[4,304,256]{2,1,0:T(8,128)(2,1)} %fusion), channel_id=1, source_target_pairs={{0,4},{4,0},{8,12},{12,8},{16,20},{20,16},{24,28},{28,24},{1,5},{5... | collective-permute-start | bytes 1867784 | tf_op jit(solution)/shard_map/ppermute | solution.py:460
  367.4 52.0 %collective-permute-start.1 = (bf16[2,304,256]{2,1,0:T(8,128)(2,1)S(1)}, bf16[2,304,256]{2,1,0:T(8,128)(2,1)S(1)}, u32[]{:S(2)}, u32[]{:S(2)}) collective-permute-start(bf16[2,304,256]{2,1,0:T(8,128)(2,1)S(1)} %fusion.1), channel_id=1, source_target_pairs={{0,8},{4,12},{8,0},{12,4},{16,24},{20,28},{24,16},{28,20},{1,9},{5... | collective-permute-start | bytes 933896 | tf_op jit(solution)/shard_map/ppermute | solution.py:460
  415.8 30.8 %all-to-all-start.4 = ((bf16[8,2,64,256]{3,2,1,0:T(8,128)(2,1)}), bf16[8,2,64,256]{3,2,1,0:T(8,128)(2,1)S(1)}, u32[]{:S(2)}, u32[]{:S(2)}) async-start(bf16[8,2,64,256]{3,2,1,0:T(8,128)(2,1)} %get-tuple-element.78), calls=%async_computation.4 | async-start | bytes 1048576 | tf_op jit(solution)/shard_map/all_to_all | solution.py:499
  419.5 0.7 copy-start.10
  423.1 17.6 %collective-permute-start.2 = (bf16[1,304,256]{2,1,0:T(8,128)(2,1)S(1)}, bf16[1,304,256]{2,1,0:T(8,128)(2,1)S(1)}, u32[]{:S(2)}, u32[]{:S(2)}) collective-permute-start(bf16[1,304,256]{2,1,0:T(8,128)(2,1)S(1)} %dynamic-slice_convert_fusion), channel_id=1, source_target_pairs={{0,16},{4,20},{8,24},{12,28},{16,0},{20,4},{24,8},{28,12},{1,17},{... | collective-permute-start | bytes 466952 | tf_op jit(solution)/shard_map/ppermute | solution.py:460
  440.7 0.7 copy-start.11
  446.7 0.8 copy-start.6

commit v3 on v2

--- a/solution.py
+++ b/solution.py
@@ -12,7 +12,7 @@
 TANH_CUBIC = 0.044715
 BF16 = jnp.bfloat16
 F32 = jnp.float32
-VMEM_LIMIT = 56 * 1024 * 1024
+MIB = 1024 * 1024
 
 
 def sigmoid(values):
@@ -34,7 +34,7 @@
     return jnp.concatenate([spread] * (width // 128), axis=1)
 
 
-def call(body, out_shape, cost, operands, in_specs, after=(), **options):
+def call(body, out_shape, cost, operands, in_specs, after=(), vmem=56, **options):
     flops, bytes_accessed = cost
     given, waits = len(operands), len(after)
 
@@ -45,7 +45,7 @@
         ordered,
         out_shape=out_shape,
         in_specs=[*in_specs, *([pl.BlockSpec(memory_space=pl.ANY)] * waits)],
-        compiler_params=pltpu.CompilerParams(vmem_limit_bytes=VMEM_LIMIT),
+        compiler_params=pltpu.CompilerParams(vmem_limit_bytes=vmem * MIB),
         cost_estimate=pl.CostEstimate(
             flops=int(flops), bytes_accessed=int(bytes_accessed), transcendentals=0
         ),
@@ -362,7 +362,9 @@
         (
             jax.ShapeDtypeStruct((rows, count, width), BF16),
             jax.ShapeDtypeStruct((rows, count, width), BF16),
-            jax.ShapeDtypeStruct((ctx, pieces, depth // ctx, count), BF16),
+            jax.ShapeDtypeStruct(sums[0].shape, BF16)
+            if sums
+            else jax.ShapeDtypeStruct((ctx, pieces * (depth // ctx), count), BF16),
         ),
         (2 * rows * depth * count * width, 2 * rows * width * (depth + 4 * count)),
         (moved, signal, slope, *sums),
@@ -377,7 +379,7 @@
         out_specs=(
             by_row,
             by_row,
-            pl.BlockSpec((ctx, 1, depth // ctx, count), lambda s: (0, k, 0, 0)),
+            pl.BlockSpec((ctx, depth // ctx, count), lambda s: (0, k, 0)),
         ),
         scratch_shapes=[
             pltpu.VMEM((width // 128, count * block, 128), F32),
@@ -406,7 +408,7 @@
 def signal_grad(factor, firsts, gates, offsets, slab, ctx, after=()):
     rows, _, width = firsts[0].shape
     depth = factor.shape[0]
-    block = min(4, rows)
+    block = min(8, rows)
     by_row = [pl.BlockSpec((block, *array.shape[1:]), lambda s: (s, 0, 0)) for array in firsts]
     return call(
         functools.partial(signal_body, offsets, slab, ctx),
@@ -421,15 +423,16 @@
     )
 
 
-def fold_body(mine_ref, values_ref, got_ref, *refs):
+def fold_body(scale, mine_ref, values_ref, got_ref, *refs):
     del mine_ref
-    refs[-1][...] = values_ref[...].reshape(refs[-1].shape) + got_ref[...].astype(F32)
-
-
-def fold(values, got, mine, after=()):
+    total = values_ref[...].reshape(refs[-1].shape) + got_ref[...].astype(F32)
+    refs[-1][...] = total * scale
+
+
+def fold(values, got, mine, scale, after=()):
     blocks, _, rows, columns = values.shape
     return pl.pallas_call(
-        fold_body,
+        functools.partial(fold_body, scale),
         out_shape=jax.ShapeDtypeStruct((blocks, rows, columns), F32),
         grid_spec=pltpu.PrefetchScalarGridSpec(
             num_scalar_prefetch=1,
@@ -441,6 +444,7 @@
             ],
             out_specs=pl.BlockSpec((1, rows, columns), lambda s, mine: (s, 0, 0)),
         ),
+        compiler_params=pltpu.CompilerParams(vmem_limit_bytes=56 * MIB),
         cost_estimate=pl.CostEstimate(
             flops=got.size, bytes_accessed=10 * got.size, transcendentals=0
         ),
@@ -448,47 +452,88 @@
     )(mine.reshape(1), values, got, *after)
 
 
-def scatter_total(values, ctx, afters):
-    if ctx & (ctx - 1):
-        return lax.psum_scatter(values, "ctx", scatter_dimension=0, tiled=False)
-    me = lax.axis_index("ctx")
-    bit, step = 1, 0
-    while bit < ctx:
-        halves = values.reshape((-1, 2) + values.shape[1:])
-        mine = (me // bit) % 2
-        give = lax.dynamic_index_in_dim(halves, 1 - mine, 1, keepdims=False)
-        got = lax.ppermute(give.astype(BF16), "ctx", [(i, i ^ bit) for i in range(ctx)])
-        values = fold(halves, got, mine, afters[step] if step < len(afters) else ())
-        bit, step = bit * 2, step + 1
-    return values[0]
-
-
-def block_total_body(scale, parts_ref, total_ref):
-    ctx, pieces, _, count = parts_ref.shape
+class Halving:
+    def __init__(self, values, ctx, scale):
+        self.ctx, self.bit, self.scale = ctx, 1, scale
+        self.values = values
+        self.halve()
+
+    def halve(self):
+        self.halves = self.values.reshape((-1, 2) + self.values.shape[1:])
+        self.mine = (lax.axis_index("ctx") // self.bit) % 2
+        self.give = lax.dynamic_index_in_dim(
+            self.halves, 1 - self.mine, 1, keepdims=False
+        ).astype(BF16)
+
+    def send(self):
+        bit = self.bit
+        self.got = lax.ppermute(self.give, "ctx", [(i, i ^ bit) for i in range(self.ctx)])
+        return self.got
+
+    def keep(self, after=()):
+        self.bit = 2 * self.bit
+        scale = 1.0 if self.bit < self.ctx else self.scale
+        self.values = fold(self.halves, self.got, self.mine, scale, after)
+        if self.bit < self.ctx:
+            self.halve()
+
+    def finish(self, after=()):
+        while self.bit < self.ctx:
+            self.send()
+            self.keep(after)
+        return self.values[0]
+
+
+def block_total_body(pieces, ctx, scale, parts_ref, first_ref, *rest):
+    rows = first_ref.shape[0]
+    count = parts_ref.shape[2]
     size = count // ctx
+
+    def total_of(start, stop):
+        total = parts_ref[0, start:stop].astype(F32)
+        for source in range(1, ctx):
+            total += parts_ref[source, start:stop].astype(F32)
+        return total * scale
+
     for k in range(pieces):
-        total = parts_ref[0, k].astype(F32)
-        for source in range(1, ctx):
-            total += parts_ref[source, k].astype(F32)
-        total *= scale
+        total = total_of(k * rows, (k + 1) * rows)
         for d in range(ctx):
             place = (d * pieces + k) * size
-            total_ref[:, place : place + size] = total[:, d * size : (d + 1) * size]
-
-
-def block_total(parts, scale, after=()):
-    _, pieces, rows, count = parts.shape
+            first_ref[:, place : place + size] = total[:, d * size : (d + 1) * size]
+    if rest:
+        rest[0][...] = total_of(pieces * rows, parts_ref.shape[1])
+
+
+def block_total(parts, pieces, ctx, scale, after=()):
+    _, all_rows, count = parts.shape
+    depth = pieces * count
+    more = all_rows - pieces * (depth // ctx)
+    shapes = [jax.ShapeDtypeStruct((depth // ctx, depth), F32)]
+    if more:
+        shapes.append(jax.ShapeDtypeStruct((more, count), F32))
     return call(
-        functools.partial(block_total_body, scale),
-        jax.ShapeDtypeStruct((rows, pieces * count), F32),
+        functools.partial(block_total_body, pieces, ctx, scale),
+        tuple(shapes),
         (parts.size, 4 * parts.size),
         (parts,),
         [whole(parts)],
         after,
         grid=(1,),
-        out_specs=pl.BlockSpec((rows, pieces * count), lambda s: (0, 0)),
+        out_specs=tuple(pl.BlockSpec(shape.shape, lambda s: (0, 0)) for shape in shapes),
         name="block_total",
     )
+
+
+def hold(array, after):
+    return pl.pallas_call(
+        lambda *refs: None,
+        out_shape=jax.ShapeDtypeStruct(array.shape, array.dtype),
+        in_specs=[pl.BlockSpec(memory_space=pl.ANY)] * (1 + len(after)),
+        out_specs=pl.BlockSpec(memory_space=pl.ANY),
+        input_output_aliases={0: 0},
+        compiler_params=pltpu.CompilerParams(vmem_limit_bytes=56 * MIB),
+        name="hold",
+    )(array, *after)
 
 
 def from_groups(partial_value):
@@ -526,6 +571,8 @@
         slopes.append(slope)
         arrived.append(exchange(gated).reshape(ctx, size, rows, width))
     waits = ()
+    scale = token_count ** (-0.5)
+    gain_width = width // ctx
     for k in range(pieces):
         square = from_groups(squares(arrived[k], factor_turned, inner, waits))
         crosses = []
@@ -537,51 +584,69 @@
             layer_pull = (layer, pull)
             crosses.append(cross)
         cross = from_groups(jnp.concatenate(crosses))
+        waits = ()
+        if k == pieces - 1:
+            up_sum, down_sum, gain_sum = sums
+            packed = jnp.concatenate(
+                [
+                    up_sum.reshape(ctx, gain_width * (hidden // tall), tall),
+                    down_sum.T.reshape(ctx, hidden * width // (ctx * tall), tall),
+                    jnp.pad(
+                        gain_sum.reshape(ctx, 1, gain_width),
+                        ((0, 0), (0, 15), (0, tall - gain_width)),
+                    ),
+                ],
+                axis=1,
+            )
+            weights = Halving(packed, ctx, scale)
+            waits = (weights.give,)
         back, second_sum = second(
             arrived[k], factor, factor_turned, square, cross, pull, cotangent, k * size,
-            second_sum, channels,
+            second_sum, channels, waits,
         )
         waits = (back,)
+        if pieces > 1 and k == pieces - 1:
+            back = hold(back, (weights.send(),))
+            weights.keep((back,))
         moved.append(exchange(back.reshape(ctx * size, rows, width)))
-    up_sum, down_sum, gain_sum = sums
-    gain_width = width // ctx
-    packed = jnp.concatenate(
-        [
-            up_sum.reshape(ctx, gain_width * (hidden // tall), tall),
-            down_sum.T.reshape(ctx, hidden * width // (ctx * tall), tall),
-            second_sum.reshape(ctx, tall // ctx, tall),
-            jnp.pad(gain_sum.reshape(ctx, 1, gain_width), ((0, 0), (0, 15), (0, tall - gain_width))),
-        ],
-        axis=1,
-    )
-    sums, firsts, gates = (), [], []
+    count = ctx * size
+    own_rows, joint = tall // ctx, count == tall
+    sums, firsts, gates, waits = (), [], [], ()
+    factor_sorted = jnp.concatenate(columns, axis=1)
+    if joint:
+        above = ((0, 0), (pieces * (depth // ctx), 0), (0, 0))
+        sums = (jnp.pad(second_sum.reshape(ctx, own_rows, tall).astype(BF16), above),)
     for k in range(pieces):
+        if k == pieces - 1:
+            packed = weights.finish(tuple(firsts))
+            a = gain_width * (hidden // tall)
+            b = a + hidden * width // (ctx * tall)
+            grad_up = packed[:a].reshape(1, gain_width, hidden)
+            grad_down = packed[a:b].reshape(1, hidden // ctx, width)
+            grad_gain = packed[b, :gain_width][None]
+            waits = (grad_up, grad_down, grad_gain, factor_sorted)
         first_grad, gate_grad, first_sum = gate(
-            moved[k], signal, slopes[k], slab, k, pieces, sums, ctx
+            moved[k], signal, slopes[k], slab, k, pieces, sums, ctx, waits
         )
         sums = (first_sum,)
         firsts.append(first_grad)
         gates.append(gate_grad)
-    packed = scatter_total(packed, ctx, ((firsts[0],), (firsts[-1],)))
     parts = exchange(first_sum)
     grad_signal = signal_grad(
-        jnp.concatenate(columns, axis=1), firsts, gates, tuple(k * size for k in range(pieces)),
-        slab, ctx,
-    )
-    scale = token_count ** (-0.5)
-    grad_first = block_total(parts, scale, (grad_signal,))
-    packed = packed * scale
-    a = gain_width * (hidden // tall)
-    b = a + hidden * width // (ctx * tall)
-    c = b + tall // ctx
+        factor_sorted, firsts, gates, tuple(k * size for k in range(pieces)), slab, ctx
+    )
+    grad_first, *rest = block_total(parts, pieces, ctx, scale, (grad_signal,))
+    grad_second = (
+        rest[0] if joint else Halving(second_sum.reshape(ctx, own_rows, tall), ctx, scale).finish()
+    )
     return (
         layer,
         grad_signal,
         grad_first[None],
-        packed[b:c][None],
-        packed[:a].reshape(1, gain_width, hidden),
-        packed[a:b].reshape(1, hidden // ctx, width),
-        packed[c, :gain_width][None],
+        grad_second[None],
+        grad_up,
+        grad_down,
+        grad_gain,
     )
 
 

time: 451 us -> 455 us (level)
    ppermute x3, waiting for transfers between devices: 31.9 us -> 76 us  [send(): lax.ppermute(self.give, 'ctx', [(i, i ^ bit) for i in range(self.ctx)])]
    all_to_all x5, waiting for transfers between devices: 134 us -> 93.1 us  [exchange(): return lax.all_to_all(block, 'ctx', split_axis=0, concat_axis=0, tiled=True)]
  transfers between devices with their start and end apart: 8 -> 8, of which waited for: 6 -> 6; matrix products, arithmetic and copies ran while one was open for 5% -> 4% of each run, Pallas kernels for 42% -> 39%
where the time goes in v3:
time: 455 us; the launch traced here: 454 us
  Pallas kernels  200 us (44%)
  waiting for transfers between devices  169 us (37%)
  starting transfers between devices  33.5 us (7%)
  blocking collectives  25.9 us (6%)
  local copies, waits for them, and re-layouts  22 us (5%)
    pallas_call x14, Pallas kernels, call(): pl.pallas_call(ordered, out_shape=out_shape, in_specs=[*in_specs, *[pl.Bl...  193 us
    all_to_all x5, waiting for transfers between devices, exchange(): return lax.all_to_all(block, 'ctx', split_axis=0, concat_axis=0, tiled=True)  93.1 us
    ppermute x3, waiting for transfers between devices, send(): lax.ppermute(self.give, 'ctx', [(i, i ^ bit) for i in range(self.ctx)])  76 us
    all_gather x4, blocking collectives, from_groups(): return lax.all_gather(partial_value, 'ch')  25.9 us
    all_to_all x5, starting transfers between devices, exchange(): return lax.all_to_all(block, 'ctx', split_axis=0, concat_axis=0, tiled=True)  25.9 us
  transfers between devices with their start and end apart: 8, of which 6 were waited for; matrix products, arithmetic and copies ran while one was open for 4% of the time, Pallas kernels for 39%

profile of v3, /device:TPU:0, one launch (start us, length us, event | category | flops | bytes accessed | tf_op | source)
XLA Modules:
  0.0 453.6 jit_solution(11147481235890485119)
XLA Ops:
  2.7 10.1 %first_mix.3 = (bf16[256,32,256]{2,1,0:T(8,128)(2,1)}, bf16[32,256,256]{2,1,0:T(8,128)(2,1)}) custom-call(bf16[32,512,256]{2,1,0:T(8,128)(2,1)} %refs_1_.3, bf16[256,512]{1,0:T(8,128)(2,1)} %bitcast.69), custom_call_target="tpu_custom_call" | custom-call | flops 2147483648 | bytes 16777216 | tf_op jit(solution)/shard_map/first_mix/pallas_call | solution.py:44
  12.8 7.3 %all-to-all-start.1 = ((bf16[256,32,256]{2,1,0:T(8,128)(2,1)}), bf16[256,32,256]{2,1,0:T(8,128)(2,1)}, u32[]{:S(2)}, u32[]{:S(2)}) async-start(bf16[256,32,256]{2,1,0:T(8,128)(2,1)} %get-tuple-element.48), calls=%async_computation.1 | async-start | bytes 8388608 | tf_op jit(solution)/shard_map/all_to_all | solution.py:544
  20.1 9.9 %first_mix.2 = (bf16[256,32,256]{2,1,0:T(8,128)(2,1)}, bf16[32,256,256]{2,1,0:T(8,128)(2,1)}) custom-call(bf16[32,512,256]{2,1,0:T(8,128)(2,1)} %refs_1_.3, bf16[256,512]{1,0:T(8,128)(2,1)} %bitcast.67), custom_call_target="tpu_custom_call" | custom-call | flops 2147483648 | bytes 16777216 | tf_op jit(solution)/shard_map/first_mix/pallas_call | solution.py:44
  30.0 83.4 %all-to-all-done.1 = bf16[256,32,256]{2,1,0:T(8,128)(2,1)} async-done(((bf16[256,32,256]{2,1,0:T(8,128)(2,1)}), bf16[256,32,256]{2,1,0:T(8,128)(2,1)}, u32[]{:S(2)}, u32[]{:S(2)}) %all-to-all-start.1) | async-done | bytes 4194336 | tf_op jit(solution)/shard_map/all_to_all | solution.py:544
  113.4 4.7 %all-to-all-start = ((bf16[256,32,256]{2,1,0:T(8,128)(2,1)}), bf16[256,32,256]{2,1,0:T(8,128)(2,1)}, u32[]{:S(2)}, u32[]{:S(2)}) async-start(bf16[256,32,256]{2,1,0:T(8,128)(2,1)} %get-tuple-element.47), calls=%async_computation | async-start | bytes 8388608 | tf_op jit(solution)/shard_map/all_to_all | solution.py:544
  120.9 5.5 %squares.2 = f32[16,2,256]{2,1,0:T(2,128)} custom-call(bf16[8,32,32,256]{3,2,1,0:T(8,128)(2,1)} %bitcast.9.refs_0_, bf16[256,256]{1,0:T(8,128)(2,1)} %bitcast.58), custom_call_target="tpu_custom_call" | custom-call | flops 1073741824 | bytes 4194304 | tf_op jit(solution)/shard_map/squares/pallas_call | solution.py:44
  126.4 7.1 %all-gather = f32[64,2,256]{2,1,0:T(2,128)} all-gather(f32[16,2,256]{2,1,0:T(2,128)} %squares.2), channel_id=2, replica_groups=mesh['ctx'=8,'ch'=4] {'ch'}, dimensions={0}, use_global_device_ids=true | all-gather | bytes 163840 | tf_op jit(solution)/shard_map/all_gather | solution.py:540
  136.3 25.2 %mlp.4 = (bf16[64,256,256]{2,1,0:T(8,128)(2,1)}, bf16[64,256,256]{2,1,0:T(8,128)(2,1)}, f32[8,2,256]{2,1,0:T(2,128)}, f32[256,1024]{1,0:T(8,128)}, f32[256,1024]{1,0:T(8,128)}, /*index=5*/f32[1,256]{1,0:T(1,128)}) custom-call(bf16[8,32,32,256]{3,2,1,0:T(8,128)(2,1)} %bitcast.9.refs_0_, ...), custom_call_target="tpu_custom_call", output_to_operand_aliasing={{3}: (9, {}), {4}: (10, {}), {5}: (11, {})} | custom-call | flops 12884901888 | bytes 8388608 | tf_op jit(solution)/shard_map/mlp/pallas_call | solution.py:44
  161.5 25.3 %mlp.5 = (bf16[64,256,256]{2,1,0:T(8,128)(2,1)}, bf16[64,256,256]{2,1,0:T(8,128)(2,1)}, f32[8,2,256]{2,1,0:T(2,128)}, f32[256,1024]{1,0:T(8,128)}, f32[256,1024]{1,0:T(8,128)}, /*index=5*/f32[1,256]{1,0:T(1,128)}) custom-call(bf16[8,32,32,256]{3,2,1,0:T(8,128)(2,1)} %bitcast.9.refs_0_,, ...), custom_call_target="tpu_custom_call", output_to_operand_aliasing={{3}: (9, {}), {4}: (10, {}), {5}: (11, {}), {0}: (12, {}), ... | custom-call | flops 12884901888 | bytes 8388608 | tf_op jit(solution)/shard_map/mlp/pallas_call | solution.py:44
  187.6 5.9 %all-gather.1 = f32[64,2,256]{2,1,0:T(2,128)} all-gather(f32[16,2,256]{2,1,0:T(2,128)S(1)} %pad_maximum_fusion.2), channel_id=3, replica_groups=mesh['ctx'=8,'ch'=4] {'ch'}, dimensions={0}, use_global_device_ids=true | all-gather | bytes 163840 | tf_op jit(solution)/shard_map/all_gather | solution.py:540
  194.2 12.4 %second.2 = (bf16[8,32,32,256]{3,2,1,0:T(8,128)(2,1)}, f32[256,256]{1,0:T(8,128)}) custom-call(bf16[8,32,32,256]{3,2,1,0:T(8,128)(2,1)} %bitcast.9.refs_0_, bf16[256,256]{1,0:T(8,128)(2,1)} %bitcast.72, bf16[256,256]{1,0:T(8,128)(2,1)} %bitcast.61, f32[4,16,2,256]{3,2,1,0:T(2,128)} %bitcast.80, ...), custom_call_target="tpu_custom_call", output_to_operand_aliasing={{1}: (7, {})} | custom-call | flops 3221225472 | bytes 16777216 | tf_op jit(solution)/shard_map/second/pallas_call | solution.py:44
  215.2 5.5 %squares.3 = f32[16,2,256]{2,1,0:T(2,128)} custom-call(bf16[8,32,32,256]{3,2,1,0:T(8,128)(2,1)} %bitcast.3.refs_0_, bf16[256,256]{1,0:T(8,128)(2,1)} %bitcast.62, bf16[8,32,32,256]{3,2,1,0:T(8,128)(2,1)} %get-tuple-element.57.refs_2_), custom_call_target="tpu_custom_call" | custom-call | flops 1073741824 | bytes 4194304 | tf_op jit(solution)/shard_map/squares/pallas_call | solution.py:44
  220.8 7.1 %all-gather.2 = f32[64,2,256]{2,1,0:T(2,128)} all-gather(f32[16,2,256]{2,1,0:T(2,128)} %squares.3), channel_id=4, replica_groups=mesh['ctx'=8,'ch'=4] {'ch'}, dimensions={0}, use_global_device_ids=true | all-gather | bytes 163840 | tf_op jit(solution)/shard_map/all_gather | solution.py:540
  227.9 25.3 %mlp.6 = (bf16[64,256,256]{2,1,0:T(8,128)(2,1)}, bf16[64,256,256]{2,1,0:T(8,128)(2,1)}, f32[8,2,256]{2,1,0:T(2,128)}, f32[256,1024]{1,0:T(8,128)}, f32[256,1024]{1,0:T(8,128)}, /*index=5*/f32[1,256]{1,0:T(1,128)}) custom-call(bf16[8,32,32,256]{3,2,1,0:T(8,128)(2,1)} %bitcast.3.refs_0_,, ...), custom_call_target="tpu_custom_call", output_to_operand_aliasing={{3}: (9, {}), {4}: (10, {}), {5}: (11, {}), {0}: (12, {}), ... | custom-call | flops 12884901888 | bytes 8388608 | tf_op jit(solution)/shard_map/mlp/pallas_call | solution.py:44
  253.2 25.4 %mlp.7 = (bf16[64,256,256]{2,1,0:T(8,128)(2,1)}, bf16[64,256,256]{2,1,0:T(8,128)(2,1)}, f32[8,2,256]{2,1,0:T(2,128)}, f32[256,1024]{1,0:T(8,128)}, f32[256,1024]{1,0:T(8,128)}, /*index=5*/f32[1,256]{1,0:T(1,128)}) custom-call(bf16[8,32,32,256]{3,2,1,0:T(8,128)(2,1)} %bitcast.3.refs_0_,, ...), custom_call_target="tpu_custom_call", output_to_operand_aliasing={{3}: (9, {}), {4}: (10, {}), {5}: (11, {}), {0}: (12, {}), ... | custom-call | flops 12884901888 | bytes 8388608 | tf_op jit(solution)/shard_map/mlp/pallas_call | solution.py:44
  285.4 5.9 %all-gather.3 = f32[64,2,256]{2,1,0:T(2,128)} all-gather(f32[16,2,256]{2,1,0:T(2,128)S(1)} %pad_maximum_fusion.3), channel_id=5, replica_groups=mesh['ctx'=8,'ch'=4] {'ch'}, dimensions={0}, use_global_device_ids=true | all-gather | bytes 163840 | tf_op jit(solution)/shard_map/all_gather | solution.py:540
  291.3 12.6 %second.3 = (bf16[8,32,32,256]{3,2,1,0:T(8,128)(2,1)}, f32[256,256]{1,0:T(8,128)}) custom-call(bf16[8,32,32,256]{3,2,1,0:T(8,128)(2,1)} %bitcast.3.refs_0_, bf16[256,256]{1,0:T(8,128)(2,1)} %bitcast.73, bf16[256,256]{1,0:T(8,128)(2,1)} %bitcast.65, f32[4,16,2,256]{3,2,1,0:T(2,128)} %bitcast.77, ...), custom_call_target="tpu_custom_call", output_to_operand_aliasing={{1}: (7, {})} | custom-call | flops 3221225472 | bytes 16777216 | tf_op jit(solution)/shard_map/second/pallas_call | solution.py:44
  307.9 5.7 %all-to-all-start.3 = ((bf16[256,32,256]{2,1,0:T(8,128)(2,1)}), bf16[256,32,256]{2,1,0:T(8,128)(2,1)}, u32[]{:S(2)}, u32[]{:S(2)}) async-start(bf16[256,32,256]{2,1,0:T(8,128)(2,1)} %bitcast.52), calls=%async_computation.3 | async-start | bytes 8388608 | tf_op jit(solution)/shard_map/all_to_all | solution.py:544
  321.2 10.8 %gate.2 = (bf16[32,256,256]{2,1,0:T(8,128)(2,1)}, bf16[32,256,256]{2,1,0:T(8,128)(2,1)}, bf16[8,160,256]{2,1,0:T(8,128)(2,1)}) custom-call(bf16[256,32,256]{2,1,0:T(8,128)(2,1)} %all-to-all-done.2.refs_0_, bf16[32,512,256]{2,1,0:T(8,128)(2,1)} %refs_1_.3, bf16[32,256,256]{2,1,0:T(8,128)(2,1)} %get-tuple-element.68.refs_2_, ...), custom_call_target="tpu_custom_call", output_to_operand_aliasing={{2}: (3, {})} | custom-call | flops 2147483648 | bytes 25165824 | tf_op jit(solution)/shard_map/gate/pallas_call | solution.py:44
  332.0 56.6 %collective-permute-done.1.got_ref = bf16[2,272,256]{2,1,0:T(8,128)(2,1)S(1)} collective-permute-done((bf16[2,272,256]{2,1,0:T(8,128)(2,1)S(1)}, bf16[2,272,256]{2,1,0:T(8,128)(2,1)S(1)}, u32[]{:S(2)}, u32[]{:S(2)}) %collective-permute-start.1) | collective-permute-done | bytes 278560 | tf_op jit(solution)/shard_map/ppermute | solution.py:470
  396.8 16.1 %collective-permute-done.2.got_ref = bf16[1,272,256]{2,1,0:T(8,128)(2,1)S(1)} collective-permute-done((bf16[1,272,256]{2,1,0:T(8,128)(2,1)S(1)}, bf16[1,272,256]{2,1,0:T(8,128)(2,1)S(1)}, u32[]{:S(2)}, u32[]{:S(2)}) %collective-permute-start.2) | collective-permute-done | bytes 139296 | tf_op jit(solution)/shard_map/ppermute | solution.py:470
  418.9 10.8 %gate.3 = (bf16[32,256,256]{2,1,0:T(8,128)(2,1)}, bf16[32,256,256]{2,1,0:T(8,128)(2,1)}, bf16[8,160,256]{2,1,0:T(8,128)(2,1)}) custom-call(bf16[256,32,256]{2,1,0:T(8,128)(2,1)} %all-to-all-done.3.refs_0_, bf16[32,512,256]{2,1,0:T(8,128)(2,1)} %refs_1_.3, bf16[32,256,256]{2,1,0:T(8,128)(2,1)} %get-tuple-element.79.refs_2_, ...), custom_call_target="tpu_custom_call", output_to_operand_aliasing={{2}: (3, {})} | custom-call | flops 2147483648 | bytes 25165824 | tf_op jit(solution)/shard_map/gate/pallas_call | solution.py:44
  433.3 11.8 %signal_grad.1.refs_1_ = bf16[32,512,256]{2,1,0:T(8,128)(2,1)} custom-call(bf16[512,512]{1,0:T(8,128)(2,1)} %pad_maximum_fusion.1.refs_7_.refs_0_, bf16[32,256,256]{2,1,0:T(8,128)(2,1)} %get-tuple-element.77.refs_0_.refs_1_, bf16[32,256,256]{2,1,0:T(8,128)(2,1)} %get-tuple-element.81.refs_2_, bf16[32,256,256]{2,1,0:T(8,128)(2,1)} %get-tuple-element.82.refs_3_, ...), custom_call_target="tpu_custom_call" | custom-call | flops 4294967296 | bytes 25165824 | tf_op jit(solution)/shard_map/signal_grad/pallas_call | solution.py:44
  445.1 5.7 %all-to-all-done.4.refs_0_ = bf16[8,160,256]{2,1,0:T(8,128)(2,1)S(1)} async-done(((bf16[8,160,256]{2,1,0:T(8,128)(2,1)}), bf16[8,160,256]{2,1,0:T(8,128)(2,1)S(1)}, u32[]{:S(2)}, u32[]{:S(2)}) %all-to-all-start.4) | async-done | bytes 655392 | tf_op jit(solution)/shard_map/all_to_all | solution.py:544
  (75 shorter events, 56.7 us)
Async XLA Ops:
  12.8 100.6 %all-to-all-start.1 = ((bf16[256,32,256]{2,1,0:T(8,128)(2,1)}), bf16[256,32,256]{2,1,0:T(8,128)(2,1)}, u32[]{:S(2)}, u32[]{:S(2)}) async-start(bf16[256,32,256]{2,1,0:T(8,128)(2,1)} %get-tuple-element.48), calls=%async_computation.1 | async-start | bytes 8388608 | tf_op jit(solution)/shard_map/all_to_all | solution.py:544
  113.4 4.7 %copy-start.7 = (bf16[1,256,256]{2,1,0:T(8,128)(2,1)S(1)}, bf16[1,256,256]{2,1,0:T(8,128)(2,1)}, u32[]{:S(2)}) copy-start(bf16[1,256,256]{2,1,0:T(8,128)(2,1)} %param.9) | copy-start | bytes 393220
  113.4 5.5 %copy-start.8 = (bf16[1,256,1024]{2,1,0:T(8,128)(2,1)S(1)}, bf16[1,256,1024]{2,1,0:T(8,128)(2,1)}, u32[]{:S(2)}) copy-start(bf16[1,256,1024]{2,1,0:T(8,128)(2,1)} %param.10) | copy-start | bytes 1572868
  113.4 6.5 %copy-start.9 = (bf16[1,1024,256]{2,1,0:T(8,128)(2,1)S(1)}, bf16[1,1024,256]{2,1,0:T(8,128)(2,1)}, u32[]{:S(2)}) copy-start(bf16[1,1024,256]{2,1,0:T(8,128)(2,1)} %param.11) | copy-start | bytes 1572868
  113.4 97.2 %all-to-all-start = ((bf16[256,32,256]{2,1,0:T(8,128)(2,1)}), bf16[256,32,256]{2,1,0:T(8,128)(2,1)}, u32[]{:S(2)}, u32[]{:S(2)}) async-start(bf16[256,32,256]{2,1,0:T(8,128)(2,1)} %get-tuple-element.47), calls=%async_computation | async-start | bytes 8388608 | tf_op jit(solution)/shard_map/all_to_all | solution.py:544
  161.5 25.3 %copy-start.14 = (f32[8,2,256]{2,1,0:T(2,128)S(1)}, f32[8,2,256]{2,1,0:T(2,128)}, u32[]{:S(2)}) copy-start(f32[8,2,256]{2,1,0:T(2,128)} %get-tuple-element.49) | copy-start | bytes 49156
  210.6 97.3 %all-to-all-start.2 = ((bf16[256,32,256]{2,1,0:T(8,128)(2,1)}), bf16[256,32,256]{2,1,0:T(8,128)(2,1)}, u32[]{:S(2)}, u32[]{:S(2)}) async-start(bf16[256,32,256]{2,1,0:T(8,128)(2,1)} %bitcast.53), calls=%async_computation.2 | async-start | bytes 8388608 | tf_op jit(solution)/shard_map/all_to_all | solution.py:544
  278.7 3.7 copy-start.15
  280.2 5.1 %copy-start.12 = (f32[8,2,256]{2,1,0:T(2,128)S(1)}, f32[8,2,256]{2,1,0:T(2,128)}, u32[]{:S(2)}) copy-start(f32[8,2,256]{2,1,0:T(2,128)} %get-tuple-element.69) | copy-start | bytes 49156
  280.3 5.1 %copy-start.13 = (f32[8,2,256]{2,1,0:T(2,128)S(1)}, f32[8,2,256]{2,1,0:T(2,128)}, u32[]{:S(2)}) copy-start(f32[8,2,256]{2,1,0:T(2,128)} %get-tuple-element.70) | copy-start | bytes 49156
  283.3 20.5 %copy-start = (f32[4,2,272,256]{3,2,1,0:T(8,128)}, f32[4,2,272,256]{3,2,1,0:T(8,128)S(1)}, u32[]{:S(2)}) copy-start(f32[4,2,272,256]{3,2,1,0:T(8,128)S(1)} %pad_maximum_fusion.values_ref) | copy-start | bytes 6684676
  283.4 7.8 %copy-start.6 = (bf16[4,272,256]{2,1,0:T(8,128)(2,1)}, bf16[4,272,256]{2,1,0:T(8,128)(2,1)S(1)}, u32[]{:S(2)}) copy-start(bf16[4,272,256]{2,1,0:T(8,128)(2,1)S(1)} %fusion.refs_8_) | copy-start | bytes 1671172
  283.4 23.7 %collective-permute-start = (bf16[4,272,256]{2,1,0:T(8,128)(2,1)S(1)}, bf16[4,272,256]{2,1,0:T(8,128)(2,1)S(1)}, u32[]{:S(2)}, u32[]{:S(2)}) collective-permute-start(bf16[4,272,256]{2,1,0:T(8,128)(2,1)S(1)} %fusion.refs_8_), channel_id=1, source_target_pairs={{0,4},{4,0},{8,12},{12,8},{16,20},{20,16},{24,28},{28,24},{1,5},{5... | collective-permute-start | bytes 1671176 | tf_op jit(solution)/shard_map/ppermute | solution.py:470
  307.1 0.8 copy-start.5
  307.9 111.0 %all-to-all-start.3 = ((bf16[256,32,256]{2,1,0:T(8,128)(2,1)}), bf16[256,32,256]{2,1,0:T(8,128)(2,1)}, u32[]{:S(2)}, u32[]{:S(2)}) async-start(bf16[256,32,256]{2,1,0:T(8,128)(2,1)} %bitcast.52), calls=%async_computation.3 | async-start | bytes 8388608 | tf_op jit(solution)/shard_map/all_to_all | solution.py:544
  313.6 6.7 %copy-start.1 = (f32[256,256]{1,0:T(8,128)S(1)}, f32[256,256]{1,0:T(8,128)}, u32[]{:S(2)}) copy-start(f32[256,256]{1,0:T(8,128)} %get-tuple-element.76) | copy-start | bytes 786436
  318.2 70.4 %collective-permute-start.1 = (bf16[2,272,256]{2,1,0:T(8,128)(2,1)S(1)}, bf16[2,272,256]{2,1,0:T(8,128)(2,1)S(1)}, u32[]{:S(2)}, u32[]{:S(2)}) collective-permute-start(bf16[2,272,256]{2,1,0:T(8,128)(2,1)S(1)} %fusion.1), channel_id=1, source_target_pairs={{0,8},{4,12},{8,0},{12,4},{16,24},{20,28},{24,16},{28,20},{1,9},{5... | collective-permute-start | bytes 835592 | tf_op jit(solution)/shard_map/ppermute | solution.py:470
  332.0 63.7 %copy-start.4 = (bf16[512,8,1,32]{0,3,2,1:T(8,128)(2,1)S(1)}, bf16[512,8,1,32]{0,3,2,1:T(8,128)(2,1)}, u32[]{:S(2)}) copy-start(bf16[512,8,1,32]{0,3,2,1:T(8,128)(2,1)} %get-tuple-element.87) | copy-start | bytes 786436
  332.0 63.8 %copy-start.3 = (bf16[512,8,1,32]{0,3,2,1:T(8,128)(2,1)S(1)}, bf16[512,8,1,32]{0,3,2,1:T(8,128)(2,1)}, u32[]{:S(2)}) copy-start(bf16[512,8,1,32]{0,3,2,1:T(8,128)(2,1)} %get-tuple-element.88) | copy-start | bytes 786436
  388.6 0.7 copy-start.10
  392.2 20.8 %collective-permute-start.2 = (bf16[1,272,256]{2,1,0:T(8,128)(2,1)S(1)}, bf16[1,272,256]{2,1,0:T(8,128)(2,1)S(1)}, u32[]{:S(2)}, u32[]{:S(2)}) collective-permute-start(bf16[1,272,256]{2,1,0:T(8,128)(2,1)S(1)} %dynamic-slice_convert_fusion), channel_id=1, source_target_pairs={{0,16},{4,20},{8,24},{12,28},{16,0},{20,4},{24,8},{28,12},{1,17},{... | collective-permute-start | bytes 417800 | tf_op jit(solution)/shard_map/ppermute | solution.py:470
  413.0 0.7 copy-start.11
  429.6 21.1 %all-to-all-start.4 = ((bf16[8,160,256]{2,1,0:T(8,128)(2,1)}), bf16[8,160,256]{2,1,0:T(8,128)(2,1)S(1)}, u32[]{:S(2)}, u32[]{:S(2)}) async-start(bf16[8,160,256]{2,1,0:T(8,128)(2,1)} %get-tuple-element.84), calls=%async_computation.4 | async-start | bytes 1310720 | tf_op jit(solution)/shard_map/all_to_all | solution.py:544
  450.8 0.9 copy-start.2

commit v4 on v3

--- a/solution.py
+++ b/solution.py
@@ -452,6 +452,43 @@
     )(mine.reshape(1), values, got, *after)
 
 
+def finish_body(scale, mine_ref, values_ref, got_ref, *refs):
+    del mine_ref
+    up_ref, down_ref, gain_ref = refs[-3:]
+    total = (values_ref[0, 0] + got_ref[0].astype(F32)) * scale
+    rows, width = up_ref.shape[0], total.shape[1]
+    start = 0
+    for lane in range(0, up_ref.shape[1], width):
+        up_ref[:, lane : lane + width] = total[start : start + rows]
+        start += rows
+    down_ref[...] = total[start : start + down_ref.shape[0]]
+    start += down_ref.shape[0]
+    gain_ref[...] = total[start : start + 1, : gain_ref.shape[1]]
+
+
+def finish_weights(values, got, mine, shapes, scale, after):
+    _, _, rows, columns = values.shape
+    return pl.pallas_call(
+        functools.partial(finish_body, scale),
+        out_shape=tuple(jax.ShapeDtypeStruct(shape, F32) for shape in shapes),
+        grid_spec=pltpu.PrefetchScalarGridSpec(
+            num_scalar_prefetch=1,
+            grid=(1,),
+            in_specs=[
+                pl.BlockSpec((1, 1, rows, columns), lambda s, mine: (0, mine[0], 0, 0)),
+                pl.BlockSpec((1, rows, columns), lambda s, mine: (0, 0, 0)),
+                *([pl.BlockSpec(memory_space=pl.ANY)] * len(after)),
+            ],
+            out_specs=tuple(pl.BlockSpec(shape, lambda s, mine: (0, 0)) for shape in shapes),
+        ),
+        compiler_params=pltpu.CompilerParams(vmem_limit_bytes=56 * MIB),
+        cost_estimate=pl.CostEstimate(
+            flops=got.size, bytes_accessed=10 * got.size, transcendentals=0
+        ),
+        name="finish_weights",
+    )(mine.reshape(1), values, got, *after)
+
+
 class Halving:
     def __init__(self, values, ctx, scale):
         self.ctx, self.bit, self.scale = ctx, 1, scale
@@ -589,11 +626,13 @@
             up_sum, down_sum, gain_sum = sums
             packed = jnp.concatenate(
                 [
-                    up_sum.reshape(ctx, gain_width * (hidden // tall), tall),
-                    down_sum.T.reshape(ctx, hidden * width // (ctx * tall), tall),
+                    up_sum.reshape(ctx, gain_width, hidden // width, width)
+                    .transpose(0, 2, 1, 3)
+                    .reshape(ctx, hidden // ctx, width),
+                    down_sum.T.reshape(ctx, hidden // ctx, width),
                     jnp.pad(
                         gain_sum.reshape(ctx, 1, gain_width),
-                        ((0, 0), (0, 15), (0, tall - gain_width)),
+                        ((0, 0), (0, 15), (0, width - gain_width)),
                     ),
                 ],
                 axis=1,
@@ -618,13 +657,10 @@
         sums = (jnp.pad(second_sum.reshape(ctx, own_rows, tall).astype(BF16), above),)
     for k in range(pieces):
         if k == pieces - 1:
-            packed = weights.finish(tuple(firsts))
-            a = gain_width * (hidden // tall)
-            b = a + hidden * width // (ctx * tall)
-            grad_up = packed[:a].reshape(1, gain_width, hidden)
-            grad_down = packed[a:b].reshape(1, hidden // ctx, width)
-            grad_gain = packed[b, :gain_width][None]
-            waits = (grad_up, grad_down, grad_gain, factor_sorted)
+            while 2 * weights.bit < ctx:
+                weights.send()
+                weights.keep(tuple(firsts))
+            waits = (weights.give, factor_sorted)
         first_grad, gate_grad, first_sum = gate(
             moved[k], signal, slopes[k], slab, k, pieces, sums, ctx, waits
         )
@@ -635,7 +671,11 @@
     grad_signal = signal_grad(
         factor_sorted, firsts, gates, tuple(k * size for k in range(pieces)), slab, ctx
     )
-    grad_first, *rest = block_total(parts, pieces, ctx, scale, (grad_signal,))
+    grad_up, grad_down, grad_gain = finish_weights(
+        weights.halves, weights.send(), weights.mine,
+        ((gain_width, hidden), (hidden // ctx, width), (1, gain_width)), scale, (grad_signal,),
+    )
+    grad_first, *rest = block_total(parts, pieces, ctx, scale, (grad_signal, grad_gain))
     grad_second = (
         rest[0] if joint else Halving(second_sum.reshape(ctx, own_rows, tall), ctx, scale).finish()
     )
@@ -644,8 +684,8 @@
         grad_signal,
         grad_first[None],
         grad_second[None],
-        grad_up,
-        grad_down,
+        grad_up[None],
+        grad_down[None],
         grad_gain,
     )
 

time: 455 us -> 452 us (level)
    all_to_all x5, waiting for transfers between devices: 93.1 us -> 102 us  [exchange(): return lax.all_to_all(block, 'ctx', split_axis=0, concat_axis=0, tiled=True)]
    ppermute x3, waiting for transfers between devices: 76 us -> 67.9 us  [send(): lax.ppermute(self.give, 'ctx', [(i, i ^ bit) for i in range(self.ctx)])]
  transfers between devices with their start and end apart: 8 -> 8, of which waited for: 6 -> 7; matrix products, arithmetic and copies ran while one was open for 4% -> 3% of each run, Pallas kernels for 39% -> 39%
where the time goes in v4:
time: 452 us; the launch traced here: 450 us
  Pallas kernels  200 us (44%)
  waiting for transfers between devices  170 us (38%)
  starting transfers between devices  33.1 us (7%)
  blocking collectives  25.9 us (6%)
  local copies, waits for them, and re-layouts  18.3 us (4%)
    pallas_call x14, Pallas kernels, call(): pl.pallas_call(ordered, out_shape=out_shape, in_specs=[*in_specs, *[pl.Bl...  192 us
    all_to_all x5, waiting for transfers between devices, exchange(): return lax.all_to_all(block, 'ctx', split_axis=0, concat_axis=0, tiled=True)  102 us
    ppermute x3, waiting for transfers between devices, send(): lax.ppermute(self.give, 'ctx', [(i, i ^ bit) for i in range(self.ctx)])  67.9 us
    all_to_all x5, starting transfers between devices, exchange(): return lax.all_to_all(block, 'ctx', split_axis=0, concat_axis=0, tiled=True)  26.2 us
    all_gather x4, blocking collectives, from_groups(): return lax.all_gather(partial_value, 'ch')  25.9 us
  transfers between devices with their start and end apart: 8, of which 7 were waited for; matrix products, arithmetic and copies ran while one was open for 3% of the time, Pallas kernels for 39%

profile of v4, /device:TPU:0, one launch (start us, length us, event | category | flops | bytes accessed | tf_op | source)
XLA Modules:
  0.0 450.3 jit_solution(11629602124611019532)
XLA Ops:
  2.7 10.1 %first_mix.3 = (bf16[256,32,256]{2,1,0:T(8,128)(2,1)}, bf16[32,256,256]{2,1,0:T(8,128)(2,1)}) custom-call(bf16[32,512,256]{2,1,0:T(8,128)(2,1)} %refs_1_.3, bf16[256,512]{1,0:T(8,128)(2,1)} %bitcast.74), custom_call_target="tpu_custom_call" | custom-call | flops 2147483648 | bytes 16777216 | tf_op jit(solution)/shard_map/first_mix/pallas_call | solution.py:44
  12.8 7.3 %all-to-all-start.1 = ((bf16[256,32,256]{2,1,0:T(8,128)(2,1)}), bf16[256,32,256]{2,1,0:T(8,128)(2,1)}, u32[]{:S(2)}, u32[]{:S(2)}) async-start(bf16[256,32,256]{2,1,0:T(8,128)(2,1)} %get-tuple-element.51), calls=%async_computation.1 | async-start | bytes 8388608 | tf_op jit(solution)/shard_map/all_to_all | solution.py:581
  20.1 9.9 %first_mix.2 = (bf16[256,32,256]{2,1,0:T(8,128)(2,1)}, bf16[32,256,256]{2,1,0:T(8,128)(2,1)}) custom-call(bf16[32,512,256]{2,1,0:T(8,128)(2,1)} %refs_1_.3, bf16[256,512]{1,0:T(8,128)(2,1)} %bitcast.72), custom_call_target="tpu_custom_call" | custom-call | flops 2147483648 | bytes 16777216 | tf_op jit(solution)/shard_map/first_mix/pallas_call | solution.py:44
  30.0 83.4 %all-to-all-done.1 = bf16[256,32,256]{2,1,0:T(8,128)(2,1)} async-done(((bf16[256,32,256]{2,1,0:T(8,128)(2,1)}), bf16[256,32,256]{2,1,0:T(8,128)(2,1)}, u32[]{:S(2)}, u32[]{:S(2)}) %all-to-all-start.1) | async-done | bytes 4194336 | tf_op jit(solution)/shard_map/all_to_all | solution.py:581
  113.4 4.7 %all-to-all-start = ((bf16[256,32,256]{2,1,0:T(8,128)(2,1)}), bf16[256,32,256]{2,1,0:T(8,128)(2,1)}, u32[]{:S(2)}, u32[]{:S(2)}) async-start(bf16[256,32,256]{2,1,0:T(8,128)(2,1)} %get-tuple-element.50), calls=%async_computation | async-start | bytes 8388608 | tf_op jit(solution)/shard_map/all_to_all | solution.py:581
  120.9 5.5 %squares.2 = f32[16,2,256]{2,1,0:T(2,128)} custom-call(bf16[8,32,32,256]{3,2,1,0:T(8,128)(2,1)} %bitcast.9.refs_0_, bf16[256,256]{1,0:T(8,128)(2,1)} %bitcast.63), custom_call_target="tpu_custom_call" | custom-call | flops 1073741824 | bytes 4194304 | tf_op jit(solution)/shard_map/squares/pallas_call | solution.py:44
  126.4 7.1 %all-gather = f32[64,2,256]{2,1,0:T(2,128)} all-gather(f32[16,2,256]{2,1,0:T(2,128)} %squares.2), channel_id=2, replica_groups=mesh['ctx'=8,'ch'=4] {'ch'}, dimensions={0}, use_global_device_ids=true | all-gather | bytes 163840 | tf_op jit(solution)/shard_map/all_gather | solution.py:577
  136.2 25.2 %mlp.4 = (bf16[64,256,256]{2,1,0:T(8,128)(2,1)}, bf16[64,256,256]{2,1,0:T(8,128)(2,1)}, f32[8,2,256]{2,1,0:T(2,128)}, f32[256,1024]{1,0:T(8,128)}, f32[256,1024]{1,0:T(8,128)}, /*index=5*/f32[1,256]{1,0:T(1,128)}) custom-call(bf16[8,32,32,256]{3,2,1,0:T(8,128)(2,1)} %bitcast.9.refs_0_, ...), custom_call_target="tpu_custom_call", output_to_operand_aliasing={{3}: (9, {}), {4}: (10, {}), {5}: (11, {})} | custom-call | flops 12884901888 | bytes 8388608 | tf_op jit(solution)/shard_map/mlp/pallas_call | solution.py:44
  161.5 25.3 %mlp.5 = (bf16[64,256,256]{2,1,0:T(8,128)(2,1)}, bf16[64,256,256]{2,1,0:T(8,128)(2,1)}, f32[8,2,256]{2,1,0:T(2,128)}, f32[256,1024]{1,0:T(8,128)}, f32[256,1024]{1,0:T(8,128)}, /*index=5*/f32[1,256]{1,0:T(1,128)}) custom-call(bf16[8,32,32,256]{3,2,1,0:T(8,128)(2,1)} %bitcast.9.refs_0_,, ...), custom_call_target="tpu_custom_call", output_to_operand_aliasing={{3}: (9, {}), {4}: (10, {}), {5}: (11, {}), {0}: (12, {}), ... | custom-call | flops 12884901888 | bytes 8388608 | tf_op jit(solution)/shard_map/mlp/pallas_call | solution.py:44
  187.5 5.9 %all-gather.1 = f32[64,2,256]{2,1,0:T(2,128)} all-gather(f32[16,2,256]{2,1,0:T(2,128)S(1)} %pad_maximum_fusion.2), channel_id=3, replica_groups=mesh['ctx'=8,'ch'=4] {'ch'}, dimensions={0}, use_global_device_ids=true | all-gather | bytes 163840 | tf_op jit(solution)/shard_map/all_gather | solution.py:577
  194.1 12.4 %second.2 = (bf16[8,32,32,256]{3,2,1,0:T(8,128)(2,1)}, f32[256,256]{1,0:T(8,128)}) custom-call(bf16[8,32,32,256]{3,2,1,0:T(8,128)(2,1)} %bitcast.9.refs_0_, bf16[256,256]{1,0:T(8,128)(2,1)} %bitcast.77, bf16[256,256]{1,0:T(8,128)(2,1)} %bitcast.66, f32[4,16,2,256]{3,2,1,0:T(2,128)} %bitcast.84, ...), custom_call_target="tpu_custom_call", output_to_operand_aliasing={{1}: (7, {})} | custom-call | flops 3221225472 | bytes 16777216 | tf_op jit(solution)/shard_map/second/pallas_call | solution.py:44
  215.3 5.5 %squares.3 = f32[16,2,256]{2,1,0:T(2,128)} custom-call(bf16[8,32,32,256]{3,2,1,0:T(8,128)(2,1)} %bitcast.3.refs_0_, bf16[256,256]{1,0:T(8,128)(2,1)} %bitcast.67, bf16[8,32,32,256]{3,2,1,0:T(8,128)(2,1)} %get-tuple-element.60.refs_2_), custom_call_target="tpu_custom_call" | custom-call | flops 1073741824 | bytes 4194304 | tf_op jit(solution)/shard_map/squares/pallas_call | solution.py:44
  220.8 7.1 %all-gather.2 = f32[64,2,256]{2,1,0:T(2,128)} all-gather(f32[16,2,256]{2,1,0:T(2,128)} %squares.3), channel_id=4, replica_groups=mesh['ctx'=8,'ch'=4] {'ch'}, dimensions={0}, use_global_device_ids=true | all-gather | bytes 163840 | tf_op jit(solution)/shard_map/all_gather | solution.py:577
  227.9 25.3 %mlp.6 = (bf16[64,256,256]{2,1,0:T(8,128)(2,1)}, bf16[64,256,256]{2,1,0:T(8,128)(2,1)}, f32[8,2,256]{2,1,0:T(2,128)}, f32[256,1024]{1,0:T(8,128)}, f32[256,1024]{1,0:T(8,128)}, /*index=5*/f32[1,256]{1,0:T(1,128)}) custom-call(bf16[8,32,32,256]{3,2,1,0:T(8,128)(2,1)} %bitcast.3.refs_0_,, ...), custom_call_target="tpu_custom_call", output_to_operand_aliasing={{3}: (9, {}), {4}: (10, {}), {5}: (11, {}), {0}: (12, {}), ... | custom-call | flops 12884901888 | bytes 8388608 | tf_op jit(solution)/shard_map/mlp/pallas_call | solution.py:44
  253.2 25.4 %mlp.7 = (bf16[64,256,256]{2,1,0:T(8,128)(2,1)}, bf16[64,256,256]{2,1,0:T(8,128)(2,1)}, f32[8,2,256]{2,1,0:T(2,128)}, f32[256,1024]{1,0:T(8,128)}, f32[256,1024]{1,0:T(8,128)}, /*index=5*/f32[1,256]{1,0:T(1,128)}) custom-call(bf16[8,32,32,256]{3,2,1,0:T(8,128)(2,1)} %bitcast.3.refs_0_,, ...), custom_call_target="tpu_custom_call", output_to_operand_aliasing={{3}: (9, {}), {4}: (10, {}), {5}: (11, {}), {0}: (12, {}), ... | custom-call | flops 12884901888 | bytes 8388608 | tf_op jit(solution)/shard_map/mlp/pallas_call | solution.py:44
  284.6 5.9 %all-gather.3 = f32[64,2,256]{2,1,0:T(2,128)} all-gather(f32[16,2,256]{2,1,0:T(2,128)S(1)} %pad_maximum_fusion.3), channel_id=5, replica_groups=mesh['ctx'=8,'ch'=4] {'ch'}, dimensions={0}, use_global_device_ids=true | all-gather | bytes 163840 | tf_op jit(solution)/shard_map/all_gather | solution.py:577
  290.4 12.5 %second.3 = (bf16[8,32,32,256]{3,2,1,0:T(8,128)(2,1)}, f32[256,256]{1,0:T(8,128)}) custom-call(bf16[8,32,32,256]{3,2,1,0:T(8,128)(2,1)} %bitcast.3.refs_0_, bf16[256,256]{1,0:T(8,128)(2,1)} %bitcast.78, bf16[256,256]{1,0:T(8,128)(2,1)} %bitcast.70, f32[4,16,2,256]{3,2,1,0:T(2,128)} %bitcast.81, ...), custom_call_target="tpu_custom_call", output_to_operand_aliasing={{1}: (7, {})} | custom-call | flops 3221225472 | bytes 16777216 | tf_op jit(solution)/shard_map/second/pallas_call | solution.py:44
  307.8 5.9 %all-to-all-start.3 = ((bf16[256,32,256]{2,1,0:T(8,128)(2,1)}), bf16[256,32,256]{2,1,0:T(8,128)(2,1)}, u32[]{:S(2)}, u32[]{:S(2)}) async-start(bf16[256,32,256]{2,1,0:T(8,128)(2,1)} %bitcast.56), calls=%async_computation.3 | async-start | bytes 8388608 | tf_op jit(solution)/shard_map/all_to_all | solution.py:581
  322.5 10.7 %gate.2 = (bf16[32,256,256]{2,1,0:T(8,128)(2,1)}, bf16[32,256,256]{2,1,0:T(8,128)(2,1)}, bf16[8,160,256]{2,1,0:T(8,128)(2,1)}) custom-call(bf16[256,32,256]{2,1,0:T(8,128)(2,1)} %all-to-all-done.2.refs_0_, bf16[32,512,256]{2,1,0:T(8,128)(2,1)} %refs_1_.3, bf16[32,256,256]{2,1,0:T(8,128)(2,1)} %get-tuple-element.71.refs_2_, ...), custom_call_target="tpu_custom_call", output_to_operand_aliasing={{2}: (3, {})} | custom-call | flops 2147483648 | bytes 25165824 | tf_op jit(solution)/shard_map/gate/pallas_call | solution.py:44
  333.3 55.5 %collective-permute-done.1.got_ref = bf16[2,272,256]{2,1,0:T(8,128)(2,1)S(1)} collective-permute-done((bf16[2,272,256]{2,1,0:T(8,128)(2,1)S(1)}, bf16[2,272,256]{2,1,0:T(8,128)(2,1)S(1)}, u32[]{:S(2)}, u32[]{:S(2)}) %collective-permute-start.1) | collective-permute-done | bytes 278560 | tf_op jit(solution)/shard_map/ppermute | solution.py:507
  393.0 14.3 %all-to-all-done.3.refs_0_ = bf16[256,32,256]{2,1,0:T(8,128)(2,1)} async-done(((bf16[256,32,256]{2,1,0:T(8,128)(2,1)}), bf16[256,32,256]{2,1,0:T(8,128)(2,1)}, u32[]{:S(2)}, u32[]{:S(2)}) %all-to-all-start.3) | async-done | bytes 4194336 | tf_op jit(solution)/shard_map/all_to_all | solution.py:581
  407.3 10.8 %gate.3 = (bf16[32,256,256]{2,1,0:T(8,128)(2,1)}, bf16[32,256,256]{2,1,0:T(8,128)(2,1)}, bf16[8,160,256]{2,1,0:T(8,128)(2,1)}) custom-call(bf16[256,32,256]{2,1,0:T(8,128)(2,1)} %all-to-all-done.3.refs_0_, bf16[32,512,256]{2,1,0:T(8,128)(2,1)} %refs_1_.3, bf16[32,256,256]{2,1,0:T(8,128)(2,1)} %get-tuple-element.82.refs_2_, ...), custom_call_target="tpu_custom_call", output_to_operand_aliasing={{2}: (3, {})} | custom-call | flops 2147483648 | bytes 25165824 | tf_op jit(solution)/shard_map/gate/pallas_call | solution.py:44
  424.6 11.8 %signal_grad.1.refs_0_.refs_1_ = bf16[32,512,256]{2,1,0:T(8,128)(2,1)} custom-call(bf16[512,512]{1,0:T(8,128)(2,1)} %pad_maximum_fusion.1.refs_5_.refs_0_, bf16[32,256,256]{2,1,0:T(8,128)(2,1)} %get-tuple-element.80.refs_0_.refs_1_, bf16[32,256,256]{2,1,0:T(8,128)(2,1)} %get-tuple-element.84.refs_2_, bf16[32,256,256]{2,1,0:T(8,128)(2,1)} %get-tuple-element.85.refs_3_, ...), custom_call_target="tpu_custom_call" | custom-call | flops 4294967296 | bytes 25165824 | tf_op jit(solution)/shard_map/signal_grad/pallas_call | solution.py:44
  436.4 8.8 %collective-permute-done.2.got_ref = bf16[1,272,256]{2,1,0:T(8,128)(2,1)S(1)} collective-permute-done((bf16[1,272,256]{2,1,0:T(8,128)(2,1)S(1)}, bf16[1,272,256]{2,1,0:T(8,128)(2,1)S(1)}, u32[]{:S(2)}, u32[]{:S(2)}) %collective-permute-start.2) | collective-permute-done | bytes 139296 | tf_op jit(solution)/shard_map/ppermute | solution.py:507
  (77 shorter events, 53.1 us)
Async XLA Ops:
  12.8 100.6 %all-to-all-start.1 = ((bf16[256,32,256]{2,1,0:T(8,128)(2,1)}), bf16[256,32,256]{2,1,0:T(8,128)(2,1)}, u32[]{:S(2)}, u32[]{:S(2)}) async-start(bf16[256,32,256]{2,1,0:T(8,128)(2,1)} %get-tuple-element.51), calls=%async_computation.1 | async-start | bytes 8388608 | tf_op jit(solution)/shard_map/all_to_all | solution.py:581
  113.4 4.7 %copy-start.8 = (bf16[1,256,256]{2,1,0:T(8,128)(2,1)S(1)}, bf16[1,256,256]{2,1,0:T(8,128)(2,1)}, u32[]{:S(2)}) copy-start(bf16[1,256,256]{2,1,0:T(8,128)(2,1)} %param.9) | copy-start | bytes 393220
  113.4 5.5 %copy-start.10 = (bf16[1,256,1024]{2,1,0:T(8,128)(2,1)S(1)}, bf16[1,256,1024]{2,1,0:T(8,128)(2,1)}, u32[]{:S(2)}) copy-start(bf16[1,256,1024]{2,1,0:T(8,128)(2,1)} %param.10) | copy-start | bytes 1572868
  113.4 6.5 %copy-start.11 = (bf16[1,1024,256]{2,1,0:T(8,128)(2,1)S(1)}, bf16[1,1024,256]{2,1,0:T(8,128)(2,1)}, u32[]{:S(2)}) copy-start(bf16[1,1024,256]{2,1,0:T(8,128)(2,1)} %param.11) | copy-start | bytes 1572868
  113.4 97.2 %all-to-all-start = ((bf16[256,32,256]{2,1,0:T(8,128)(2,1)}), bf16[256,32,256]{2,1,0:T(8,128)(2,1)}, u32[]{:S(2)}, u32[]{:S(2)}) async-start(bf16[256,32,256]{2,1,0:T(8,128)(2,1)} %get-tuple-element.50), calls=%async_computation | async-start | bytes 8388608 | tf_op jit(solution)/shard_map/all_to_all | solution.py:581
  161.5 25.3 %copy-start.16 = (f32[8,2,256]{2,1,0:T(2,128)S(1)}, f32[8,2,256]{2,1,0:T(2,128)}, u32[]{:S(2)}) copy-start(f32[8,2,256]{2,1,0:T(2,128)} %get-tuple-element.52) | copy-start | bytes 49156
  210.7 97.2 %all-to-all-start.2 = ((bf16[256,32,256]{2,1,0:T(8,128)(2,1)}), bf16[256,32,256]{2,1,0:T(8,128)(2,1)}, u32[]{:S(2)}, u32[]{:S(2)}) async-start(bf16[256,32,256]{2,1,0:T(8,128)(2,1)} %bitcast.57), calls=%async_computation.2 | async-start | bytes 8388608 | tf_op jit(solution)/shard_map/all_to_all | solution.py:581
  278.6 2.0 copy-start.2
  278.6 2.9 copy-start.17
  280.6 3.9 copy-start.14
  280.6 3.9 copy-start.15
  282.5 20.5 %copy-start = (f32[4,2,272,256]{3,2,1,0:T(8,128)}, f32[4,2,272,256]{3,2,1,0:T(8,128)S(1)}, u32[]{:S(2)}) copy-start(f32[4,2,272,256]{3,2,1,0:T(8,128)S(1)} %pad_maximum_fusion.values_ref) | copy-start | bytes 6684676
  282.6 7.8 %copy-start.7 = (bf16[4,272,256]{2,1,0:T(8,128)(2,1)}, bf16[4,272,256]{2,1,0:T(8,128)(2,1)S(1)}, u32[]{:S(2)}) copy-start(bf16[4,272,256]{2,1,0:T(8,128)(2,1)S(1)} %fusion.refs_8_) | copy-start | bytes 1671172
  282.6 24.0 %collective-permute-start = (bf16[4,272,256]{2,1,0:T(8,128)(2,1)S(1)}, bf16[4,272,256]{2,1,0:T(8,128)(2,1)S(1)}, u32[]{:S(2)}, u32[]{:S(2)}) collective-permute-start(bf16[4,272,256]{2,1,0:T(8,128)(2,1)S(1)} %fusion.refs_8_), channel_id=1, source_target_pairs={{0,4},{4,0},{8,12},{12,8},{16,20},{20,16},{24,28},{28,24},{1,5},{5... | collective-permute-start | bytes 1671176 | tf_op jit(solution)/shard_map/ppermute | solution.py:507
  306.6 0.8 copy-start.6
  307.8 6.0 %copy-start.5 = (bf16[512,8,1,32]{0,3,2,1:T(8,128)(2,1)S(1)}, bf16[512,8,1,32]{0,3,2,1:T(8,128)(2,1)}, u32[]{:S(2)}) copy-start(bf16[512,8,1,32]{0,3,2,1:T(8,128)(2,1)} %get-tuple-element.93) | copy-start | bytes 786436
  307.8 6.1 %copy-start.4 = (bf16[512,8,1,32]{0,3,2,1:T(8,128)(2,1)S(1)}, bf16[512,8,1,32]{0,3,2,1:T(8,128)(2,1)}, u32[]{:S(2)}) copy-start(bf16[512,8,1,32]{0,3,2,1:T(8,128)(2,1)} %get-tuple-element.94) | copy-start | bytes 786436
  307.8 99.4 %all-to-all-start.3 = ((bf16[256,32,256]{2,1,0:T(8,128)(2,1)}), bf16[256,32,256]{2,1,0:T(8,128)(2,1)}, u32[]{:S(2)}, u32[]{:S(2)}) async-start(bf16[256,32,256]{2,1,0:T(8,128)(2,1)} %bitcast.56), calls=%async_computation.3 | async-start | bytes 8388608 | tf_op jit(solution)/shard_map/all_to_all | solution.py:581
  314.1 7.5 %copy-start.1 = (f32[256,256]{1,0:T(8,128)S(1)}, f32[256,256]{1,0:T(8,128)}, u32[]{:S(2)}) copy-start(f32[256,256]{1,0:T(8,128)} %get-tuple-element.79) | copy-start | bytes 786436
  318.7 70.0 %collective-permute-start.1 = (bf16[2,272,256]{2,1,0:T(8,128)(2,1)S(1)}, bf16[2,272,256]{2,1,0:T(8,128)(2,1)S(1)}, u32[]{:S(2)}, u32[]{:S(2)}) collective-permute-start(bf16[2,272,256]{2,1,0:T(8,128)(2,1)S(1)} %fusion.1), channel_id=1, source_target_pairs={{0,8},{4,12},{8,0},{12,4},{16,24},{20,28},{24,16},{28,20},{1,9},{5... | collective-permute-start | bytes 835592 | tf_op jit(solution)/shard_map/ppermute | solution.py:507
  407.3 14.4 %copy-start.9 = (bf16[1,272,256]{2,1,0:T(8,128)(2,1)S(1)}, bf16[1,272,256]{2,1,0:T(8,128)(2,1)}, u32[]{:S(2)}) copy-start(bf16[1,272,256]{2,1,0:T(8,128)(2,1)} %dynamic-slice_convert_fusion.refs_4_) | copy-start | bytes 417796
  418.1 29.4 %all-to-all-start.4 = ((bf16[8,160,256]{2,1,0:T(8,128)(2,1)}), bf16[8,160,256]{2,1,0:T(8,128)(2,1)S(1)}, u32[]{:S(2)}, u32[]{:S(2)}) async-start(bf16[8,160,256]{2,1,0:T(8,128)(2,1)} %get-tuple-element.87), calls=%async_computation.4 | async-start | bytes 1310720 | tf_op jit(solution)/shard_map/all_to_all | solution.py:581
  421.7 23.4 %collective-permute-start.2 = (bf16[1,272,256]{2,1,0:T(8,128)(2,1)S(1)}, bf16[1,272,256]{2,1,0:T(8,128)(2,1)S(1)}, u32[]{:S(2)}, u32[]{:S(2)}) collective-permute-start(bf16[1,272,256]{2,1,0:T(8,128)(2,1)S(1)} %copy-done.9), channel_id=1, source_target_pairs={{0,16},{4,20},{8,24},{12,28},{16,0},{20,4},{24,8},{28,12},{1,17},{... | collective-permute-start | bytes 417800 | tf_op jit(solution)/shard_map/ppermute | solution.py:507
  447.5 0.9 copy-start.3
  (2 other events, 1.4 us)

commit v5 on v4

--- a/solution.py
+++ b/solution.py
@@ -667,12 +667,13 @@
         sums = (first_sum,)
         firsts.append(first_grad)
         gates.append(gate_grad)
-    parts = exchange(first_sum)
+    last_got = weights.send()
+    parts = exchange(hold(first_sum, (last_got,)))
     grad_signal = signal_grad(
         factor_sorted, firsts, gates, tuple(k * size for k in range(pieces)), slab, ctx
     )
     grad_up, grad_down, grad_gain = finish_weights(
-        weights.halves, weights.send(), weights.mine,
+        weights.halves, last_got, weights.mine,
         ((gain_width, hidden), (hidden // ctx, width), (1, gain_width)), scale, (grad_signal,),
     )
     grad_first, *rest = block_total(parts, pieces, ctx, scale, (grad_signal, grad_gain))

time: 452 us -> 447 us (0.989)
    ppermute x3, waiting for transfers between devices: 67.9 us -> 59.1 us  [send(): lax.ppermute(self.give, 'ctx', [(i, i ^ bit) for i in range(self.ctx)])]
  transfers between devices with their start and end apart: 8 -> 8, of which waited for: 7 -> 7; matrix products, arithmetic and copies ran while one was open for 3% -> 3% of each run, Pallas kernels for 39% -> 42%
where the time goes in v5:
time: 447 us; the launch traced here: 446 us
  Pallas kernels  200 us (45%)
  waiting for transfers between devices  166 us (37%)
  starting transfers between devices  33.6 us (8%)
  blocking collectives  25.9 us (6%)
  local copies, waits for them, and re-layouts  17.6 us (4%)
    pallas_call x14, Pallas kernels, call(): pl.pallas_call(ordered, out_shape=out_shape, in_specs=[*in_specs, *[pl.Bl...  192 us
    all_to_all x5, waiting for transfers between devices, exchange(): return lax.all_to_all(block, 'ctx', split_axis=0, concat_axis=0, tiled=True)  106 us
    ppermute x3, waiting for transfers between devices, send(): lax.ppermute(self.give, 'ctx', [(i, i ^ bit) for i in range(self.ctx)])  59.1 us
    all_to_all x5, starting transfers between devices, exchange(): return lax.all_to_all(block, 'ctx', split_axis=0, concat_axis=0, tiled=True)  26.1 us
    all_gather x4, blocking collectives, from_groups(): return lax.all_gather(partial_value, 'ch')  25.9 us
  transfers between devices with their start and end apart: 8, of which 7 were waited for; matrix products, arithmetic and copies ran while one was open for 3% of the time, Pallas kernels for 42%

profile of v5, /device:TPU:0, one launch (start us, length us, event | category | flops | bytes accessed | tf_op | source)
XLA Modules:
  0.0 445.6 jit_solution(6590259980689024455)
XLA Ops:
  2.7 10.1 %first_mix.3 = (bf16[256,32,256]{2,1,0:T(8,128)(2,1)}, bf16[32,256,256]{2,1,0:T(8,128)(2,1)}) custom-call(bf16[32,512,256]{2,1,0:T(8,128)(2,1)} %refs_1_.3, bf16[256,512]{1,0:T(8,128)(2,1)} %bitcast.74), custom_call_target="tpu_custom_call" | custom-call | flops 2147483648 | bytes 16777216 | tf_op jit(solution)/shard_map/first_mix/pallas_call | solution.py:44
  12.8 7.3 %all-to-all-start.1 = ((bf16[256,32,256]{2,1,0:T(8,128)(2,1)}), bf16[256,32,256]{2,1,0:T(8,128)(2,1)}, u32[]{:S(2)}, u32[]{:S(2)}) async-start(bf16[256,32,256]{2,1,0:T(8,128)(2,1)} %get-tuple-element.51), calls=%async_computation.1 | async-start | bytes 8388608 | tf_op jit(solution)/shard_map/all_to_all | solution.py:581
  20.1 9.9 %first_mix.2 = (bf16[256,32,256]{2,1,0:T(8,128)(2,1)}, bf16[32,256,256]{2,1,0:T(8,128)(2,1)}) custom-call(bf16[32,512,256]{2,1,0:T(8,128)(2,1)} %refs_1_.3, bf16[256,512]{1,0:T(8,128)(2,1)} %bitcast.72), custom_call_target="tpu_custom_call" | custom-call | flops 2147483648 | bytes 16777216 | tf_op jit(solution)/shard_map/first_mix/pallas_call | solution.py:44
  30.0 83.4 %all-to-all-done.1 = bf16[256,32,256]{2,1,0:T(8,128)(2,1)} async-done(((bf16[256,32,256]{2,1,0:T(8,128)(2,1)}), bf16[256,32,256]{2,1,0:T(8,128)(2,1)}, u32[]{:S(2)}, u32[]{:S(2)}) %all-to-all-start.1) | async-done | bytes 4194336 | tf_op jit(solution)/shard_map/all_to_all | solution.py:581
  113.4 4.7 %all-to-all-start = ((bf16[256,32,256]{2,1,0:T(8,128)(2,1)}), bf16[256,32,256]{2,1,0:T(8,128)(2,1)}, u32[]{:S(2)}, u32[]{:S(2)}) async-start(bf16[256,32,256]{2,1,0:T(8,128)(2,1)} %get-tuple-element.50), calls=%async_computation | async-start | bytes 8388608 | tf_op jit(solution)/shard_map/all_to_all | solution.py:581
  120.9 5.5 %squares.2 = f32[16,2,256]{2,1,0:T(2,128)} custom-call(bf16[8,32,32,256]{3,2,1,0:T(8,128)(2,1)} %bitcast.9.refs_0_, bf16[256,256]{1,0:T(8,128)(2,1)} %bitcast.63), custom_call_target="tpu_custom_call" | custom-call | flops 1073741824 | bytes 4194304 | tf_op jit(solution)/shard_map/squares/pallas_call | solution.py:44
  126.4 7.1 %all-gather = f32[64,2,256]{2,1,0:T(2,128)} all-gather(f32[16,2,256]{2,1,0:T(2,128)} %squares.2), channel_id=2, replica_groups=mesh['ctx'=8,'ch'=4] {'ch'}, dimensions={0}, use_global_device_ids=true | all-gather | bytes 163840 | tf_op jit(solution)/shard_map/all_gather | solution.py:577
  136.2 25.2 %mlp.4 = (bf16[64,256,256]{2,1,0:T(8,128)(2,1)}, bf16[64,256,256]{2,1,0:T(8,128)(2,1)}, f32[8,2,256]{2,1,0:T(2,128)}, f32[256,1024]{1,0:T(8,128)}, f32[256,1024]{1,0:T(8,128)}, /*index=5*/f32[1,256]{1,0:T(1,128)}) custom-call(bf16[8,32,32,256]{3,2,1,0:T(8,128)(2,1)} %bitcast.9.refs_0_, ...), custom_call_target="tpu_custom_call", output_to_operand_aliasing={{3}: (9, {}), {4}: (10, {}), {5}: (11, {})} | custom-call | flops 12884901888 | bytes 8388608 | tf_op jit(solution)/shard_map/mlp/pallas_call | solution.py:44
  161.5 25.3 %mlp.5 = (bf16[64,256,256]{2,1,0:T(8,128)(2,1)}, bf16[64,256,256]{2,1,0:T(8,128)(2,1)}, f32[8,2,256]{2,1,0:T(2,128)}, f32[256,1024]{1,0:T(8,128)}, f32[256,1024]{1,0:T(8,128)}, /*index=5*/f32[1,256]{1,0:T(1,128)}) custom-call(bf16[8,32,32,256]{3,2,1,0:T(8,128)(2,1)} %bitcast.9.refs_0_,, ...), custom_call_target="tpu_custom_call", output_to_operand_aliasing={{3}: (9, {}), {4}: (10, {}), {5}: (11, {}), {0}: (12, {}), ... | custom-call | flops 12884901888 | bytes 8388608 | tf_op jit(solution)/shard_map/mlp/pallas_call | solution.py:44
  187.5 5.9 %all-gather.1 = f32[64,2,256]{2,1,0:T(2,128)} all-gather(f32[16,2,256]{2,1,0:T(2,128)S(1)} %pad_maximum_fusion.2), channel_id=3, replica_groups=mesh['ctx'=8,'ch'=4] {'ch'}, dimensions={0}, use_global_device_ids=true | all-gather | bytes 163840 | tf_op jit(solution)/shard_map/all_gather | solution.py:577
  194.1 12.4 %second.2 = (bf16[8,32,32,256]{3,2,1,0:T(8,128)(2,1)}, f32[256,256]{1,0:T(8,128)}) custom-call(bf16[8,32,32,256]{3,2,1,0:T(8,128)(2,1)} %bitcast.9.refs_0_, bf16[256,256]{1,0:T(8,128)(2,1)} %bitcast.77, bf16[256,256]{1,0:T(8,128)(2,1)} %bitcast.66, f32[4,16,2,256]{3,2,1,0:T(2,128)} %bitcast.84, ...), custom_call_target="tpu_custom_call", output_to_operand_aliasing={{1}: (7, {})} | custom-call | flops 3221225472 | bytes 16777216 | tf_op jit(solution)/shard_map/second/pallas_call | solution.py:44
  210.7 4.6 %all-to-all-start.2 = ((bf16[256,32,256]{2,1,0:T(8,128)(2,1)}), bf16[256,32,256]{2,1,0:T(8,128)(2,1)}, u32[]{:S(2)}, u32[]{:S(2)}) async-start(bf16[256,32,256]{2,1,0:T(8,128)(2,1)} %bitcast.57), calls=%async_computation.2 | async-start | bytes 8388608 | tf_op jit(solution)/shard_map/all_to_all | solution.py:581
  215.3 5.5 %squares.3 = f32[16,2,256]{2,1,0:T(2,128)} custom-call(bf16[8,32,32,256]{3,2,1,0:T(8,128)(2,1)} %bitcast.3.refs_0_, bf16[256,256]{1,0:T(8,128)(2,1)} %bitcast.67, bf16[8,32,32,256]{3,2,1,0:T(8,128)(2,1)} %get-tuple-element.60.refs_2_), custom_call_target="tpu_custom_call" | custom-call | flops 1073741824 | bytes 4194304 | tf_op jit(solution)/shard_map/squares/pallas_call | solution.py:44
  220.8 7.1 %all-gather.2 = f32[64,2,256]{2,1,0:T(2,128)} all-gather(f32[16,2,256]{2,1,0:T(2,128)} %squares.3), channel_id=4, replica_groups=mesh['ctx'=8,'ch'=4] {'ch'}, dimensions={0}, use_global_device_ids=true | all-gather | bytes 163840 | tf_op jit(solution)/shard_map/all_gather | solution.py:577
  227.9 25.3 %mlp.6 = (bf16[64,256,256]{2,1,0:T(8,128)(2,1)}, bf16[64,256,256]{2,1,0:T(8,128)(2,1)}, f32[8,2,256]{2,1,0:T(2,128)}, f32[256,1024]{1,0:T(8,128)}, f32[256,1024]{1,0:T(8,128)}, /*index=5*/f32[1,256]{1,0:T(1,128)}) custom-call(bf16[8,32,32,256]{3,2,1,0:T(8,128)(2,1)} %bitcast.3.refs_0_,, ...), custom_call_target="tpu_custom_call", output_to_operand_aliasing={{3}: (9, {}), {4}: (10, {}), {5}: (11, {}), {0}: (12, {}), ... | custom-call | flops 12884901888 | bytes 8388608 | tf_op jit(solution)/shard_map/mlp/pallas_call | solution.py:44
  253.2 25.4 %mlp.7 = (bf16[64,256,256]{2,1,0:T(8,128)(2,1)}, bf16[64,256,256]{2,1,0:T(8,128)(2,1)}, f32[8,2,256]{2,1,0:T(2,128)}, f32[256,1024]{1,0:T(8,128)}, f32[256,1024]{1,0:T(8,128)}, /*index=5*/f32[1,256]{1,0:T(1,128)}) custom-call(bf16[8,32,32,256]{3,2,1,0:T(8,128)(2,1)} %bitcast.3.refs_0_,, ...), custom_call_target="tpu_custom_call", output_to_operand_aliasing={{3}: (9, {}), {4}: (10, {}), {5}: (11, {}), {0}: (12, {}), ... | custom-call | flops 12884901888 | bytes 8388608 | tf_op jit(solution)/shard_map/mlp/pallas_call | solution.py:44
  284.6 5.9 %all-gather.3 = f32[64,2,256]{2,1,0:T(2,128)} all-gather(f32[16,2,256]{2,1,0:T(2,128)S(1)} %pad_maximum_fusion.3), channel_id=5, replica_groups=mesh['ctx'=8,'ch'=4] {'ch'}, dimensions={0}, use_global_device_ids=true | all-gather | bytes 163840 | tf_op jit(solution)/shard_map/all_gather | solution.py:577
  290.4 12.5 %second.3 = (bf16[8,32,32,256]{3,2,1,0:T(8,128)(2,1)}, f32[256,256]{1,0:T(8,128)}) custom-call(bf16[8,32,32,256]{3,2,1,0:T(8,128)(2,1)} %bitcast.3.refs_0_, bf16[256,256]{1,0:T(8,128)(2,1)} %bitcast.78, bf16[256,256]{1,0:T(8,128)(2,1)} %bitcast.70, f32[4,16,2,256]{3,2,1,0:T(2,128)} %bitcast.81, ...), custom_call_target="tpu_custom_call", output_to_operand_aliasing={{1}: (7, {})} | custom-call | flops 3221225472 | bytes 16777216 | tf_op jit(solution)/shard_map/second/pallas_call | solution.py:44
  307.8 5.9 %all-to-all-start.3 = ((bf16[256,32,256]{2,1,0:T(8,128)(2,1)}), bf16[256,32,256]{2,1,0:T(8,128)(2,1)}, u32[]{:S(2)}, u32[]{:S(2)}) async-start(bf16[256,32,256]{2,1,0:T(8,128)(2,1)} %bitcast.56), calls=%async_computation.3 | async-start | bytes 8388608 | tf_op jit(solution)/shard_map/all_to_all | solution.py:581
  322.5 10.7 %gate.2 = (bf16[32,256,256]{2,1,0:T(8,128)(2,1)}, bf16[32,256,256]{2,1,0:T(8,128)(2,1)}, bf16[8,160,256]{2,1,0:T(8,128)(2,1)}) custom-call(bf16[256,32,256]{2,1,0:T(8,128)(2,1)} %all-to-all-done.2.refs_0_, bf16[32,512,256]{2,1,0:T(8,128)(2,1)} %refs_1_.3, bf16[32,256,256]{2,1,0:T(8,128)(2,1)} %get-tuple-element.71.refs_2_, ...), custom_call_target="tpu_custom_call", output_to_operand_aliasing={{2}: (3, {})} | custom-call | flops 2147483648 | bytes 25165824 | tf_op jit(solution)/shard_map/gate/pallas_call | solution.py:44
  333.3 55.5 %collective-permute-done.1.got_ref = bf16[2,272,256]{2,1,0:T(8,128)(2,1)S(1)} collective-permute-done((bf16[2,272,256]{2,1,0:T(8,128)(2,1)S(1)}, bf16[2,272,256]{2,1,0:T(8,128)(2,1)S(1)}, u32[]{:S(2)}, u32[]{:S(2)}) %collective-permute-start.1) | collective-permute-done | bytes 278560 | tf_op jit(solution)/shard_map/ppermute | solution.py:507
  395.9 15.6 %all-to-all-done.3.refs_0_ = bf16[256,32,256]{2,1,0:T(8,128)(2,1)} async-done(((bf16[256,32,256]{2,1,0:T(8,128)(2,1)}), bf16[256,32,256]{2,1,0:T(8,128)(2,1)}, u32[]{:S(2)}, u32[]{:S(2)}) %all-to-all-start.3) | async-done | bytes 4194336 | tf_op jit(solution)/shard_map/all_to_all | solution.py:581
  411.4 10.8 %gate.3 = (bf16[32,256,256]{2,1,0:T(8,128)(2,1)}, bf16[32,256,256]{2,1,0:T(8,128)(2,1)}, bf16[8,160,256]{2,1,0:T(8,128)(2,1)}) custom-call(bf16[256,32,256]{2,1,0:T(8,128)(2,1)} %all-to-all-done.3.refs_0_, bf16[32,512,256]{2,1,0:T(8,128)(2,1)} %refs_1_.3, bf16[32,256,256]{2,1,0:T(8,128)(2,1)} %get-tuple-element.82.refs_2_, ...), custom_call_target="tpu_custom_call", output_to_operand_aliasing={{2}: (3, {})} | custom-call | flops 2147483648 | bytes 25165824 | tf_op jit(solution)/shard_map/gate/pallas_call | solution.py:44
  426.4 11.8 %signal_grad.1.refs_0_.refs_1_ = bf16[32,512,256]{2,1,0:T(8,128)(2,1)} custom-call(bf16[512,512]{1,0:T(8,128)(2,1)} %pad_maximum_fusion.1.refs_5_.refs_0_, bf16[32,256,256]{2,1,0:T(8,128)(2,1)} %get-tuple-element.80.refs_0_.refs_1_, bf16[32,256,256]{2,1,0:T(8,128)(2,1)} %get-tuple-element.84.refs_2_, bf16[32,256,256]{2,1,0:T(8,128)(2,1)} %get-tuple-element.85.refs_3_, ...), custom_call_target="tpu_custom_call" | custom-call | flops 4294967296 | bytes 25165824 | tf_op jit(solution)/shard_map/signal_grad/pallas_call | solution.py:44
  (78 shorter events, 51.3 us)
Async XLA Ops:
  12.8 100.6 %all-to-all-start.1 = ((bf16[256,32,256]{2,1,0:T(8,128)(2,1)}), bf16[256,32,256]{2,1,0:T(8,128)(2,1)}, u32[]{:S(2)}, u32[]{:S(2)}) async-start(bf16[256,32,256]{2,1,0:T(8,128)(2,1)} %get-tuple-element.51), calls=%async_computation.1 | async-start | bytes 8388608 | tf_op jit(solution)/shard_map/all_to_all | solution.py:581
  113.4 4.7 %copy-start.8 = (bf16[1,256,256]{2,1,0:T(8,128)(2,1)S(1)}, bf16[1,256,256]{2,1,0:T(8,128)(2,1)}, u32[]{:S(2)}) copy-start(bf16[1,256,256]{2,1,0:T(8,128)(2,1)} %param.9) | copy-start | bytes 393220
  113.4 5.5 %copy-start.11 = (bf16[1,256,1024]{2,1,0:T(8,128)(2,1)S(1)}, bf16[1,256,1024]{2,1,0:T(8,128)(2,1)}, u32[]{:S(2)}) copy-start(bf16[1,256,1024]{2,1,0:T(8,128)(2,1)} %param.10) | copy-start | bytes 1572868
  113.4 6.5 %copy-start.12 = (bf16[1,1024,256]{2,1,0:T(8,128)(2,1)S(1)}, bf16[1,1024,256]{2,1,0:T(8,128)(2,1)}, u32[]{:S(2)}) copy-start(bf16[1,1024,256]{2,1,0:T(8,128)(2,1)} %param.11) | copy-start | bytes 1572868
  113.4 97.2 %all-to-all-start = ((bf16[256,32,256]{2,1,0:T(8,128)(2,1)}), bf16[256,32,256]{2,1,0:T(8,128)(2,1)}, u32[]{:S(2)}, u32[]{:S(2)}) async-start(bf16[256,32,256]{2,1,0:T(8,128)(2,1)} %get-tuple-element.50), calls=%async_computation | async-start | bytes 8388608 | tf_op jit(solution)/shard_map/all_to_all | solution.py:581
  161.5 25.3 %copy-start.16 = (f32[8,2,256]{2,1,0:T(2,128)S(1)}, f32[8,2,256]{2,1,0:T(2,128)}, u32[]{:S(2)}) copy-start(f32[8,2,256]{2,1,0:T(2,128)} %get-tuple-element.52) | copy-start | bytes 49156
  210.7 97.2 %all-to-all-start.2 = ((bf16[256,32,256]{2,1,0:T(8,128)(2,1)}), bf16[256,32,256]{2,1,0:T(8,128)(2,1)}, u32[]{:S(2)}, u32[]{:S(2)}) async-start(bf16[256,32,256]{2,1,0:T(8,128)(2,1)} %bitcast.57), calls=%async_computation.2 | async-start | bytes 8388608 | tf_op jit(solution)/shard_map/all_to_all | solution.py:581
  278.6 2.0 copy-start.2
  278.6 2.9 copy-start.17
  280.6 3.9 copy-start.14
  280.6 3.9 copy-start.15
  282.5 20.5 %copy-start = (f32[4,2,272,256]{3,2,1,0:T(8,128)}, f32[4,2,272,256]{3,2,1,0:T(8,128)S(1)}, u32[]{:S(2)}) copy-start(f32[4,2,272,256]{3,2,1,0:T(8,128)S(1)} %pad_maximum_fusion.values_ref) | copy-start | bytes 6684676
  282.6 7.8 %copy-start.7 = (bf16[4,272,256]{2,1,0:T(8,128)(2,1)}, bf16[4,272,256]{2,1,0:T(8,128)(2,1)S(1)}, u32[]{:S(2)}) copy-start(bf16[4,272,256]{2,1,0:T(8,128)(2,1)S(1)} %fusion.refs_8_) | copy-start | bytes 1671172
  282.6 24.0 %collective-permute-start = (bf16[4,272,256]{2,1,0:T(8,128)(2,1)S(1)}, bf16[4,272,256]{2,1,0:T(8,128)(2,1)S(1)}, u32[]{:S(2)}, u32[]{:S(2)}) collective-permute-start(bf16[4,272,256]{2,1,0:T(8,128)(2,1)S(1)} %fusion.refs_8_), channel_id=1, source_target_pairs={{0,4},{4,0},{8,12},{12,8},{16,20},{20,16},{24,28},{28,24},{1,5},{5... | collective-permute-start | bytes 1671176 | tf_op jit(solution)/shard_map/ppermute | solution.py:507
  306.6 0.8 copy-start.6
  307.8 6.0 %copy-start.5 = (bf16[512,8,1,32]{0,3,2,1:T(8,128)(2,1)S(1)}, bf16[512,8,1,32]{0,3,2,1:T(8,128)(2,1)}, u32[]{:S(2)}) copy-start(bf16[512,8,1,32]{0,3,2,1:T(8,128)(2,1)} %get-tuple-element.93) | copy-start | bytes 786436
  307.8 6.1 %copy-start.4 = (bf16[512,8,1,32]{0,3,2,1:T(8,128)(2,1)S(1)}, bf16[512,8,1,32]{0,3,2,1:T(8,128)(2,1)}, u32[]{:S(2)}) copy-start(bf16[512,8,1,32]{0,3,2,1:T(8,128)(2,1)} %get-tuple-element.94) | copy-start | bytes 786436
  307.8 103.6 %all-to-all-start.3 = ((bf16[256,32,256]{2,1,0:T(8,128)(2,1)}), bf16[256,32,256]{2,1,0:T(8,128)(2,1)}, u32[]{:S(2)}, u32[]{:S(2)}) async-start(bf16[256,32,256]{2,1,0:T(8,128)(2,1)} %bitcast.56), calls=%async_computation.3 | async-start | bytes 8388608 | tf_op jit(solution)/shard_map/all_to_all | solution.py:581
  314.1 7.5 %copy-start.1 = (f32[256,256]{1,0:T(8,128)S(1)}, f32[256,256]{1,0:T(8,128)}, u32[]{:S(2)}) copy-start(f32[256,256]{1,0:T(8,128)} %get-tuple-element.79) | copy-start | bytes 786436
  318.7 70.0 %collective-permute-start.1 = (bf16[2,272,256]{2,1,0:T(8,128)(2,1)S(1)}, bf16[2,272,256]{2,1,0:T(8,128)(2,1)S(1)}, u32[]{:S(2)}, u32[]{:S(2)}) collective-permute-start(bf16[2,272,256]{2,1,0:T(8,128)(2,1)S(1)} %fusion.1), channel_id=1, source_target_pairs={{0,8},{4,12},{8,0},{12,4},{16,24},{20,28},{24,16},{28,20},{1,9},{5... | collective-permute-start | bytes 835592 | tf_op jit(solution)/shard_map/ppermute | solution.py:507
  392.3 19.1 %copy-start.10 = (bf16[1,272,256]{2,1,0:T(8,128)(2,1)}, bf16[1,272,256]{2,1,0:T(8,128)(2,1)S(1)}, u32[]{:S(2)}) copy-start(bf16[1,272,256]{2,1,0:T(8,128)(2,1)S(1)} %dynamic-slice_convert_fusion.refs_4_) | copy-start | bytes 417796
  392.3 29.9 %collective-permute-start.2 = (bf16[1,272,256]{2,1,0:T(8,128)(2,1)S(1)}, bf16[1,272,256]{2,1,0:T(8,128)(2,1)S(1)}, u32[]{:S(2)}, u32[]{:S(2)}) collective-permute-start(bf16[1,272,256]{2,1,0:T(8,128)(2,1)S(1)} %dynamic-slice_convert_fusion.refs_4_), channel_id=1, source_target_pairs={{0,16},{4,20},{8,24},{12,28},{16,0},{20,4},{24,8},{28,12},{1,17},{... | collective-permute-start | bytes 417800 | tf_op jit(solution)/shard_map/ppermute | solution.py:507
  422.8 20.0 %all-to-all-start.4 = ((bf16[8,160,256]{2,1,0:T(8,128)(2,1)}), bf16[8,160,256]{2,1,0:T(8,128)(2,1)S(1)}, u32[]{:S(2)}, u32[]{:S(2)}) async-start(bf16[8,160,256]{2,1,0:T(8,128)(2,1)} %hold.3), calls=%async_computation.4 | async-start | bytes 1310720 | tf_op jit(solution)/shard_map/all_to_all | solution.py:581
  442.8 0.9 copy-start.3
  (2 other events, 1.4 us)

commit v6 on v5

--- a/solution.py
+++ b/solution.py
@@ -493,17 +493,23 @@
     def __init__(self, values, ctx, scale):
         self.ctx, self.bit, self.scale = ctx, 1, scale
         self.values = values
+        if ctx >= 4:
+            quarters = values.reshape((ctx // 4, 2, 2) + values.shape[1:])
+            self.values = jnp.swapaxes(quarters, 1, 2).reshape(values.shape)
         self.halve()
+
+    def away(self):
+        return {1: 2, 2: 1}.get(self.bit, self.bit) if self.ctx >= 4 else self.bit
 
     def halve(self):
         self.halves = self.values.reshape((-1, 2) + self.values.shape[1:])
-        self.mine = (lax.axis_index("ctx") // self.bit) % 2
+        self.mine = (lax.axis_index("ctx") // self.away()) % 2
         self.give = lax.dynamic_index_in_dim(
             self.halves, 1 - self.mine, 1, keepdims=False
         ).astype(BF16)
 
     def send(self):
-        bit = self.bit
+        bit = self.away()
         self.got = lax.ppermute(self.give, "ctx", [(i, i ^ bit) for i in range(self.ctx)])
         return self.got
 

time: 447 us -> 457 us (1.022)
  waiting for transfers between devices: 166 us -> 178 us
    all_to_all x5, waiting for transfers between devices: 106 us -> 142 us  [exchange(): return lax.all_to_all(block, 'ctx', split_axis=0, concat_axis=0, tiled=True)]
    ppermute x3, waiting for transfers between devices: 59.1 us -> 36 us  [send(): lax.ppermute(self.give, 'ctx', [(i, i ^ bit) for i in range(self.ctx)])]
  transfers between devices with their start and end apart: 8 -> 8, of which waited for: 7 -> 6; matrix products, arithmetic and copies ran while one was open for 3% -> 4% of each run, Pallas kernels for 42% -> 41%
where the time goes in v6:
time: 457 us; the launch traced here: 456 us
  Pallas kernels  200 us (44%)
  waiting for transfers between devices  178 us (39%)
  starting transfers between devices  30 us (7%)
  blocking collectives  25.9 us (6%)
  local copies, waits for them, and re-layouts  19.4 us (4%)
    pallas_call x14, Pallas kernels, call(): pl.pallas_call(ordered, out_shape=out_shape, in_specs=[*in_specs, *[pl.Bl...  193 us
    all_to_all x5, waiting for transfers between devices, exchange(): return lax.all_to_all(block, 'ctx', split_axis=0, concat_axis=0, tiled=True)  142 us
    ppermute x3, waiting for transfers between devices, send(): lax.ppermute(self.give, 'ctx', [(i, i ^ bit) for i in range(self.ctx)])  36 us
    all_gather x4, blocking collectives, from_groups(): return lax.all_gather(partial_value, 'ch')  25.9 us
    all_to_all x5, starting transfers between devices, exchange(): return lax.all_to_all(block, 'ctx', split_axis=0, concat_axis=0, tiled=True)  25.1 us
  transfers between devices with their start and end apart: 8, of which 6 were waited for; matrix products, arithmetic and copies ran while one was open for 4% of the time, Pallas kernels for 41%

profile of v6, /device:TPU:0, one launch (start us, length us, event | category | flops | bytes accessed | tf_op | source)
XLA Modules:
  0.0 456.1 jit_solution(3630515001546072277)
XLA Ops:
  2.7 10.1 %first_mix.3 = (bf16[256,32,256]{2,1,0:T(8,128)(2,1)}, bf16[32,256,256]{2,1,0:T(8,128)(2,1)}) custom-call(bf16[32,512,256]{2,1,0:T(8,128)(2,1)} %refs_1_.3, bf16[256,512]{1,0:T(8,128)(2,1)} %bitcast.75), custom_call_target="tpu_custom_call" | custom-call | flops 2147483648 | bytes 16777216 | tf_op jit(solution)/shard_map/first_mix/pallas_call | solution.py:44
  12.8 7.3 %all-to-all-start.1 = ((bf16[256,32,256]{2,1,0:T(8,128)(2,1)}), bf16[256,32,256]{2,1,0:T(8,128)(2,1)}, u32[]{:S(2)}, u32[]{:S(2)}) async-start(bf16[256,32,256]{2,1,0:T(8,128)(2,1)} %get-tuple-element.51), calls=%async_computation.1 | async-start | bytes 8388608 | tf_op jit(solution)/shard_map/all_to_all | solution.py:587
  20.1 9.9 %first_mix.2 = (bf16[256,32,256]{2,1,0:T(8,128)(2,1)}, bf16[32,256,256]{2,1,0:T(8,128)(2,1)}) custom-call(bf16[32,512,256]{2,1,0:T(8,128)(2,1)} %refs_1_.3, bf16[256,512]{1,0:T(8,128)(2,1)} %bitcast.73), custom_call_target="tpu_custom_call" | custom-call | flops 2147483648 | bytes 16777216 | tf_op jit(solution)/shard_map/first_mix/pallas_call | solution.py:44
  30.0 83.4 %all-to-all-done.1 = bf16[256,32,256]{2,1,0:T(8,128)(2,1)} async-done(((bf16[256,32,256]{2,1,0:T(8,128)(2,1)}), bf16[256,32,256]{2,1,0:T(8,128)(2,1)}, u32[]{:S(2)}, u32[]{:S(2)}) %all-to-all-start.1) | async-done | bytes 4194336 | tf_op jit(solution)/shard_map/all_to_all | solution.py:587
  113.4 4.7 %all-to-all-start = ((bf16[256,32,256]{2,1,0:T(8,128)(2,1)}), bf16[256,32,256]{2,1,0:T(8,128)(2,1)}, u32[]{:S(2)}, u32[]{:S(2)}) async-start(bf16[256,32,256]{2,1,0:T(8,128)(2,1)} %get-tuple-element.50), calls=%async_computation | async-start | bytes 8388608 | tf_op jit(solution)/shard_map/all_to_all | solution.py:587
  120.9 5.5 %squares.2 = f32[16,2,256]{2,1,0:T(2,128)} custom-call(bf16[8,32,32,256]{3,2,1,0:T(8,128)(2,1)} %bitcast.9.refs_0_, bf16[256,256]{1,0:T(8,128)(2,1)} %bitcast.64), custom_call_target="tpu_custom_call" | custom-call | flops 1073741824 | bytes 4194304 | tf_op jit(solution)/shard_map/squares/pallas_call | solution.py:44
  126.4 7.1 %all-gather = f32[64,2,256]{2,1,0:T(2,128)} all-gather(f32[16,2,256]{2,1,0:T(2,128)} %squares.2), channel_id=2, replica_groups=mesh['ctx'=8,'ch'=4] {'ch'}, dimensions={0}, use_global_device_ids=true | all-gather | bytes 163840 | tf_op jit(solution)/shard_map/all_gather | solution.py:583
  136.3 25.3 %mlp.4 = (bf16[64,256,256]{2,1,0:T(8,128)(2,1)}, bf16[64,256,256]{2,1,0:T(8,128)(2,1)}, f32[8,2,256]{2,1,0:T(2,128)}, f32[256,1024]{1,0:T(8,128)}, f32[256,1024]{1,0:T(8,128)}, /*index=5*/f32[1,256]{1,0:T(1,128)}) custom-call(bf16[8,32,32,256]{3,2,1,0:T(8,128)(2,1)} %bitcast.9.refs_0_, ...), custom_call_target="tpu_custom_call", output_to_operand_aliasing={{3}: (9, {}), {4}: (10, {}), {5}: (11, {})} | custom-call | flops 12884901888 | bytes 8388608 | tf_op jit(solution)/shard_map/mlp/pallas_call | solution.py:44
  161.6 25.3 %mlp.5 = (bf16[64,256,256]{2,1,0:T(8,128)(2,1)}, bf16[64,256,256]{2,1,0:T(8,128)(2,1)}, f32[8,2,256]{2,1,0:T(2,128)}, f32[256,1024]{1,0:T(8,128)}, f32[256,1024]{1,0:T(8,128)}, /*index=5*/f32[1,256]{1,0:T(1,128)}) custom-call(bf16[8,32,32,256]{3,2,1,0:T(8,128)(2,1)} %bitcast.9.refs_0_,, ...), custom_call_target="tpu_custom_call", output_to_operand_aliasing={{3}: (9, {}), {4}: (10, {}), {5}: (11, {}), {0}: (12, {}), ... | custom-call | flops 12884901888 | bytes 8388608 | tf_op jit(solution)/shard_map/mlp/pallas_call | solution.py:44
  187.6 5.9 %all-gather.1 = f32[64,2,256]{2,1,0:T(2,128)} all-gather(f32[16,2,256]{2,1,0:T(2,128)S(1)} %pad_maximum_fusion.1), channel_id=3, replica_groups=mesh['ctx'=8,'ch'=4] {'ch'}, dimensions={0}, use_global_device_ids=true | all-gather | bytes 163840 | tf_op jit(solution)/shard_map/all_gather | solution.py:583
  194.2 12.4 %second.2 = (bf16[8,32,32,256]{3,2,1,0:T(8,128)(2,1)}, f32[256,256]{1,0:T(8,128)}) custom-call(bf16[8,32,32,256]{3,2,1,0:T(8,128)(2,1)} %bitcast.9.refs_0_, bf16[256,256]{1,0:T(8,128)(2,1)} %bitcast.78, bf16[256,256]{1,0:T(8,128)(2,1)} %bitcast.67, f32[4,16,2,256]{3,2,1,0:T(2,128)} %bitcast.85, ...), custom_call_target="tpu_custom_call", output_to_operand_aliasing={{1}: (7, {})} | custom-call | flops 3221225472 | bytes 16777216 | tf_op jit(solution)/shard_map/second/pallas_call | solution.py:44
  215.3 5.5 %squares.3 = f32[16,2,256]{2,1,0:T(2,128)} custom-call(bf16[8,32,32,256]{3,2,1,0:T(8,128)(2,1)} %bitcast.3.refs_0_, bf16[256,256]{1,0:T(8,128)(2,1)} %bitcast.68, bf16[8,32,32,256]{3,2,1,0:T(8,128)(2,1)} %get-tuple-element.60.refs_2_), custom_call_target="tpu_custom_call" | custom-call | flops 1073741824 | bytes 4194304 | tf_op jit(solution)/shard_map/squares/pallas_call | solution.py:44
  220.8 7.1 %all-gather.2 = f32[64,2,256]{2,1,0:T(2,128)} all-gather(f32[16,2,256]{2,1,0:T(2,128)} %squares.3), channel_id=4, replica_groups=mesh['ctx'=8,'ch'=4] {'ch'}, dimensions={0}, use_global_device_ids=true | all-gather | bytes 163840 | tf_op jit(solution)/shard_map/all_gather | solution.py:583
  227.9 25.3 %mlp.6 = (bf16[64,256,256]{2,1,0:T(8,128)(2,1)}, bf16[64,256,256]{2,1,0:T(8,128)(2,1)}, f32[8,2,256]{2,1,0:T(2,128)}, f32[256,1024]{1,0:T(8,128)}, f32[256,1024]{1,0:T(8,128)}, /*index=5*/f32[1,256]{1,0:T(1,128)}) custom-call(bf16[8,32,32,256]{3,2,1,0:T(8,128)(2,1)} %bitcast.3.refs_0_,, ...), custom_call_target="tpu_custom_call", output_to_operand_aliasing={{3}: (9, {}), {4}: (10, {}), {5}: (11, {}), {0}: (12, {}), ... | custom-call | flops 12884901888 | bytes 8388608 | tf_op jit(solution)/shard_map/mlp/pallas_call | solution.py:44
  253.2 25.4 %mlp.7 = (bf16[64,256,256]{2,1,0:T(8,128)(2,1)}, bf16[64,256,256]{2,1,0:T(8,128)(2,1)}, f32[8,2,256]{2,1,0:T(2,128)}, f32[256,1024]{1,0:T(8,128)}, f32[256,1024]{1,0:T(8,128)}, /*index=5*/f32[1,256]{1,0:T(1,128)}) custom-call(bf16[8,32,32,256]{3,2,1,0:T(8,128)(2,1)} %bitcast.3.refs_0_,, ...), custom_call_target="tpu_custom_call", output_to_operand_aliasing={{3}: (9, {}), {4}: (10, {}), {5}: (11, {}), {0}: (12, {}), ... | custom-call | flops 12884901888 | bytes 8388608 | tf_op jit(solution)/shard_map/mlp/pallas_call | solution.py:44
  284.8 5.9 %all-gather.3 = f32[64,2,256]{2,1,0:T(2,128)} all-gather(f32[16,2,256]{2,1,0:T(2,128)S(1)} %pad_maximum_fusion.2), channel_id=5, replica_groups=mesh['ctx'=8,'ch'=4] {'ch'}, dimensions={0}, use_global_device_ids=true | all-gather | bytes 163840 | tf_op jit(solution)/shard_map/all_gather | solution.py:583
  290.6 12.5 %second.3 = (bf16[8,32,32,256]{3,2,1,0:T(8,128)(2,1)}, f32[256,256]{1,0:T(8,128)}) custom-call(bf16[8,32,32,256]{3,2,1,0:T(8,128)(2,1)} %bitcast.3.refs_0_, bf16[256,256]{1,0:T(8,128)(2,1)} %bitcast.79, bf16[256,256]{1,0:T(8,128)(2,1)} %bitcast.71, f32[4,16,2,256]{3,2,1,0:T(2,128)} %bitcast.82, ...), custom_call_target="tpu_custom_call", output_to_operand_aliasing={{1}: (7, {})} | custom-call | flops 3221225472 | bytes 16777216 | tf_op jit(solution)/shard_map/second/pallas_call | solution.py:44
  303.1 15.6 %collective-permute-done.refs_1_.got_ref = bf16[4,272,256]{2,1,0:T(8,128)(2,1)S(1)} collective-permute-done((bf16[4,272,256]{2,1,0:T(8,128)(2,1)S(1)}, bf16[4,272,256]{2,1,0:T(8,128)(2,1)S(1)}, u32[]{:S(2)}, u32[]{:S(2)}) %collective-permute-start) | collective-permute-done | bytes 557088 | tf_op jit(solution)/shard_map/ppermute | solution.py:513
  319.6 5.0 %all-to-all-start.3 = ((bf16[256,32,256]{2,1,0:T(8,128)(2,1)}), bf16[256,32,256]{2,1,0:T(8,128)(2,1)}, u32[]{:S(2)}, u32[]{:S(2)}) async-start(bf16[256,32,256]{2,1,0:T(8,128)(2,1)} %bitcast.55), calls=%async_computation.3 | async-start | bytes 8388608 | tf_op jit(solution)/shard_map/all_to_all | solution.py:587
  334.6 10.8 %gate.2 = (bf16[32,256,256]{2,1,0:T(8,128)(2,1)}, bf16[32,256,256]{2,1,0:T(8,128)(2,1)}, bf16[8,160,256]{2,1,0:T(8,128)(2,1)}) custom-call(bf16[256,32,256]{2,1,0:T(8,128)(2,1)} %all-to-all-done.2.refs_0_, bf16[32,512,256]{2,1,0:T(8,128)(2,1)} %refs_1_.3, bf16[32,256,256]{2,1,0:T(8,128)(2,1)} %get-tuple-element.71.refs_2_, ...), custom_call_target="tpu_custom_call", output_to_operand_aliasing={{2}: (3, {})} | custom-call | flops 2147483648 | bytes 25165824 | tf_op jit(solution)/shard_map/gate/pallas_call | solution.py:44
  345.4 20.4 %collective-permute-done.1.got_ref = bf16[2,272,256]{2,1,0:T(8,128)(2,1)S(1)} collective-permute-done((bf16[2,272,256]{2,1,0:T(8,128)(2,1)S(1)}, bf16[2,272,256]{2,1,0:T(8,128)(2,1)S(1)}, u32[]{:S(2)}, u32[]{:S(2)}) %collective-permute-start.1) | collective-permute-done | bytes 278560 | tf_op jit(solution)/shard_map/ppermute | solution.py:513
  370.6 51.3 %all-to-all-done.3.refs_0_ = bf16[256,32,256]{2,1,0:T(8,128)(2,1)} async-done(((bf16[256,32,256]{2,1,0:T(8,128)(2,1)}), bf16[256,32,256]{2,1,0:T(8,128)(2,1)}, u32[]{:S(2)}, u32[]{:S(2)}) %all-to-all-start.3) | async-done | bytes 4194336 | tf_op jit(solution)/shard_map/all_to_all | solution.py:587
  421.9 10.7 %gate.3 = (bf16[32,256,256]{2,1,0:T(8,128)(2,1)}, bf16[32,256,256]{2,1,0:T(8,128)(2,1)}, bf16[8,160,256]{2,1,0:T(8,128)(2,1)}) custom-call(bf16[256,32,256]{2,1,0:T(8,128)(2,1)} %all-to-all-done.3.refs_0_, bf16[32,512,256]{2,1,0:T(8,128)(2,1)} %refs_1_.3, bf16[32,256,256]{2,1,0:T(8,128)(2,1)} %get-tuple-element.82.refs_2_, ...), custom_call_target="tpu_custom_call", output_to_operand_aliasing={{2}: (3, {})} | custom-call | flops 2147483648 | bytes 25165824 | tf_op jit(solution)/shard_map/gate/pallas_call | solution.py:44
  436.8 11.8 %signal_grad.1.refs_0_.refs_1_ = bf16[32,512,256]{2,1,0:T(8,128)(2,1)} custom-call(bf16[512,512]{1,0:T(8,128)(2,1)} %pad_maximum_fusion.refs_5_.refs_0_, bf16[32,256,256]{2,1,0:T(8,128)(2,1)} %get-tuple-element.80.refs_0_.refs_1_, bf16[32,256,256]{2,1,0:T(8,128)(2,1)} %get-tuple-element.84.refs_2_, bf16[32,256,256]{2,1,0:T(8,128)(2,1)} %get-tuple-element.85.refs_3_, ...), custom_call_target="tpu_custom_call" | custom-call | flops 4294967296 | bytes 25165824 | tf_op jit(solution)/shard_map/signal_grad/pallas_call | solution.py:44
  (78 shorter events, 50.8 us)
Async XLA Ops:
  12.8 100.6 %all-to-all-start.1 = ((bf16[256,32,256]{2,1,0:T(8,128)(2,1)}), bf16[256,32,256]{2,1,0:T(8,128)(2,1)}, u32[]{:S(2)}, u32[]{:S(2)}) async-start(bf16[256,32,256]{2,1,0:T(8,128)(2,1)} %get-tuple-element.51), calls=%async_computation.1 | async-start | bytes 8388608 | tf_op jit(solution)/shard_map/all_to_all | solution.py:587
  113.4 4.8 %copy-start.7 = (bf16[1,256,256]{2,1,0:T(8,128)(2,1)S(1)}, bf16[1,256,256]{2,1,0:T(8,128)(2,1)}, u32[]{:S(2)}) copy-start(bf16[1,256,256]{2,1,0:T(8,128)(2,1)} %param.9) | copy-start | bytes 393220
  113.4 5.5 %copy-start.10 = (bf16[1,256,1024]{2,1,0:T(8,128)(2,1)S(1)}, bf16[1,256,1024]{2,1,0:T(8,128)(2,1)}, u32[]{:S(2)}) copy-start(bf16[1,256,1024]{2,1,0:T(8,128)(2,1)} %param.10) | copy-start | bytes 1572868
  113.4 6.5 %copy-start.11 = (bf16[1,1024,256]{2,1,0:T(8,128)(2,1)S(1)}, bf16[1,1024,256]{2,1,0:T(8,128)(2,1)}, u32[]{:S(2)}) copy-start(bf16[1,1024,256]{2,1,0:T(8,128)(2,1)} %param.11) | copy-start | bytes 1572868
  113.4 97.2 %all-to-all-start = ((bf16[256,32,256]{2,1,0:T(8,128)(2,1)}), bf16[256,32,256]{2,1,0:T(8,128)(2,1)}, u32[]{:S(2)}, u32[]{:S(2)}) async-start(bf16[256,32,256]{2,1,0:T(8,128)(2,1)} %get-tuple-element.50), calls=%async_computation | async-start | bytes 8388608 | tf_op jit(solution)/shard_map/all_to_all | solution.py:587
  161.6 25.3 %copy-start.15 = (f32[8,2,256]{2,1,0:T(2,128)S(1)}, f32[8,2,256]{2,1,0:T(2,128)}, u32[]{:S(2)}) copy-start(f32[8,2,256]{2,1,0:T(2,128)} %get-tuple-element.52) | copy-start | bytes 49156
  210.6 109.0 %all-to-all-start.2 = ((bf16[256,32,256]{2,1,0:T(8,128)(2,1)}), bf16[256,32,256]{2,1,0:T(8,128)(2,1)}, u32[]{:S(2)}, u32[]{:S(2)}) async-start(bf16[256,32,256]{2,1,0:T(8,128)(2,1)} %bitcast.56), calls=%async_computation.2 | async-start | bytes 8388608 | tf_op jit(solution)/shard_map/all_to_all | solution.py:587
  278.7 2.0 copy-start.1
  278.7 2.9 copy-start.16
  282.3 2.4 copy-start.13
  282.3 2.4 copy-start.14
  282.7 7.9 %copy-start.6 = (bf16[4,272,256]{2,1,0:T(8,128)(2,1)}, bf16[4,272,256]{2,1,0:T(8,128)(2,1)S(1)}, u32[]{:S(2)}) copy-start(bf16[4,272,256]{2,1,0:T(8,128)(2,1)S(1)} %fusion.refs_8_) | copy-start | bytes 1671172
  282.7 36.0 %collective-permute-start = (bf16[4,272,256]{2,1,0:T(8,128)(2,1)S(1)}, bf16[4,272,256]{2,1,0:T(8,128)(2,1)S(1)}, u32[]{:S(2)}, u32[]{:S(2)}) collective-permute-start(bf16[4,272,256]{2,1,0:T(8,128)(2,1)S(1)} %fusion.refs_8_), channel_id=1, source_target_pairs={{0,8},{4,12},{8,0},{12,4},{16,24},{20,28},{24,16},{28,20},{1,9},{5... | collective-permute-start | bytes 1671176 | tf_op jit(solution)/shard_map/ppermute | solution.py:513
  318.8 0.8 copy-start.5
  319.6 5.1 %copy-start.4 = (bf16[512,8,1,32]{0,3,2,1:T(8,128)(2,1)S(1)}, bf16[512,8,1,32]{0,3,2,1:T(8,128)(2,1)}, u32[]{:S(2)}) copy-start(bf16[512,8,1,32]{0,3,2,1:T(8,128)(2,1)} %get-tuple-element.93) | copy-start | bytes 786436
  319.6 5.2 %copy-start.3 = (bf16[512,8,1,32]{0,3,2,1:T(8,128)(2,1)S(1)}, bf16[512,8,1,32]{0,3,2,1:T(8,128)(2,1)}, u32[]{:S(2)}) copy-start(bf16[512,8,1,32]{0,3,2,1:T(8,128)(2,1)} %get-tuple-element.94) | copy-start | bytes 786436
  319.6 102.3 %all-to-all-start.3 = ((bf16[256,32,256]{2,1,0:T(8,128)(2,1)}), bf16[256,32,256]{2,1,0:T(8,128)(2,1)}, u32[]{:S(2)}, u32[]{:S(2)}) async-start(bf16[256,32,256]{2,1,0:T(8,128)(2,1)} %bitcast.55), calls=%async_computation.3 | async-start | bytes 8388608 | tf_op jit(solution)/shard_map/all_to_all | solution.py:587
  326.6 7.1 %copy-start = (f32[256,256]{1,0:T(8,128)S(1)}, f32[256,256]{1,0:T(8,128)}, u32[]{:S(2)}) copy-start(f32[256,256]{1,0:T(8,128)} %get-tuple-element.79) | copy-start | bytes 786436
  331.2 34.6 %collective-permute-start.1 = (bf16[2,272,256]{2,1,0:T(8,128)(2,1)S(1)}, bf16[2,272,256]{2,1,0:T(8,128)(2,1)S(1)}, u32[]{:S(2)}, u32[]{:S(2)}) collective-permute-start(bf16[2,272,256]{2,1,0:T(8,128)(2,1)S(1)} %fusion.1), channel_id=1, source_target_pairs={{0,4},{4,0},{8,12},{12,8},{16,20},{20,16},{24,28},{28,24},{1,5},{5... | collective-permute-start | bytes 835592 | tf_op jit(solution)/shard_map/ppermute | solution.py:513
  365.8 0.7 copy-start.12
  369.4 52.5 %copy-start.9 = (bf16[1,272,256]{2,1,0:T(8,128)(2,1)}, bf16[1,272,256]{2,1,0:T(8,128)(2,1)S(1)}, u32[]{:S(2)}) copy-start(bf16[1,272,256]{2,1,0:T(8,128)(2,1)S(1)} %dynamic-slice_convert_fusion.1.refs_4_) | copy-start | bytes 417796
  369.4 63.2 %collective-permute-start.2 = (bf16[1,272,256]{2,1,0:T(8,128)(2,1)S(1)}, bf16[1,272,256]{2,1,0:T(8,128)(2,1)S(1)}, u32[]{:S(2)}, u32[]{:S(2)}) collective-permute-start(bf16[1,272,256]{2,1,0:T(8,128)(2,1)S(1)} %dynamic-slice_convert_fusion.1.refs_4_), channel_id=1, source_target_pairs={{0,16},{4,20},{8,24},{12,28},{16,0},{20,4},{24,8},{28,12},{1,17},{... | collective-permute-start | bytes 417800 | tf_op jit(solution)/shard_map/ppermute | solution.py:513
  433.3 20.0 %all-to-all-start.4 = ((bf16[8,160,256]{2,1,0:T(8,128)(2,1)}), bf16[8,160,256]{2,1,0:T(8,128)(2,1)S(1)}, u32[]{:S(2)}, u32[]{:S(2)}) async-start(bf16[8,160,256]{2,1,0:T(8,128)(2,1)} %hold.3), calls=%async_computation.4 | async-start | bytes 1310720 | tf_op jit(solution)/shard_map/all_to_all | solution.py:587
  453.3 0.9 copy-start.2
  (1 other events, 0.7 us)
